TPU v7x, 512 devices: a whole 4x4x16 slice. The times are simulated.
512 devices in a mesh: ew: 32 (over z, x_hi), ns: 16 (over y, x_lo, core).
Axes of the slice: x: 4 (x_hi: 2, x_lo: 2; x = x_hi * 2 + x_lo), y: 4, z: 16, core: 2. Of those that a mesh axis runs over, the one named last changes fastest.
Arguments:
- frame: bfloat16 [8, 256, 4096], P(None, 'ns', 'ew'), may hold values from -6 to 6
- hidden_prev: bfloat16 [64, 256, 4096], P(None, 'ns', 'ew'), may hold values from -0.94921875 to 0.94921875
- cell_prev: float32 [64, 256, 4096], P(None, 'ns', 'ew'), may hold values from -6 to 6
- kernel: bfloat16 [256, 648], replicated, may hold values from -0.25 to 0.25
- bias: float32 [256], replicated, may hold values from -4 to 4
- grad_hidden: float32 [64, 256, 4096], P(None, 'ns', 'ew'), may hold values from -6 to 6
- grad_cell: float32 [64, 256, 4096], P(None, 'ns', 'ew'), may hold values from -6 to 6
Outputs:
- hidden: bfloat16 [64, 256, 4096], P(None, 'ns', 'ew')
- cell: float32 [64, 256, 4096], P(None, 'ns', 'ew')
- grad_frame: bfloat16 [8, 256, 4096], P(None, 'ns', 'ew')
- grad_hidden_prev: bfloat16 [64, 256, 4096], P(None, 'ns', 'ew')
- grad_cell_prev: float32 [64, 256, 4096], P(None, 'ns', 'ew')
- kernel_step: float32 [256, 648], replicated
- bias_step: float32 [256], replicated
All inputs are finite; a program needn't handle non-finite values.
Results may differ from a plain program's by a relative error of at most 0.0049.
Values may be sent and summed in bfloat16 or wider, within the bound.
No kernel may reach another device: no remote copies, remote signals or barrier semaphores. Data moves between devices by JAX's collectives and lax.ppermute only.
A program may use at most 128 MiB of HBM per device.

v0:
```python
import jax
import jax.numpy as jnp
from jax import lax
from jax.sharding import PartitionSpec as P

CLIP_NORM = 100.0


def padded_2(block, sides, width):
    for axis, dim in sides:
        count = lax.axis_size(axis)
        forward = [(i, i + 1) for i in range(count - 1)]
        backward = [(target, source) for source, target in forward]
        low = lax.ppermute(
            lax.slice_in_dim(block, block.shape[dim] - width, None, axis=dim), axis, forward
        )
        high = lax.ppermute(lax.slice_in_dim(block, 0, width, axis=dim), axis, backward)
        block = jnp.concatenate([low, block, high], axis=dim)
    return block


def cell_step(gate_sums, cell_prev, grad_hidden, grad_cell):
    units = cell_prev.shape[0]
    input_gate = jax.nn.sigmoid(gate_sums[:units])
    forget_gate = jax.nn.sigmoid(gate_sums[units : 2 * units])
    cand_gate = jnp.tanh(gate_sums[2 * units : 3 * units])
    output_gate = jax.nn.sigmoid(gate_sums[3 * units :])
    cell = forget_gate * cell_prev + input_gate * cand_gate
    cell_tanh = jnp.tanh(cell)
    hidden = (output_gate * cell_tanh).astype(jnp.bfloat16)
    cell_grad = grad_cell + grad_hidden * output_gate * (1.0 - cell_tanh * cell_tanh)
    grad_gates = jnp.concatenate(
        [
            cell_grad * cand_gate * input_gate * (1.0 - input_gate),
            cell_grad * cell_prev * forget_gate * (1.0 - forget_gate),
            cell_grad * input_gate * (1.0 - cand_gate * cand_gate),
            grad_hidden * cell_tanh * output_gate * (1.0 - output_gate),
        ],
        0,
    ).astype(jnp.bfloat16)
    return (hidden, cell, grad_gates, cell_grad * forget_gate)


def build_patches(padded, height, breadth):
    channels = padded.shape[0]
    windows = [
        padded[:, row_off : row_off + height, col_off : col_off + breadth]
        for row_off in range(3)
        for col_off in range(3)
    ]
    return jnp.stack(windows, 0).reshape(9 * channels, height * breadth)


def spread_back(kernel, padded_grads, height, breadth):
    gate_rows = kernel.shape[0]
    channels = kernel.shape[1] // 9
    product = lax.dot_general(
        kernel,
        padded_grads.reshape(gate_rows, -1),
        (((0,), (0,)), ((), ())),
        preferred_element_type=jnp.float32,
    )
    product = product.reshape(9, channels, height + 2, breadth + 2)
    total = jnp.zeros((channels, height, breadth), jnp.float32)
    for row_off in range(3):
        for col_off in range(3):
            total = (
                total
                + product[
                    3 * row_off + col_off,
                    :,
                    2 - row_off : 2 - row_off + height,
                    2 - col_off : 2 - col_off + breadth,
                ]
            )
    return total


def per_device(frame, hidden_prev, cell_prev, kernel, bias, grad_hidden, grad_cell):
    joined = jnp.concatenate([frame, hidden_prev], 0)
    channels, height, breadth = joined.shape
    gate_rows = kernel.shape[0]
    padded = padded_2(joined, (("ew", 2), ("ns", 1)), 1)
    inner = build_patches(padded, height, breadth)
    gate_sums = jnp.dot(kernel, inner, preferred_element_type=jnp.float32) + bias[:, None]
    gate_sums = gate_sums.reshape(gate_rows, height, breadth)
    hidden, cell, grad_gates, grad_cell_prev = cell_step(
        gate_sums, cell_prev, grad_hidden, grad_cell
    )
    padded_grads = padded_2(grad_gates, (("ew", 2), ("ns", 1)), 1)
    weight_local = lax.dot_general(
        grad_gates.reshape(gate_rows, -1),
        inner,
        (((1,), (1,)), ((), ())),
        preferred_element_type=jnp.float32,
    )
    bias_local = jnp.sum(grad_gates.astype(jnp.float32), axis=(1, 2))
    joined_grad = spread_back(kernel, padded_grads, height, breadth)
    inputs_count = frame.shape[0]
    grad_frame = joined_grad[:inputs_count].astype(jnp.bfloat16)
    grad_hidden_prev = joined_grad[inputs_count:].astype(jnp.bfloat16)
    weight_grad, bias_grad = lax.psum((weight_local, bias_local), ("ew", "ns"))
    total_norm = jnp.sqrt(jnp.sum(weight_grad * weight_grad) + jnp.sum(bias_grad * bias_grad))
    factor = jnp.minimum(1.0, CLIP_NORM / total_norm)
    kernel_step = weight_grad * factor
    return (
        hidden,
        cell,
        grad_frame,
        grad_hidden_prev,
        grad_cell_prev,
        kernel_step,
        bias_grad * factor,
    )


def solution(mesh):
    placed = (
        P(None, "ns", "ew"),
        P(None, "ns", "ew"),
        P(None, "ns", "ew"),
        P(),
        P(),
        P(None, "ns", "ew"),
        P(None, "ns", "ew"),
    )
    return jax.shard_map(
        per_device,
        mesh=mesh,
        in_specs=placed,
        out_specs=(
            P(None, "ns", "ew"),
            P(None, "ns", "ew"),
            P(None, "ns", "ew"),
            P(None, "ns", "ew"),
            P(None, "ns", "ew"),
            P(),
            P(),
        ),
        check_vma=False,
    )
```

profile of v0, /device:TPU:1, one launch (start us, length us, event | category | flops | bytes accessed | tf_op | source)
XLA Modules:
  0.0 543.5 jit_solution(16963853435787537002)
XLA Ops:
  7.2 0.8 constant_dynamic-update-slice_fusion.1
  8.0 1.0 constant_dynamic-update-slice_fusion
  9.2 5.5 %collective-permute-start = (bf16[72,16,1]{2,1,0:T(8,128)(2,1)S(1)}, bf16[72,16,1]{2,1,0:T(8,128)(2,1)S(1)}, u32[]{:S(2)}, u32[]{:S(2)}) collective-permute-start(bf16[72,16,1]{2,1,0:T(8,128)(2,1)S(1)} %get-tuple-element.43), channel_id=1, source_target_pairs={{0,16},{16,32},{32,48},{48,64},{64,80},{80,96},{96,112},{112,128},... | collective-permute-start | bytes 6920 | tf_op jit(solution)/shard_map/ppermute | solution.py:14
  14.7 1.3 collective-permute-start.1
  16.0 2.6 collective-permute-done
  18.5 5.1 collective-permute-done.1
  23.6 0.4 pad_maximum_fusion.6
  24.1 6.4 %collective-permute-start.3 = (bf16[72,1,130]{2,1,0:T(2,128)(2,1)S(1)}, bf16[72,1,130]{2,1,0:T(2,128)(2,1)S(1)}, u32[]{:S(2)}, u32[]{:S(2)}) collective-permute-start(bf16[72,1,130]{2,1,0:T(2,128)(2,1)S(1)} %get-tuple-element.40), channel_id=1, source_target_pairs={{1,0},{2,1},{3,2},{4,3},{5,4},{6,5},{7,6},{8,7},{9,8},{10,9},{11,1... | collective-permute-start | bytes 56168 | tf_op jit(solution)/shard_map/ppermute | solution.py:17
  30.5 2.1 collective-permute-start.2
  32.7 1.3 collective-permute-done.2
  34.0 1.1 pad_maximum_fusion.3
  35.9 0.3 fusion.45
  36.3 0.3 fusion.42
  36.6 0.3 fusion.41
  36.9 1.5 copy-done.9
  38.4 1.0 fusion
  39.5 0.5 fusion.32
  40.4 0.6 copy-done.5
  41.3 1.1 bitcast_multiply_fusion.4
  42.4 1.1 fusion.17
  43.8 1.0 convert_reduce_fusion
  44.9 0.5 fusion.55
  45.4 0.9 copy.73
  46.3 0.9 copy.74
  47.3 1.3 collective-permute-start.5
  48.5 6.8 %collective-permute-start.4 = (bf16[256,16,1]{0,1,2:T(8,128)(2,1)S(1)}, bf16[256,16,1]{0,1,2:T(8,128)(2,1)S(1)}, u32[]{:S(2)}, u32[]{:S(2)}) collective-permute-start(bf16[256,16,1]{0,1,2:T(8,128)(2,1)S(1)} %copy.73), channel_id=1, source_target_pairs={{0,16},{16,32},{32,48},{48,64},{64,80},{80,96},{96,112},{112,128},... | collective-permute-start | bytes 24584 | tf_op jit(solution)/shard_map/ppermute | solution.py:14
  55.4 3.5 fusion.1
  59.0 113.3 %psum.15 = f32[256]{0:T(256)S(1)} all-reduce(f32[256]{0:T(256)S(1)} %get-tuple-element.21), channel_id=1, replica_groups=mesh['ew'=32,'ns'=16] {'ew','ns'}, use_global_device_ids=true, to_apply=%region_3.0 | all-reduce | flops 256 | bytes 2048 | tf_op jit(solution)/shard_map/psum | solution.py:102
  172.3 1.0 copy.75
  173.3 1.9 copy.76
  175.2 3.3 pad_maximum_fusion
  178.5 1.2 fusion.54
  179.7 2.6 collective-permute-start.6
  182.3 2.4 collective-permute-start.7
  184.8 0.7 multiply_reduce_fusion.1
  185.4 2.0 copy.78
  187.4 1.1 copy.77
  188.5 2.5 collective-permute-done.7
  191.0 1.1 copy.79
  192.6 3.7 convolution_bitcast_fusion
  196.3 13.6 %reshape.63 = f32[9,72,18,130]{3,2,1,0:T(8,128)} reshape(f32[648,2340]{1,0:T(8,128)} %convolution_bitcast_fusion) | data formatting | bytes 12130560 | tf_op jit(solution)/shard_map/reshape | solution.py:63
  209.9 5.4 fusion.13
  215.3 0.6 slice_bitcast_fusion.7
  215.9 0.7 slice_bitcast_fusion.6
  216.6 314.3 %all-reduce.2.cloned.1.call-done = f32[256,648]{0,1:T(8,128)} async-done(((f32[256,648]{0,1:T(8,128)}), f32[256,648]{0,1:T(8,128)}) %all-reduce.2.cloned.1.call-update) | async-done | bytes 663568 | tf_op jit(solution)/shard_map/psum | solution.py:102
  530.9 1.9 multiply_reduce_fusion
  534.1 0.6 broadcast_multiply_fusion.1
  534.7 2.0 broadcast_multiply_fusion
  (43 shorter events, 2.6 us)
Async XLA Ops:
  7.2 31.3 %copy-start = (bf16[256,648]{0,1:T(8,128)(2,1)S(1)}, bf16[256,648]{0,1:T(8,128)(2,1)}, u32[]{:S(2)}) copy-start(bf16[256,648]{0,1:T(8,128)(2,1)} %param.10) | copy-start | bytes 995332
  7.2 523.7 %all-reduce.2.cloned.1.call-start = ((), (), s32[]{:S(2)}) async-start(), calls=%async_computation | async-start | bytes 1327104 | tf_op jit(solution)/shard_map/psum | solution.py:102
  9.2 9.4 %collective-permute-start = (bf16[72,16,1]{2,1,0:T(8,128)(2,1)S(1)}, bf16[72,16,1]{2,1,0:T(8,128)(2,1)S(1)}, u32[]{:S(2)}, u32[]{:S(2)}) collective-permute-start(bf16[72,16,1]{2,1,0:T(8,128)(2,1)S(1)} %get-tuple-element.43), channel_id=1, source_target_pairs={{0,16},{16,32},{32,48},{48,64},{64,80},{80,96},{96,112},{112,128},... | collective-permute-start | bytes 6920 | tf_op jit(solution)/shard_map/ppermute | solution.py:14
  14.7 9.0 %collective-permute-start.1 = (bf16[72,16,1]{2,1,0:T(8,128)(2,1)S(1)}, bf16[72,16,1]{2,1,0:T(8,128)(2,1)S(1)}, u32[]{:S(2)}, u32[]{:S(2)}) collective-permute-start(bf16[72,16,1]{2,1,0:T(8,128)(2,1)S(1)} %get-tuple-element.44), channel_id=1, source_target_pairs={{16,0},{32,16},{48,32},{64,48},{80,64},{96,80},{112,96},{128,112},... | collective-permute-start | bytes 6920 | tf_op jit(solution)/shard_map/ppermute | solution.py:17
  24.1 8.7 %collective-permute-start.3 = (bf16[72,1,130]{2,1,0:T(2,128)(2,1)S(1)}, bf16[72,1,130]{2,1,0:T(2,128)(2,1)S(1)}, u32[]{:S(2)}, u32[]{:S(2)}) collective-permute-start(bf16[72,1,130]{2,1,0:T(2,128)(2,1)S(1)} %get-tuple-element.40), channel_id=1, source_target_pairs={{1,0},{2,1},{3,2},{4,3},{5,4},{6,5},{7,6},{8,7},{9,8},{10,9},{11,1... | collective-permute-start | bytes 56168 | tf_op jit(solution)/shard_map/ppermute | solution.py:17
  30.5 3.5 collective-permute-start.2
  35.2 3.2 copy-start.10
  36.9 1.5 copy-start.9
  40.0 1.0 copy-start.5
  40.0 1.2 copy-start.6
  40.0 1.3 copy-start.8
  42.4 1.1 copy-start.7
  43.5 1.9 copy-start.1
  43.5 1.9 copy-start.2
  43.6 1.9 copy-start.3
  43.6 1.9 copy-start.4
  47.3 126.0 %collective-permute-start.5 = (bf16[256,16,1]{0,1,2:T(8,128)(2,1)S(1)}, bf16[256,16,1]{0,1,2:T(8,128)(2,1)S(1)}, u32[]{:S(2)}, u32[]{:S(2)}) collective-permute-start(bf16[256,16,1]{0,1,2:T(8,128)(2,1)S(1)} %copy.74), channel_id=1, source_target_pairs={{16,0},{32,16},{48,32},{64,48},{80,64},{96,80},{112,96},{128,112},... | collective-permute-start | bytes 24584 | tf_op jit(solution)/shard_map/ppermute | solution.py:17
  48.5 123.7 %collective-permute-start.4 = (bf16[256,16,1]{0,1,2:T(8,128)(2,1)S(1)}, bf16[256,16,1]{0,1,2:T(8,128)(2,1)S(1)}, u32[]{:S(2)}, u32[]{:S(2)}) collective-permute-start(bf16[256,16,1]{0,1,2:T(8,128)(2,1)S(1)} %copy.73), channel_id=1, source_target_pairs={{0,16},{16,32},{32,48},{48,64},{64,80},{80,96},{96,112},{112,128},... | collective-permute-start | bytes 24584 | tf_op jit(solution)/shard_map/ppermute | solution.py:14
  179.7 7.7 %collective-permute-start.6 = (bf16[256,1,130]{2,1,0:T(2,128)(2,1)}, bf16[256,1,130]{2,1,0:T(2,128)(2,1)}, u32[]{:S(2)}, u32[]{:S(2)}) collective-permute-start(bf16[256,1,130]{2,1,0:T(2,128)(2,1)} %get-tuple-element.26), channel_id=1, source_target_pairs={{0,1},{1,2},{2,3},{3,4},{4,5},{5,6},{6,7},{7,8},{8,9},{9,10},{10,1... | collective-permute-start | bytes 199688 | tf_op jit(solution)/shard_map/ppermute | solution.py:14
  182.3 8.7 %collective-permute-start.7 = (bf16[256,1,130]{2,1,0:T(2,128)(2,1)}, bf16[256,1,130]{2,1,0:T(2,128)(2,1)}, u32[]{:S(2)}, u32[]{:S(2)}) collective-permute-start(bf16[256,1,130]{2,1,0:T(2,128)(2,1)} %get-tuple-element.27), channel_id=1, source_target_pairs={{1,0},{2,1},{3,2},{4,3},{5,4},{6,5},{7,6},{8,7},{9,8},{10,9},{11,1... | collective-permute-start | bytes 199688 | tf_op jit(solution)/shard_map/ppermute | solution.py:17
Sparse Core Ops, SparseCore 0:
  59.1 471.7 all-reduce.1
where the time goes:
time: 544 us; the launch traced here: 543 us
  waiting for transfers between devices  326 us (60%)
  blocking collectives  113 us (21%)
  local copies, waits for them, and re-layouts  32.1 us (6%)
  starting transfers between devices  28.5 us (5%)
  other arithmetic  19.7 us (4%)
  between operations  15.7 us (3%)
  matrix products  8.29 us (2%)
    psum x1, waiting for transfers between devices, per_device(): weight_grad, bias_grad = lax.psum((weight_local, bias_local), ('ew', 'ns'))  314 us
    psum x1, blocking collectives, per_device(): weight_grad, bias_grad = lax.psum((weight_local, bias_local), ('ew', 'ns'))  113 us
    ppermute x4, starting transfers between devices, padded_2(): lax.ppermute(lax.slice_in_dim(block, block.shape[dim] - width, None, axis...  17 us
    reshape x1, local copies, waits for them, and re-layouts, spread_back(): product = product.reshape(9, channels, height + 2, breadth + 2)  13.6 us
    ppermute x4, starting transfers between devices, padded_2(): lax.ppermute(lax.slice_in_dim(block, 0, width, axis=dim), axis, backward)  11.4 us
  transfers between devices with their start and end apart: 9, of which 6 were waited for; matrix products, arithmetic and copies ran while one was open for 7% of the time, Pallas kernels for 0%

commit v1 on v0

--- a/solution.py
+++ b/solution.py
@@ -1,9 +1,12 @@
 import jax
 import jax.numpy as jnp
 from jax import lax
-from jax.sharding import PartitionSpec as P
+from jax.sharding import Mesh, PartitionSpec as P
 
 CLIP_NORM = 100.0
+EW = ("z", "x_hi")
+NS = ("y", "x_lo", "core")
+PLANE = ("x_hi", "y", "x_lo", "core")
 
 
 def padded_2(block, sides, width):
@@ -76,18 +79,36 @@
     return total
 
 
+def sum_everywhere(weight_local, bias_local):
+    rows, columns = weight_local.shape
+    width = -(-(columns + 1) // 128) * 128
+    terms = jnp.concatenate([weight_local, bias_local[:, None]], 1)
+    terms = jnp.pad(terms, ((0, 0), (0, width - columns - 1))).astype(jnp.bfloat16)
+    plane = lax.axis_size(PLANE)
+    deep = lax.axis_size("z")
+    share = rows // plane
+    mine = lax.all_to_all(terms, PLANE, 0, 0, tiled=True).reshape(plane, share, width)
+    mine = jnp.sum(mine.astype(jnp.float32), 0)
+    mine = jnp.broadcast_to(mine[None], (deep, share, width))
+    mine = lax.all_to_all(mine, "z", 0, 0, tiled=True)
+    mine = jnp.sum(mine, 0).astype(jnp.bfloat16)
+    mine = jnp.broadcast_to(mine[None], (plane, share, width)).reshape(rows, width)
+    total = lax.all_to_all(mine, PLANE, 0, 0, tiled=True).astype(jnp.float32)
+    return total[:, :columns], total[:, columns]
+
+
 def per_device(frame, hidden_prev, cell_prev, kernel, bias, grad_hidden, grad_cell):
     joined = jnp.concatenate([frame, hidden_prev], 0)
     channels, height, breadth = joined.shape
     gate_rows = kernel.shape[0]
-    padded = padded_2(joined, (("ew", 2), ("ns", 1)), 1)
+    padded = padded_2(joined, ((EW, 2), (NS, 1)), 1)
     inner = build_patches(padded, height, breadth)
     gate_sums = jnp.dot(kernel, inner, preferred_element_type=jnp.float32) + bias[:, None]
     gate_sums = gate_sums.reshape(gate_rows, height, breadth)
     hidden, cell, grad_gates, grad_cell_prev = cell_step(
         gate_sums, cell_prev, grad_hidden, grad_cell
     )
-    padded_grads = padded_2(grad_gates, (("ew", 2), ("ns", 1)), 1)
+    padded_grads = padded_2(grad_gates, ((EW, 2), (NS, 1)), 1)
     weight_local = lax.dot_general(
         grad_gates.reshape(gate_rows, -1),
         inner,
@@ -99,7 +120,7 @@
     inputs_count = frame.shape[0]
     grad_frame = joined_grad[:inputs_count].astype(jnp.bfloat16)
     grad_hidden_prev = joined_grad[inputs_count:].astype(jnp.bfloat16)
-    weight_grad, bias_grad = lax.psum((weight_local, bias_local), ("ew", "ns"))
+    weight_grad, bias_grad = sum_everywhere(weight_local, bias_local)
     total_norm = jnp.sqrt(jnp.sum(weight_grad * weight_grad) + jnp.sum(bias_grad * bias_grad))
     factor = jnp.minimum(1.0, CLIP_NORM / total_norm)
     kernel_step = weight_grad * factor
@@ -115,25 +136,26 @@
 
 
 def solution(mesh):
+    mesh = Mesh(mesh.devices.reshape(16, 2, 4, 2, 2), EW + NS)
     placed = (
-        P(None, "ns", "ew"),
-        P(None, "ns", "ew"),
-        P(None, "ns", "ew"),
+        P(None, NS, EW),
+        P(None, NS, EW),
+        P(None, NS, EW),
         P(),
         P(),
-        P(None, "ns", "ew"),
-        P(None, "ns", "ew"),
+        P(None, NS, EW),
+        P(None, NS, EW),
     )
     return jax.shard_map(
         per_device,
         mesh=mesh,
         in_specs=placed,
         out_specs=(
-            P(None, "ns", "ew"),
-            P(None, "ns", "ew"),
-            P(None, "ns", "ew"),
-            P(None, "ns", "ew"),
-            P(None, "ns", "ew"),
+            P(None, NS, EW),
+            P(None, NS, EW),
+            P(None, NS, EW),
+            P(None, NS, EW),
+            P(None, NS, EW),
             P(),
             P(),
         ),

time: 544 us -> 160 us (0.29)
  waiting for transfers between devices: 326 us -> 24.3 us
  blocking collectives: 113 us -> 20.8 us
  starting transfers between devices: 28.5 us -> 53.9 us
  between operations: 15.7 us -> 2.4 us
    psum x1 -> x0, waiting for transfers between devices: 314 us -> none  [per_device(): weight_grad, bias_grad = lax.psum((weight_local, bias_local), ('ew', 'ns'))]
    psum x1 -> x0, blocking collectives: 113 us -> none  [per_device(): weight_grad, bias_grad = lax.psum((weight_local, bias_local), ('ew', 'ns'))]
    all_to_all x0 -> x2, starting transfers between devices: none -> 27.5 us  [the longest x1 15.7 us: sum_everywhere(): mine = lax.all_to_all(mine, 'z', 0, 0, tiled=True)]
    all_to_all x0 -> x1, blocking collectives: none -> 20.8 us  [sum_everywhere(): lax.all_to_all(terms, PLANE, 0, 0, tiled=True).reshape(plane, share, width)]
    all_to_all x0 -> x2, waiting for transfers between devices: none -> 8.52 us  [the longest x1 8.52 us: sum_everywhere(): total = lax.all_to_all(mine, PLANE, 0, 0, tiled=True).astype(jnp.float32)]
  transfers between devices with their start and end apart: 9 -> 10, of which waited for: 6 -> 7; matrix products, arithmetic and copies ran while one was open for 7% -> 24% of each run, Pallas kernels for 0% -> 0%
where the time goes in v1:
time: 160 us; the launch traced here: 159 us
  starting transfers between devices  53.9 us (34%)
  local copies, waits for them, and re-layouts  33.4 us (21%)
  waiting for transfers between devices  24.3 us (15%)
  blocking collectives  20.8 us (13%)
  other arithmetic  18.1 us (11%)
  matrix products  5.71 us (4%)
  between operations  2.4 us (2%)
    all_to_all x1, blocking collectives, sum_everywhere(): lax.all_to_all(terms, PLANE, 0, 0, tiled=True).reshape(plane, share, width)  20.8 us
    all_to_all x1, starting transfers between devices, sum_everywhere(): mine = lax.all_to_all(mine, 'z', 0, 0, tiled=True)  15.7 us
    ppermute x4, starting transfers between devices, padded_2(): lax.ppermute(lax.slice_in_dim(block, block.shape[dim] - width, None, axis...  15.3 us
    reshape x1, local copies, waits for them, and re-layouts, spread_back(): product = product.reshape(9, channels, height + 2, breadth + 2)  13.6 us
    ppermute x4, waiting for transfers between devices, padded_2(): lax.ppermute(lax.slice_in_dim(block, 0, width, axis=dim), axis, backward)  11.9 us
    all_to_all x1, starting transfers between devices, sum_everywhere(): total = lax.all_to_all(mine, PLANE, 0, 0, tiled=True).astype(jnp.float32)  11.8 us
    ppermute x4, starting transfers between devices, padded_2(): lax.ppermute(lax.slice_in_dim(block, 0, width, axis=dim), axis, backward)  11.1 us
    all_to_all x1, waiting for transfers between devices, sum_everywhere(): total = lax.all_to_all(mine, PLANE, 0, 0, tiled=True).astype(jnp.float32)  8.52 us
  transfers between devices with their start and end apart: 10, of which 7 were waited for; matrix products, arithmetic and copies ran while one was open for 24% of the time, Pallas kernels for 0%

profile of v1, /device:TPU:1, one launch (start us, length us, event | category | flops | bytes accessed | tf_op | source)
XLA Modules:
  0.0 158.5 jit_solution(10531952538341605004)
XLA Ops:
  0.6 0.8 constant_dynamic-update-slice_fusion.1
  1.5 1.0 constant_dynamic-update-slice_fusion
  2.6 5.5 %collective-permute-start = (bf16[72,16,1]{2,1,0:T(8,128)(2,1)S(1)}, bf16[72,16,1]{2,1,0:T(8,128)(2,1)S(1)}, u32[]{:S(2)}, u32[]{:S(2)}) collective-permute-start(bf16[72,16,1]{2,1,0:T(8,128)(2,1)S(1)} %get-tuple-element.71), channel_id=1, source_target_pairs={{0,16},{16,32},{32,48},{48,64},{64,80},{80,96},{96,112},{112,128},... | collective-permute-start | bytes 6920 | tf_op jit(solution)/shard_map/ppermute | solution.py:17
  8.1 1.3 collective-permute-start.1
  9.4 2.6 %collective-permute-done = bf16[72,16,1]{2,1,0:T(8,128)(2,1)S(1)} collective-permute-done((bf16[72,16,1]{2,1,0:T(8,128)(2,1)S(1)}, bf16[72,16,1]{2,1,0:T(8,128)(2,1)S(1)}, u32[]{:S(2)}, u32[]{:S(2)}) %collective-permute-start) | collective-permute-done | bytes 2336 | tf_op jit(solution)/shard_map/ppermute | solution.py:17
  11.9 5.1 %collective-permute-done.1 = bf16[72,16,1]{2,1,0:T(8,128)(2,1)S(1)} collective-permute-done((bf16[72,16,1]{2,1,0:T(8,128)(2,1)S(1)}, bf16[72,16,1]{2,1,0:T(8,128)(2,1)S(1)}, u32[]{:S(2)}, u32[]{:S(2)}) %collective-permute-start.1) | collective-permute-done | bytes 2336 | tf_op jit(solution)/shard_map/ppermute | solution.py:20
  17.5 6.4 %collective-permute-start.3 = (bf16[72,1,130]{2,1,0:T(2,128)(2,1)S(1)}, bf16[72,1,130]{2,1,0:T(2,128)(2,1)S(1)}, u32[]{:S(2)}, u32[]{:S(2)}) collective-permute-start(bf16[72,1,130]{2,1,0:T(2,128)(2,1)S(1)} %get-tuple-element.68), channel_id=1, source_target_pairs={{1,0},{2,1},{3,2},{4,3},{5,4},{6,5},{7,6},{8,7},{9,8},{10,9},{11,1... | collective-permute-start | bytes 56168 | tf_op jit(solution)/shard_map/ppermute | solution.py:20
  24.0 2.1 %collective-permute-start.2 = (bf16[72,1,130]{2,1,0:T(2,128)(2,1)S(1)}, bf16[72,1,130]{2,1,0:T(2,128)(2,1)S(1)}, u32[]{:S(2)}, u32[]{:S(2)}) collective-permute-start(bf16[72,1,130]{2,1,0:T(2,128)(2,1)S(1)} %get-tuple-element.69), channel_id=1, source_target_pairs={{0,1},{1,2},{2,3},{3,4},{4,5},{5,6},{6,7},{7,8},{8,9},{9,10},{10,1... | collective-permute-start | bytes 56168 | tf_op jit(solution)/shard_map/ppermute | solution.py:17
  26.2 1.3 collective-permute-done.2
  27.5 1.1 pad_maximum_fusion.3
  30.4 1.0 fusion
  31.4 0.5 fusion.35
  32.3 0.6 copy-done.5
  33.3 1.1 bitcast_multiply_fusion.4
  34.3 1.1 fusion.20
  35.7 1.0 fusion.55
  36.8 1.0 fusion.6
  38.1 20.8 %all_to_all.20 = bf16[32,8,768]{2,1,0:T(8,128)(2,1)S(1)} all-to-all(bf16[32,8,768]{2,1,0:T(8,128)(2,1)S(1)} %pad_bitcast_fusion), channel_id=1, replica_groups=mesh['z'=16,'x_hi'=2,'y'=4,'x_lo'=2,'core'=2] {'x_hi','y','x_lo','core'}, dimensions={0} | all-to-all | bytes 786432 | tf_op jit(solution)/shard_map/all_to_all | solution.py:90
  58.9 0.8 broadcast_in_dim.8
  59.7 15.7 %all-to-all-start.1 = ((f32[16,8,768]{2,1,0:T(8,128)}), f32[16,8,768]{2,1,0:T(8,128)}, u32[]{:S(2)}, u32[]{:S(2)}) async-start(f32[16,8,768]{2,1,0:T(8,128)} %broadcast_in_dim.8), calls=%async_computation.1 | async-start | bytes 786432 | tf_op jit(solution)/shard_map/all_to_all | solution.py:93
  75.9 0.9 copy.115
  76.8 2.8 %collective-permute-start.4 = (bf16[256,16,1]{0,1,2:T(8,128)(2,1)S(1)}, bf16[256,16,1]{0,1,2:T(8,128)(2,1)S(1)}, u32[]{:S(2)}, u32[]{:S(2)}) collective-permute-start(bf16[256,16,1]{0,1,2:T(8,128)(2,1)S(1)} %copy.115), channel_id=1, source_target_pairs={{0,16},{16,32},{32,48},{48,64},{64,80},{80,96},{96,112},{112,128},... | collective-permute-start | bytes 24584 | tf_op jit(solution)/shard_map/ppermute | solution.py:17
  79.6 0.9 copy.116
  80.5 1.5 collective-permute-start.5
  82.0 1.0 copy.117
  83.0 3.6 %collective-permute-done.5 = bf16[256,16,1]{0,1,2:T(8,128)(2,1)S(1)} collective-permute-done((bf16[256,16,1]{0,1,2:T(8,128)(2,1)S(1)}, bf16[256,16,1]{0,1,2:T(8,128)(2,1)S(1)}, u32[]{:S(2)}, u32[]{:S(2)}) %collective-permute-start.5) | collective-permute-done | bytes 8224 | tf_op jit(solution)/shard_map/ppermute | solution.py:20
  86.6 1.9 %copy.118 = bf16[256,16,1]{2,1,0:T(8,128)(2,1)} copy(bf16[256,16,1]{0,1,2:T(8,128)(2,1)S(1)} %collective-permute-done.5) | data formatting | bytes 16384 | tf_op jit(solution)/shard_map/ppermute | solution.py:20
  88.5 3.3 %pad_maximum_fusion = bf16[256,16,130]{2,1,0:T(8,128)(2,1)S(1)} fusion(bf16[256,16,1]{2,1,0:T(8,128)(2,1)} %copy.118, bf16[64,16,128]{2,1,0:T(8,128)(2,1)} %copy-done.4, bf16[64,16,128]{2,1,0:T(8,128)(2,1)} %copy-done.2, bf16[64,16,128]{2,1,0:T(8,128)(2,1)} %copy-done.3, bf16[64,16,128]{2,1,0:T(8,128)(2,1)} %copy-done.1, bf16[256,16,1]{2,1,0:T(8,128)(2,1)S(1)} %copy.117), kind=kLoop, calls=%fused_computation.8 | loop fusion | flops 6389760 | bytes 2129920 | tf_op jit(solution)/shard_map/concatenate | solution.py:21
  91.8 1.2 fusion.58
  93.0 4.9 %collective-permute-start.6 = (bf16[256,1,130]{2,1,0:T(2,128)(2,1)}, bf16[256,1,130]{2,1,0:T(2,128)(2,1)}, u32[]{:S(2)}, u32[]{:S(2)}) collective-permute-start(bf16[256,1,130]{2,1,0:T(2,128)(2,1)} %get-tuple-element.54), channel_id=1, source_target_pairs={{0,1},{1,2},{2,3},{3,4},{4,5},{5,6},{6,7},{7,8},{8,9},{9,10},{10,1... | collective-permute-start | bytes 199688 | tf_op jit(solution)/shard_map/ppermute | solution.py:17
  97.9 1.9 %collective-permute-start.7 = (bf16[256,1,130]{2,1,0:T(2,128)(2,1)}, bf16[256,1,130]{2,1,0:T(2,128)(2,1)}, u32[]{:S(2)}, u32[]{:S(2)}) collective-permute-start(bf16[256,1,130]{2,1,0:T(2,128)(2,1)} %get-tuple-element.55), channel_id=1, source_target_pairs={{1,0},{2,1},{3,2},{4,3},{5,4},{6,5},{7,6},{8,7},{9,8},{10,9},{11,1... | collective-permute-start | bytes 199688 | tf_op jit(solution)/shard_map/ppermute | solution.py:20
  99.9 2.0 %copy.120 = bf16[256,16,130]{0,2,1:T(8,128)(2,1)S(1)} copy(bf16[256,16,130]{2,1,0:T(8,128)(2,1)S(1)} %pad_maximum_fusion) | data formatting | bytes 2129920 | tf_op jit(solution)/shard_map/concatenate | solution.py:21
  101.9 1.1 copy.119
  103.0 3.1 %collective-permute-done.7 = bf16[256,1,130]{2,1,0:T(2,128)(2,1)} collective-permute-done((bf16[256,1,130]{2,1,0:T(2,128)(2,1)}, bf16[256,1,130]{2,1,0:T(2,128)(2,1)}, u32[]{:S(2)}, u32[]{:S(2)}) %collective-permute-start.7) | collective-permute-done | bytes 66592 | tf_op jit(solution)/shard_map/ppermute | solution.py:20
  106.1 1.1 copy.121
  107.6 3.7 %convolution_bitcast_fusion = f32[648,2340]{1,0:T(8,128)} fusion(bf16[256,2340]{0,1:T(8,128)(2,1)S(1)} %reshape.79, bf16[256,648]{0,1:T(8,128)(2,1)S(1)} %copy-done), kind=kOutput, calls=%fused_computation | convolution fusion | flops 776355840 | bytes 7595136 | tf_op jit(solution)/shard_map/dot_general | solution.py:60
  111.3 13.6 %reshape.80 = f32[9,72,18,130]{3,2,1,0:T(8,128)} reshape(f32[648,2340]{1,0:T(8,128)} %convolution_bitcast_fusion) | data formatting | bytes 12130560 | tf_op jit(solution)/shard_map/reshape | solution.py:66
  124.9 5.4 %fusion.16 = bf16[1,72,16,128]{3,2,1,0:T(8,128)(2,1)S(1)} fusion(f32[9,72,18,130]{3,2,1,0:T(8,128)} %reshape.80), kind=kLoop, calls=%fused_computation.25 | loop fusion | flops 1327104 | bytes 5603328 | tf_op jit(solution)/shard_map/convert.15
  130.3 1.0 reduce_sum.47
  131.3 0.8 broadcast_in_dim.9
  132.1 11.8 %all-to-all-start.2 = ((bf16[32,8,768]{2,1,0:T(8,128)(2,1)}), bf16[32,8,768]{2,1,0:T(8,128)(2,1)S(1)}, u32[]{:S(2)}, u32[]{:S(2)}) async-start(bf16[32,8,768]{2,1,0:T(8,128)(2,1)} %broadcast_in_dim.9), calls=%async_computation.2 | async-start | bytes 786432 | tf_op jit(solution)/shard_map/all_to_all | solution.py:96
  143.9 0.6 slice_bitcast_fusion.7
  144.5 0.7 slice_bitcast_fusion.6
  145.2 8.5 %all-to-all-done.2 = bf16[32,8,768]{2,1,0:T(8,128)(2,1)S(1)} async-done(((bf16[32,8,768]{2,1,0:T(8,128)(2,1)}), bf16[32,8,768]{2,1,0:T(8,128)(2,1)S(1)}, u32[]{:S(2)}, u32[]{:S(2)}) %all-to-all-start.2) | async-done | bytes 393248 | tf_op jit(solution)/shard_map/all_to_all | solution.py:96
  153.8 0.7 multiply_reduce_fusion.2
  154.5 0.8 multiply_reduce_fusion
  156.7 0.7 multiply_reduce_fusion.1
  157.5 1.1 copy.123
  (52 shorter events, 4.8 us)
Async XLA Ops:
  0.6 29.7 %copy-start = (bf16[256,648]{0,1:T(8,128)(2,1)S(1)}, bf16[256,648]{0,1:T(8,128)(2,1)}, u32[]{:S(2)}) copy-start(bf16[256,648]{0,1:T(8,128)(2,1)} %param.10) | copy-start | bytes 995332
  2.6 9.4 %collective-permute-start = (bf16[72,16,1]{2,1,0:T(8,128)(2,1)S(1)}, bf16[72,16,1]{2,1,0:T(8,128)(2,1)S(1)}, u32[]{:S(2)}, u32[]{:S(2)}) collective-permute-start(bf16[72,16,1]{2,1,0:T(8,128)(2,1)S(1)} %get-tuple-element.71), channel_id=1, source_target_pairs={{0,16},{16,32},{32,48},{48,64},{64,80},{80,96},{96,112},{112,128},... | collective-permute-start | bytes 6920 | tf_op jit(solution)/shard_map/ppermute | solution.py:17
  8.1 9.0 %collective-permute-start.1 = (bf16[72,16,1]{2,1,0:T(8,128)(2,1)S(1)}, bf16[72,16,1]{2,1,0:T(8,128)(2,1)S(1)}, u32[]{:S(2)}, u32[]{:S(2)}) collective-permute-start(bf16[72,16,1]{2,1,0:T(8,128)(2,1)S(1)} %get-tuple-element.72), channel_id=1, source_target_pairs={{16,0},{32,16},{48,32},{64,48},{80,64},{96,80},{112,96},{128,112},... | collective-permute-start | bytes 6920 | tf_op jit(solution)/shard_map/ppermute | solution.py:20
  17.5 8.7 %collective-permute-start.3 = (bf16[72,1,130]{2,1,0:T(2,128)(2,1)S(1)}, bf16[72,1,130]{2,1,0:T(2,128)(2,1)S(1)}, u32[]{:S(2)}, u32[]{:S(2)}) collective-permute-start(bf16[72,1,130]{2,1,0:T(2,128)(2,1)S(1)} %get-tuple-element.68), channel_id=1, source_target_pairs={{1,0},{2,1},{3,2},{4,3},{5,4},{6,5},{7,6},{8,7},{9,8},{10,9},{11,1... | collective-permute-start | bytes 56168 | tf_op jit(solution)/shard_map/ppermute | solution.py:20
  24.0 3.5 %collective-permute-start.2 = (bf16[72,1,130]{2,1,0:T(2,128)(2,1)S(1)}, bf16[72,1,130]{2,1,0:T(2,128)(2,1)S(1)}, u32[]{:S(2)}, u32[]{:S(2)}) collective-permute-start(bf16[72,1,130]{2,1,0:T(2,128)(2,1)S(1)} %get-tuple-element.69), channel_id=1, source_target_pairs={{0,1},{1,2},{2,3},{3,4},{4,5},{5,6},{6,7},{7,8},{8,9},{9,10},{10,1... | collective-permute-start | bytes 56168 | tf_op jit(solution)/shard_map/ppermute | solution.py:17
  28.6 1.7 %copy-start.9 = (f32[256]{0:T(256)S(1)}, f32[256]{0:T(256)}, u32[]{:S(2)}) copy-start(f32[256]{0:T(256)} %param.11) | copy-start | bytes 3076
  31.9 1.0 copy-start.5
  31.9 1.2 copy-start.6
  31.9 1.3 copy-start.8
  34.3 1.1 copy-start.7
  35.5 2.3 %copy-start.1 = (bf16[64,16,128]{2,1,0:T(8,128)(2,1)}, bf16[64,16,128]{2,1,0:T(8,128)(2,1)S(1)}, u32[]{:S(2)}) copy-start(bf16[64,16,128]{2,1,0:T(8,128)(2,1)S(1)} %get-tuple-element.60) | copy-start | bytes 786436
  35.5 2.4 %copy-start.2 = (bf16[64,16,128]{2,1,0:T(8,128)(2,1)}, bf16[64,16,128]{2,1,0:T(8,128)(2,1)S(1)}, u32[]{:S(2)}) copy-start(bf16[64,16,128]{2,1,0:T(8,128)(2,1)S(1)} %get-tuple-element.61) | copy-start | bytes 786436
  35.5 2.4 %copy-start.3 = (bf16[64,16,128]{2,1,0:T(8,128)(2,1)}, bf16[64,16,128]{2,1,0:T(8,128)(2,1)S(1)}, u32[]{:S(2)}) copy-start(bf16[64,16,128]{2,1,0:T(8,128)(2,1)S(1)} %get-tuple-element.70) | copy-start | bytes 786436
  35.5 2.4 %copy-start.4 = (bf16[64,16,128]{2,1,0:T(8,128)(2,1)}, bf16[64,16,128]{2,1,0:T(8,128)(2,1)S(1)}, u32[]{:S(2)}) copy-start(bf16[64,16,128]{2,1,0:T(8,128)(2,1)S(1)} %get-tuple-element.74) | copy-start | bytes 786436
  59.7 70.6 %all-to-all-start.1 = ((f32[16,8,768]{2,1,0:T(8,128)}), f32[16,8,768]{2,1,0:T(8,128)}, u32[]{:S(2)}, u32[]{:S(2)}) async-start(f32[16,8,768]{2,1,0:T(8,128)} %broadcast_in_dim.8), calls=%async_computation.1 | async-start | bytes 786432 | tf_op jit(solution)/shard_map/all_to_all | solution.py:93
  76.8 5.1 %collective-permute-start.4 = (bf16[256,16,1]{0,1,2:T(8,128)(2,1)S(1)}, bf16[256,16,1]{0,1,2:T(8,128)(2,1)S(1)}, u32[]{:S(2)}, u32[]{:S(2)}) collective-permute-start(bf16[256,16,1]{0,1,2:T(8,128)(2,1)S(1)} %copy.115), channel_id=1, source_target_pairs={{0,16},{16,32},{32,48},{48,64},{64,80},{80,96},{96,112},{112,128},... | collective-permute-start | bytes 24584 | tf_op jit(solution)/shard_map/ppermute | solution.py:17
  80.5 6.1 %collective-permute-start.5 = (bf16[256,16,1]{0,1,2:T(8,128)(2,1)S(1)}, bf16[256,16,1]{0,1,2:T(8,128)(2,1)S(1)}, u32[]{:S(2)}, u32[]{:S(2)}) collective-permute-start(bf16[256,16,1]{0,1,2:T(8,128)(2,1)S(1)} %copy.116), channel_id=1, source_target_pairs={{16,0},{32,16},{48,32},{64,48},{80,64},{96,80},{112,96},{128,112},... | collective-permute-start | bytes 24584 | tf_op jit(solution)/shard_map/ppermute | solution.py:20
  93.0 8.9 %collective-permute-start.6 = (bf16[256,1,130]{2,1,0:T(2,128)(2,1)}, bf16[256,1,130]{2,1,0:T(2,128)(2,1)}, u32[]{:S(2)}, u32[]{:S(2)}) collective-permute-start(bf16[256,1,130]{2,1,0:T(2,128)(2,1)} %get-tuple-element.54), channel_id=1, source_target_pairs={{0,1},{1,2},{2,3},{3,4},{4,5},{5,6},{6,7},{7,8},{8,9},{9,10},{10,1... | collective-permute-start | bytes 199688 | tf_op jit(solution)/shard_map/ppermute | solution.py:17
  97.9 8.1 %collective-permute-start.7 = (bf16[256,1,130]{2,1,0:T(2,128)(2,1)}, bf16[256,1,130]{2,1,0:T(2,128)(2,1)}, u32[]{:S(2)}, u32[]{:S(2)}) collective-permute-start(bf16[256,1,130]{2,1,0:T(2,128)(2,1)} %get-tuple-element.55), channel_id=1, source_target_pairs={{1,0},{2,1},{3,2},{4,3},{5,4},{6,5},{7,6},{8,7},{9,8},{10,9},{11,1... | collective-permute-start | bytes 199688 | tf_op jit(solution)/shard_map/ppermute | solution.py:20
  132.1 21.7 %all-to-all-start.2 = ((bf16[32,8,768]{2,1,0:T(8,128)(2,1)}), bf16[32,8,768]{2,1,0:T(8,128)(2,1)S(1)}, u32[]{:S(2)}, u32[]{:S(2)}) async-start(bf16[32,8,768]{2,1,0:T(8,128)(2,1)} %broadcast_in_dim.9), calls=%async_computation.2 | async-start | bytes 786432 | tf_op jit(solution)/shard_map/all_to_all | solution.py:96

commit v2 on v1

v2 whole, which is shorter than its diff:
```python
import jax
import jax.numpy as jnp
from jax import lax
from jax.experimental import pallas as pl
from jax.experimental.pallas import tpu as pltpu
from jax.sharding import Mesh, PartitionSpec as P

CLIP_NORM = 100.0
EW = ("z", "x_hi")
NS = ("y", "x_lo", "core")
PLANE = ("x_hi", "y", "x_lo", "core")
LANES = 128
STACK = 256
BF16 = jnp.bfloat16
F32 = jnp.float32


def vmem(count):
    return [pl.BlockSpec(memory_space=pltpu.VMEM)] * count


def neighbours(low_side, high_side, axes):
    count = lax.axis_size(axes)
    forward = [(i, i + 1) for i in range(count - 1)]
    backward = [(target, source) for source, target in forward]
    return lax.ppermute(high_side, axes, forward), lax.ppermute(low_side, axes, backward)


def sigmoid(x):
    return 0.5 * jnp.tanh(0.5 * x) + 0.5


def forward_kernel(
    frame, hidden_prev, top, bottom, left, right, weights, bias, cell_prev, grad_hidden, grad_cell,
    hidden, cell, grad_cell_prev, grads, edges, terms,
    joined, stacked, hidden_rows,
):
    height = grads.shape[1] // LANES
    units = hidden_prev.shape[0] // height
    inputs = frame.shape[0] // height
    channels = inputs + units
    joined[: inputs * height] = frame[...].astype(F32)
    joined[inputs * height :] = hidden_prev[...].astype(F32)
    lane = lax.broadcasted_iota(jnp.int32, (channels, LANES), 1)
    left_cells = left[...].astype(F32)
    right_cells = right[...].astype(F32)
    spare = STACK - 3 * channels
    ones_row = (lax.broadcasted_iota(jnp.int32, (spare, LANES), 0) == 0).astype(F32)
    for place in range(height + 2):
        if place == 0:
            row = top[...].astype(F32)
        elif place == height + 1:
            row = bottom[...].astype(F32)
        else:
            row = joined[pl.ds(place - 1, channels, stride=height), :]
        before = jnp.where(lane == 0, pltpu.roll(left_cells, (LANES - place) % LANES, 1), pltpu.roll(row, 1, 1))
        after = jnp.where(
            lane == LANES - 1, pltpu.roll(right_cells, LANES - 1 - place, 1), pltpu.roll(row, LANES - 1, 1)
        )
        stacked[:, place * LANES : (place + 1) * LANES] = jnp.concatenate([before, row, after, ones_row], 0).astype(
            BF16
        )
    bias_cells = jnp.broadcast_to(bias[...], (4 * units, LANES))
    for pair in range(height // 2):
        sums = jnp.zeros((4 * units, 2 * LANES), F32)
        for row_off in range(3):
            start = (2 * pair + row_off) * LANES
            sums = sums + jnp.dot(
                weights[:, row_off * STACK : (row_off + 1) * STACK],
                stacked[:, start : start + 2 * LANES],
                preferred_element_type=F32,
            )
        for half in range(2):
            n = 2 * pair + half
            at = pl.ds(n, units, stride=height)
            gates = sums[:, half * LANES : (half + 1) * LANES] + bias_cells
            input_gate = sigmoid(gates[:units])
            forget_gate = sigmoid(gates[units : 2 * units])
            cand_gate = jnp.tanh(gates[2 * units : 3 * units])
            output_gate = sigmoid(gates[3 * units :])
            old = cell_prev[at, :]
            down = grad_hidden[at, :]
            new = forget_gate * old + input_gate * cand_gate
            new_tanh = jnp.tanh(new)
            cell[at, :] = new
            hidden_rows[at, :] = output_gate * new_tanh
            cell_grad = grad_cell[at, :] + down * output_gate * (1.0 - new_tanh * new_tanh)
            grad_cell_prev[at, :] = cell_grad * forget_gate
            grads[:, n * LANES : (n + 1) * LANES] = jnp.concatenate(
                [
                    cell_grad * cand_gate * input_gate * (1.0 - input_gate),
                    cell_grad * old * forget_gate * (1.0 - forget_gate),
                    cell_grad * input_gate * (1.0 - cand_gate * cand_gate),
                    down * new_tanh * output_gate * (1.0 - output_gate),
                ],
                0,
            ).astype(BF16)
    hidden[...] = hidden_rows[...].astype(BF16)
    for row_off in range(3):
        terms[row_off * STACK : (row_off + 1) * STACK] = lax.dot_general(
            stacked[:, row_off * LANES : (row_off + height) * LANES],
            grads[...],
            (((1,), (1,)), ((), ())),
            preferred_element_type=F32,
        ).astype(BF16)
    source = lax.broadcasted_iota(jnp.int32, (height * LANES, LANES), 0)
    target = lax.broadcasted_iota(jnp.int32, (height * LANES, LANES), 1)
    wanted = jnp.where(target < height, target * LANES, (target - height) * LANES + LANES - 1)
    pick = ((source == wanted) & (target < 2 * height)).astype(F32).astype(BF16)
    edges[...] = jnp.dot(grads[...], pick, preferred_element_type=F32).astype(BF16)


def backward_kernel(weights, grads, top, bottom, left, right, grad_frame, grad_hidden_prev, sums, rows):
    height = grads.shape[1] // LANES
    inputs = grad_frame.shape[0] // height
    channels = rows.shape[0] // height
    lane = lax.broadcasted_iota(jnp.int32, (channels, LANES), 1)
    outer = jnp.dot(weights[...], jnp.concatenate([left[...], right[...]], 1), preferred_element_type=F32)
    first = jnp.zeros((channels, LANES), F32)
    last = jnp.zeros((channels, LANES), F32)
    for row_off in range(3):
        low, high = 3 * row_off * channels, (3 * row_off + 2) * channels
        first = first + pltpu.roll(outer[high : high + channels, :LANES], (LANES - 2 + row_off) % LANES, 1)
        last = last + pltpu.roll(outer[low : low + channels, LANES:], (LANES - 2 + row_off) % LANES, 1)
    for place in range(0, height + 2, 2):
        if place == 0:
            cells = jnp.concatenate([top[...], grads[:, :LANES]], 1)
        elif place == height:
            cells = jnp.concatenate([grads[:, (height - 1) * LANES :], bottom[...]], 1)
        else:
            cells = grads[:, (place - 1) * LANES : (place + 1) * LANES]
        product = jnp.dot(weights[...], cells, preferred_element_type=F32)
        for half in range(2):
            for row_off in range(3):
                n = place + half - 1 + row_off - 1
                if not 0 <= n < height:
                    continue
                for col_off in range(3):
                    start = (3 * row_off + col_off) * channels
                    piece = product[start : start + channels, half * LANES : (half + 1) * LANES]
                    if row_off == 2 or (place + half == 0):
                        sums[n, col_off] = piece
                    else:
                        sums[n, col_off] = sums[n, col_off] + piece
    for n in range(height):
        total = sums[n, 1]
        total = total + jnp.where(
            lane == LANES - 1, pltpu.roll(last, LANES - 1 - n, 1), pltpu.roll(sums[n, 0], LANES - 1, 1)
        )
        total = total + jnp.where(
            lane == 0, pltpu.roll(first, (LANES - n) % LANES, 1), pltpu.roll(sums[n, 2], 1, 1)
        )
        rows[pl.ds(n, channels, stride=height), :] = total
    grad_frame[...] = rows[: inputs * height].astype(BF16)
    grad_hidden_prev[...] = rows[inputs * height :].astype(BF16)


def finish_kernel(total, kernel_step, bias_step):
    block = kernel_step.shape[0] // 3
    parts = [total[i * STACK : i * STACK + block].astype(F32) for i in range(3)]
    bias_grad = total[block : block + 8].astype(F32)[:1]
    norm = jnp.sqrt(sum(jnp.sum(part * part) for part in parts) + jnp.sum(bias_grad * bias_grad))
    factor = jnp.minimum(1.0, CLIP_NORM / norm)
    for i, part in enumerate(parts):
        kernel_step[i * block : (i + 1) * block] = part * factor
    bias_step[...] = bias_grad * factor


def sum_everywhere(terms):
    rows, width = terms.shape
    plane = lax.axis_size(PLANE)
    deep = lax.axis_size("z")
    share = rows // plane
    mine = lax.all_to_all(terms, PLANE, 0, 0, tiled=True).reshape(plane, share, width)
    mine = jnp.sum(mine.astype(F32), 0)
    mine = jnp.broadcast_to(mine[None], (deep, share, width))
    mine = lax.all_to_all(mine, "z", 0, 0, tiled=True)
    mine = jnp.sum(mine, 0).astype(BF16)
    mine = jnp.broadcast_to(mine[None], (plane, share, width)).reshape(rows, width)
    return lax.all_to_all(mine, PLANE, 0, 0, tiled=True)


def end_columns(top, low, high, bottom):
    spare = ((0, 0), (0, LANES - low.shape[1] - 2))
    return (
        jnp.pad(jnp.concatenate([top[:, :1], low, bottom[:, :1]], 1), spare),
        jnp.pad(jnp.concatenate([top[:, -1:], high, bottom[:, -1:]], 1), spare),
    )


def shape(rows, columns, kind):
    return jax.ShapeDtypeStruct((rows, columns), kind)


def per_device(frame, hidden_prev, cell_prev, kernel, bias, grad_hidden, grad_cell):
    inputs, height, breadth = frame.shape
    units = hidden_prev.shape[0]
    channels = inputs + units
    gate_rows = kernel.shape[0]
    cells = height * breadth
    row = jnp.concatenate([frame[:, 0], hidden_prev[:, 0]], 0)
    last_row = jnp.concatenate([frame[:, -1], hidden_prev[:, -1]], 0)
    column = jnp.concatenate([frame[:, :, 0], hidden_prev[:, :, 0]], 0)
    last_column = jnp.concatenate([frame[:, :, -1], hidden_prev[:, :, -1]], 0)
    weights = kernel.reshape(gate_rows, 3, 3 * channels)
    weights = jnp.pad(weights, ((0, 0), (0, 0), (0, STACK - 3 * channels))).reshape(gate_rows, 3 * STACK)
    weights_back = kernel.T
    top, bottom = neighbours(row, last_row, NS)
    left, right = neighbours(*end_columns(top, column, last_column, bottom), EW)

    hidden, cell, grad_cell_prev, grads, edges, terms = pl.pallas_call(
        forward_kernel,
        out_shape=(
            shape(units * height, breadth, BF16),
            shape(units * height, breadth, F32),
            shape(units * height, breadth, F32),
            shape(gate_rows, cells, BF16),
            shape(gate_rows, LANES, BF16),
            shape(3 * STACK, gate_rows, BF16),
        ),
        in_specs=vmem(11),
        out_specs=tuple(vmem(6)),
        scratch_shapes=[
            pltpu.VMEM((channels * height, breadth), F32),
            pltpu.VMEM((STACK, (height + 2) * breadth), BF16),
            pltpu.VMEM((units * height, breadth), F32),
        ],
        compiler_params=pltpu.CompilerParams(vmem_limit_bytes=40 * 2**20),
        cost_estimate=pl.CostEstimate(flops=1_400_000_000, bytes_accessed=6_000_000, transcendentals=700_000),
    )(
        frame.reshape(inputs * height, breadth),
        hidden_prev.reshape(units * height, breadth),
        top,
        bottom,
        left,
        right,
        weights,
        bias[:, None],
        cell_prev.reshape(units * height, breadth),
        grad_hidden.reshape(units * height, breadth),
        grad_cell.reshape(units * height, breadth),
    )

    grad_top, grad_bottom = neighbours(grads[:, :LANES], grads[:, cells - LANES :], NS)
    grad_left, grad_right = neighbours(
        *end_columns(grad_top, edges[:, :height], edges[:, height : 2 * height], grad_bottom), EW
    )
    total = sum_everywhere(terms)
    grad_frame, grad_hidden_prev = pl.pallas_call(
        backward_kernel,
        out_shape=(shape(inputs * height, breadth, BF16), shape(units * height, breadth, BF16)),
        in_specs=vmem(6),
        out_specs=tuple(vmem(2)),
        scratch_shapes=[
            pltpu.VMEM((height, 3, channels, breadth), F32),
            pltpu.VMEM((channels * height, breadth), F32),
        ],
        compiler_params=pltpu.CompilerParams(vmem_limit_bytes=40 * 2**20),
        cost_estimate=pl.CostEstimate(flops=764_000_000, bytes_accessed=3_000_000, transcendentals=0),
    )(weights_back, grads, grad_top, grad_bottom, grad_left, grad_right)
    kernel_step, bias_step = pl.pallas_call(
        finish_kernel,
        out_shape=(shape(9 * channels, gate_rows, F32), shape(1, gate_rows, F32)),
        in_specs=vmem(1),
        out_specs=tuple(vmem(2)),
        compiler_params=pltpu.CompilerParams(vmem_limit_bytes=40 * 2**20),
    )(total)
    whole = (units, height, breadth)
    return (
        hidden.reshape(whole),
        cell.reshape(whole),
        grad_frame.reshape(frame.shape),
        grad_hidden_prev.reshape(whole),
        grad_cell_prev.reshape(whole),
        kernel_step.T,
        bias_step.reshape(gate_rows),
    )


def solution(mesh):
    mesh = Mesh(mesh.devices.reshape(16, 2, 4, 2, 2), EW + NS)
    grid = P(None, NS, EW)
    return jax.shard_map(
        per_device,
        mesh=mesh,
        in_specs=(grid, grid, grid, P(), P(), grid, grid),
        out_specs=(grid, grid, grid, grid, grid, P(), P()),
        check_vma=False,
    )
```

time: 160 us -> 108 us (0.68)
  the two profiles are of different devices: /device:TPU:1 before, /device:TPU:32 now
where the time goes in v2:
time: 108 us; the launch traced here: 107 us
  starting transfers between devices  41.5 us (38%)
  waiting for transfers between devices  29.5 us (27%)
  blocking collectives  20.3 us (19%)
  Pallas kernels  7.39 us (7%)
  local copies, waits for them, and re-layouts  7.27 us (7%)
    all_to_all x1, blocking collectives, sum_everywhere(): lax.all_to_all(terms, PLANE, 0, 0, tiled=True).reshape(plane, share, width)  20.3 us
    all_to_all x1, waiting for transfers between devices, sum_everywhere(): mine = lax.all_to_all(mine, 'z', 0, 0, tiled=True)  18.7 us
    all_to_all x1, starting transfers between devices, sum_everywhere(): mine = lax.all_to_all(mine, 'z', 0, 0, tiled=True)  15.1 us
    ppermute x4, starting transfers between devices, neighbours(): lax.ppermute(low_side, axes, backward)  12.9 us
    ppermute x4, starting transfers between devices, neighbours(): lax.ppermute(high_side, axes, forward)  9.59 us
    ppermute x4, waiting for transfers between devices, neighbours(): lax.ppermute(high_side, axes, forward)  5.63 us
    ppermute x4, waiting for transfers between devices, neighbours(): lax.ppermute(low_side, axes, backward)  5.13 us
    pallas_call x1, Pallas kernels, per_device(): pl.pallas_call(forward_kernel, out_shape=(shape(units * height, breadth,...  4.26 us
  transfers between devices with their start and end apart: 10, of which 5 were waited for; matrix products, arithmetic and copies ran while one was open for 3% of the time, Pallas kernels for 2%

profile of v2, /device:TPU:32, one launch (start us, length us, event | category | flops | bytes accessed | tf_op | source)
XLA Modules:
  0.0 107.3 jit_solution(3831692145727120784)
XLA Ops:
  0.6 0.0 copy-start
  0.6 0.8 fusion.31
  1.4 1.0 fusion.26
  2.5 1.7 %collective-permute-start = (bf16[72,128]{1,0:T(8,128)(2,1)S(1)}, bf16[72,128]{1,0:T(8,128)(2,1)S(1)}, u32[]{:S(2)}, u32[]{:S(2)}) collective-permute-start(bf16[72,128]{1,0:T(8,128)(2,1)S(1)} %pad_maximum_fusion), channel_id=1, source_target_pairs={{0,1},{1,2},{2,3},{3,4},{4,5},{5,6},{6,7},{7,8},{8,9},{9,10},{10,1... | collective-permute-start | bytes 55304 | tf_op jit(solution)/shard_map/ppermute | solution.py:26
  4.3 1.3 %collective-permute-start.1 = (bf16[72,128]{1,0:T(8,128)(2,1)S(1)}, bf16[72,128]{1,0:T(8,128)(2,1)S(1)}, u32[]{:S(2)}, u32[]{:S(2)}) collective-permute-start(bf16[72,128]{1,0:T(8,128)(2,1)S(1)} %pad_maximum_fusion.1), channel_id=1, source_target_pairs={{1,0},{2,1},{3,2},{4,3},{5,4},{6,5},{7,6},{8,7},{9,8},{10,9},{11,1... | collective-permute-start | bytes 55304 | tf_op jit(solution)/shard_map/ppermute | solution.py:26
  5.6 0.0 copy-start.2
  5.6 0.1 fusion.25
  5.7 0.6 copy-done.2
  6.4 0.1 fusion.30
  6.4 0.1 copy.89
  6.6 0.1 copy.87
  6.7 0.5 copy.90
  7.2 0.5 copy.88
  7.7 1.0 collective-permute-done.1.bottom
  8.6 0.1 fusion.33
  8.7 0.1 fusion.32
  8.8 0.1 fusion.19
  8.9 4.6 %collective-permute-start.2 = (bf16[72,128]{1,0:T(8,128)(2,1)S(1)}, bf16[72,128]{1,0:T(8,128)(2,1)S(1)}, u32[]{:S(2)}, u32[]{:S(2)}) collective-permute-start(bf16[72,128]{1,0:T(8,128)(2,1)S(1)} %fusion.19), channel_id=1, source_target_pairs={{0,16},{16,32},{32,48},{48,64},{64,80},{80,96},{96,112},{112,128},... | collective-permute-start | bytes 55304 | tf_op jit(solution)/shard_map/ppermute | solution.py:26
  13.5 0.1 fusion.22
  13.6 0.0 copy-start.6
  13.6 3.6 %collective-permute-start.3 = (bf16[72,128]{1,0:T(8,128)(2,1)S(1)}, bf16[72,128]{1,0:T(8,128)(2,1)S(1)}, u32[]{:S(2)}, u32[]{:S(2)}) collective-permute-start(bf16[72,128]{1,0:T(8,128)(2,1)S(1)} %fusion.22), channel_id=1, source_target_pairs={{16,0},{32,16},{48,32},{64,48},{80,64},{96,80},{112,96},{128,112},... | collective-permute-start | bytes 55304 | tf_op jit(solution)/shard_map/ppermute | solution.py:26
  17.3 0.1 copy.82.bias
  17.4 0.0 copy-start.4
  17.5 0.0 copy-start.3
  17.5 0.2 copy.81.weights
  17.7 3.1 %collective-permute-done.3.right = bf16[72,128]{1,0:T(8,128)(2,1)S(1)} collective-permute-done((bf16[72,128]{1,0:T(8,128)(2,1)S(1)}, bf16[72,128]{1,0:T(8,128)(2,1)S(1)}, u32[]{:S(2)}, u32[]{:S(2)}) %collective-permute-start.3) | collective-permute-done | bytes 18464 | tf_op jit(solution)/shard_map/ppermute | solution.py:26
  20.8 1.0 copy-done.5
  21.9 4.3 %shard_map.126 = (bf16[1024,128]{1,0:T(8,128)(2,1)}, f32[1024,128]{1,0:T(8,128)}, f32[1024,128]{1,0:T(8,128)}, bf16[256,2048]{1,0:T(8,128)(2,1)S(1)}, bf16[256,1...) custom-call(bf16[128,128]{1,0:T(8,128)(2,1)S(1)} %bitcast.39, bf16[1024,128]{1,0:T(8,128)(2,1)S(1)} %bitcast.35, ...), custom_call_target="tpu_custom_call" | custom-call | flops 1400000000 | bytes 6000000 | tf_op jit(solution)/shard_map/pallas_call | solution.py:211
  26.1 20.3 %all_to_all.22 = bf16[32,24,256]{2,1,0:T(8,128)(2,1)S(1)} all-to-all(bf16[32,24,256]{2,1,0:T(8,128)(2,1)S(1)} %bitcast.36), channel_id=1, replica_groups=mesh['z'=16,'x_hi'=2,'y'=4,'x_lo'=2,'core'=2] {'x_hi','y','x_lo','core'}, dimensions={0} | all-to-all | bytes 786432 | tf_op jit(solution)/shard_map/all_to_all | solution.py:174
  46.4 0.1 convert_reduce_fusion
  46.4 0.8 broadcast_in_dim.7
  47.2 15.1 %all-to-all-start.1 = ((f32[16,24,256]{2,1,0:T(8,128)}), f32[16,24,256]{2,1,0:T(8,128)S(1)}, u32[]{:S(2)}, u32[]{:S(2)}) async-start(f32[16,24,256]{2,1,0:T(8,128)} %broadcast_in_dim.7), calls=%async_computation.1 | async-start | bytes 786432 | tf_op jit(solution)/shard_map/all_to_all | solution.py:177
  62.3 1.3 %collective-permute-start.4 = (bf16[256,128]{1,0:T(8,128)(2,1)S(1)}, bf16[256,128]{1,0:T(8,128)(2,1)S(1)}, u32[]{:S(2)}, u32[]{:S(2)}) collective-permute-start(bf16[256,128]{1,0:T(8,128)(2,1)S(1)} %get-tuple-element.28), channel_id=1, source_target_pairs={{0,1},{1,2},{2,3},{3,4},{4,5},{5,6},{6,7},{7,8},{8,9},{9,10},{10,1... | collective-permute-start | bytes 196616 | tf_op jit(solution)/shard_map/ppermute | solution.py:26
  63.6 0.1 fusion.28
  63.7 1.3 %collective-permute-start.5 = (bf16[256,128]{1,0:T(8,128)(2,1)S(1)}, bf16[256,128]{1,0:T(8,128)(2,1)S(1)}, u32[]{:S(2)}, u32[]{:S(2)}) collective-permute-start(bf16[256,128]{1,0:T(8,128)(2,1)S(1)} %get-tuple-element.27), channel_id=1, source_target_pairs={{1,0},{2,1},{3,2},{4,3},{5,4},{6,5},{7,6},{8,7},{9,8},{10,9},{11,1... | collective-permute-start | bytes 196616 | tf_op jit(solution)/shard_map/ppermute | solution.py:26
  65.0 0.1 fusion.27
  65.1 18.7 %all-to-all-done.1 = f32[16,24,256]{2,1,0:T(8,128)S(1)} async-done(((f32[16,24,256]{2,1,0:T(8,128)}), f32[16,24,256]{2,1,0:T(8,128)S(1)}, u32[]{:S(2)}, u32[]{:S(2)}) %all-to-all-start.1) | async-done | bytes 393248 | tf_op jit(solution)/shard_map/all_to_all | solution.py:177
  83.9 0.8 broadcast_in_dim.8
  84.6 3.9 %all-to-all-start.2 = ((bf16[32,24,256]{2,1,0:T(8,128)(2,1)}), bf16[32,24,256]{2,1,0:T(8,128)(2,1)S(1)}, u32[]{:S(2)}, u32[]{:S(2)}) async-start(bf16[32,24,256]{2,1,0:T(8,128)(2,1)} %broadcast_in_dim.8), calls=%async_computation.2 | async-start | bytes 786432 | tf_op jit(solution)/shard_map/all_to_all | solution.py:180
  88.5 0.1 fusion.29
  88.6 0.1 fusion.9
  88.8 6.7 %collective-permute-start.7 = (bf16[256,128]{1,0:T(8,128)(2,1)S(1)}, bf16[256,128]{1,0:T(8,128)(2,1)S(1)}, u32[]{:S(2)}, u32[]{:S(2)}) collective-permute-start(bf16[256,128]{1,0:T(8,128)(2,1)S(1)} %fusion.9), channel_id=1, source_target_pairs={{16,0},{32,16},{48,32},{64,48},{80,64},{96,80},{112,96},{128,112},... | collective-permute-start | bytes 196616 | tf_op jit(solution)/shard_map/ppermute | solution.py:26
  95.5 0.1 fusion.7
  95.6 1.9 %collective-permute-start.6 = (bf16[256,128]{1,0:T(8,128)(2,1)S(1)}, bf16[256,128]{1,0:T(8,128)(2,1)S(1)}, u32[]{:S(2)}, u32[]{:S(2)}) collective-permute-start(bf16[256,128]{1,0:T(8,128)(2,1)S(1)} %fusion.7), channel_id=1, source_target_pairs={{0,16},{16,32},{32,48},{48,64},{64,80},{80,96},{96,112},{112,128},... | collective-permute-start | bytes 196616 | tf_op jit(solution)/shard_map/ppermute | solution.py:26
  97.5 1.0 collective-permute-done.7.right
  98.5 5.6 %collective-permute-done.6.left = bf16[256,128]{1,0:T(8,128)(2,1)S(1)} collective-permute-done((bf16[256,128]{1,0:T(8,128)(2,1)S(1)}, bf16[256,128]{1,0:T(8,128)(2,1)S(1)}, u32[]{:S(2)}, u32[]{:S(2)}) %collective-permute-start.6) | collective-permute-done | bytes 65568 | tf_op jit(solution)/shard_map/ppermute | solution.py:26
  104.2 1.9 %shard_map.127 = (bf16[128,128]{1,0:T(8,128)(2,1)}, bf16[1024,128]{1,0:T(8,128)(2,1)}) custom-call(bf16[648,256]{1,0:T(8,128)(2,1)S(1)} %bitcast.38, bf16[256,2048]{1,0:T(8,128)(2,1)S(1)} %get-tuple-element.19.grads, bf16[256,128]{1,0:T(8,128)(2,1)S(1)} %collective-permute-done.4.top, bf16[256,128]{1,0:T(8,128)(2,1)S(1)} %collective-permute-done.5.bottom, ...), custom_call_target="tpu_custom_call" | custom-call | flops 764000000 | bytes 3000000 | tf_op jit(solution)/shard_map/pallas_call | solution.py:249
  106.1 1.2 %shard_map.128 = (f32[648,256]{1,0:T(8,128)}, f32[1,256]{1,0:T(1,128)}) custom-call(bf16[768,256]{1,0:T(8,128)(2,1)S(1)} %bitcast.34), custom_call_target="tpu_custom_call" | custom-call | tf_op jit(solution)/shard_map/pallas_call | solution.py:261
  (21 shorter events, 0.1 us)
Async XLA Ops:
  0.6 5.0 %copy-start = (bf16[64,16,128]{2,1,0:T(8,128)(2,1)S(1)}, bf16[64,16,128]{2,1,0:T(8,128)(2,1)}, u32[]{:S(2)}) copy-start(bf16[64,16,128]{2,1,0:T(8,128)(2,1)} %param.8) | copy-start | bytes 786436
  2.5 6.2 %collective-permute-start = (bf16[72,128]{1,0:T(8,128)(2,1)S(1)}, bf16[72,128]{1,0:T(8,128)(2,1)S(1)}, u32[]{:S(2)}, u32[]{:S(2)}) collective-permute-start(bf16[72,128]{1,0:T(8,128)(2,1)S(1)} %pad_maximum_fusion), channel_id=1, source_target_pairs={{0,1},{1,2},{2,3},{3,4},{4,5},{5,6},{6,7},{7,8},{8,9},{9,10},{10,1... | collective-permute-start | bytes 55304 | tf_op jit(solution)/shard_map/ppermute | solution.py:26
  4.3 4.4 %collective-permute-start.1 = (bf16[72,128]{1,0:T(8,128)(2,1)S(1)}, bf16[72,128]{1,0:T(8,128)(2,1)S(1)}, u32[]{:S(2)}, u32[]{:S(2)}) collective-permute-start(bf16[72,128]{1,0:T(8,128)(2,1)S(1)} %pad_maximum_fusion.1), channel_id=1, source_target_pairs={{1,0},{2,1},{3,2},{4,3},{5,4},{6,5},{7,6},{8,7},{9,8},{10,9},{11,1... | collective-permute-start | bytes 55304 | tf_op jit(solution)/shard_map/ppermute | solution.py:26
  5.6 0.8 copy-start.2
  7.2 10.2 %copy-start.1 = (bf16[256,648]{0,1:T(8,128)(2,1)S(1)}, bf16[256,648]{0,1:T(8,128)(2,1)}, u32[]{:S(2)}) copy-start(bf16[256,648]{0,1:T(8,128)(2,1)} %param.10) | copy-start | bytes 995332
  8.9 8.8 %collective-permute-start.2 = (bf16[72,128]{1,0:T(8,128)(2,1)S(1)}, bf16[72,128]{1,0:T(8,128)(2,1)S(1)}, u32[]{:S(2)}, u32[]{:S(2)}) collective-permute-start(bf16[72,128]{1,0:T(8,128)(2,1)S(1)} %fusion.19), channel_id=1, source_target_pairs={{0,16},{16,32},{32,48},{48,64},{64,80},{80,96},{96,112},{112,128},... | collective-permute-start | bytes 55304 | tf_op jit(solution)/shard_map/ppermute | solution.py:26
  13.6 3.6 %copy-start.6 = (f32[256]{0:T(256)S(1)}, f32[256]{0:T(256)}, u32[]{:S(2)}) copy-start(f32[256]{0:T(256)} %param.11) | copy-start | bytes 3076
  13.6 7.2 %collective-permute-start.3 = (bf16[72,128]{1,0:T(8,128)(2,1)S(1)}, bf16[72,128]{1,0:T(8,128)(2,1)S(1)}, u32[]{:S(2)}, u32[]{:S(2)}) collective-permute-start(bf16[72,128]{1,0:T(8,128)(2,1)S(1)} %fusion.22), channel_id=1, source_target_pairs={{16,0},{32,16},{48,32},{64,48},{80,64},{96,80},{112,96},{128,112},... | collective-permute-start | bytes 55304 | tf_op jit(solution)/shard_map/ppermute | solution.py:26
  17.4 3.4 %copy-start.4 = (f32[64,16,128]{2,1,0:T(8,128)S(1)}, f32[64,16,128]{2,1,0:T(8,128)}, u32[]{:S(2)}) copy-start(f32[64,16,128]{2,1,0:T(8,128)} %param.12) | copy-start | bytes 1572868
  17.5 3.3 %copy-start.3 = (f32[64,16,128]{2,1,0:T(8,128)S(1)}, f32[64,16,128]{2,1,0:T(8,128)}, u32[]{:S(2)}) copy-start(f32[64,16,128]{2,1,0:T(8,128)} %param.9) | copy-start | bytes 1572868
  20.8 1.0 copy-start.5
  47.2 36.6 %all-to-all-start.1 = ((f32[16,24,256]{2,1,0:T(8,128)}), f32[16,24,256]{2,1,0:T(8,128)S(1)}, u32[]{:S(2)}, u32[]{:S(2)}) async-start(f32[16,24,256]{2,1,0:T(8,128)} %broadcast_in_dim.7), calls=%async_computation.1 | async-start | bytes 786432 | tf_op jit(solution)/shard_map/all_to_all | solution.py:177
  62.3 2.7 %collective-permute-start.4 = (bf16[256,128]{1,0:T(8,128)(2,1)S(1)}, bf16[256,128]{1,0:T(8,128)(2,1)S(1)}, u32[]{:S(2)}, u32[]{:S(2)}) collective-permute-start(bf16[256,128]{1,0:T(8,128)(2,1)S(1)} %get-tuple-element.28), channel_id=1, source_target_pairs={{0,1},{1,2},{2,3},{3,4},{4,5},{5,6},{6,7},{7,8},{8,9},{9,10},{10,1... | collective-permute-start | bytes 196616 | tf_op jit(solution)/shard_map/ppermute | solution.py:26
  63.7 24.8 %collective-permute-start.5 = (bf16[256,128]{1,0:T(8,128)(2,1)S(1)}, bf16[256,128]{1,0:T(8,128)(2,1)S(1)}, u32[]{:S(2)}, u32[]{:S(2)}) collective-permute-start(bf16[256,128]{1,0:T(8,128)(2,1)S(1)} %get-tuple-element.27), channel_id=1, source_target_pairs={{1,0},{2,1},{3,2},{4,3},{5,4},{6,5},{7,6},{8,7},{9,8},{10,9},{11,1... | collective-permute-start | bytes 196616 | tf_op jit(solution)/shard_map/ppermute | solution.py:26
  84.6 21.5 %all-to-all-start.2 = ((bf16[32,24,256]{2,1,0:T(8,128)(2,1)}), bf16[32,24,256]{2,1,0:T(8,128)(2,1)S(1)}, u32[]{:S(2)}, u32[]{:S(2)}) async-start(bf16[32,24,256]{2,1,0:T(8,128)(2,1)} %broadcast_in_dim.8), calls=%async_computation.2 | async-start | bytes 786432 | tf_op jit(solution)/shard_map/all_to_all | solution.py:180
  88.8 9.8 %collective-permute-start.7 = (bf16[256,128]{1,0:T(8,128)(2,1)S(1)}, bf16[256,128]{1,0:T(8,128)(2,1)S(1)}, u32[]{:S(2)}, u32[]{:S(2)}) collective-permute-start(bf16[256,128]{1,0:T(8,128)(2,1)S(1)} %fusion.9), channel_id=1, source_target_pairs={{16,0},{32,16},{48,32},{64,48},{80,64},{96,80},{112,96},{128,112},... | collective-permute-start | bytes 196616 | tf_op jit(solution)/shard_map/ppermute | solution.py:26
  95.6 8.6 %collective-permute-start.6 = (bf16[256,128]{1,0:T(8,128)(2,1)S(1)}, bf16[256,128]{1,0:T(8,128)(2,1)S(1)}, u32[]{:S(2)}, u32[]{:S(2)}) collective-permute-start(bf16[256,128]{1,0:T(8,128)(2,1)S(1)} %fusion.7), channel_id=1, source_target_pairs={{0,16},{16,32},{32,48},{48,64},{64,80},{80,96},{96,112},{112,128},... | collective-permute-start | bytes 196616 | tf_op jit(solution)/shard_map/ppermute | solution.py:26

commit v3 on v2

--- a/solution.py
+++ b/solution.py
@@ -6,7 +6,7 @@
 from jax.sharding import Mesh, PartitionSpec as P
 
 CLIP_NORM = 100.0
-EW = ("z", "x_hi")
+EW = ("z_hi", "z_lo", "x_hi")
 NS = ("y", "x_lo", "core")
 PLANE = ("x_hi", "y", "x_lo", "core")
 LANES = 128
@@ -166,18 +166,24 @@
     bias_step[...] = bias_grad * factor
 
 
-def sum_everywhere(terms):
-    rows, width = terms.shape
-    plane = lax.axis_size(PLANE)
-    deep = lax.axis_size("z")
-    share = rows // plane
-    mine = lax.all_to_all(terms, PLANE, 0, 0, tiled=True).reshape(plane, share, width)
-    mine = jnp.sum(mine.astype(F32), 0)
-    mine = jnp.broadcast_to(mine[None], (deep, share, width))
-    mine = lax.all_to_all(mine, "z", 0, 0, tiled=True)
-    mine = jnp.sum(mine, 0).astype(BF16)
-    mine = jnp.broadcast_to(mine[None], (plane, share, width)).reshape(rows, width)
-    return lax.all_to_all(mine, PLANE, 0, 0, tiled=True)
+def sum_kernel(parts, *rest):
+    copies = rest[-1]
+    total = jnp.sum(parts[...].astype(F32), 0).astype(copies.dtype)
+    copies[...] = jnp.broadcast_to(total[None], copies.shape)
+
+
+def summed(parts, copies, kind, *after):
+    return pl.pallas_call(
+        sum_kernel,
+        out_shape=jax.ShapeDtypeStruct((copies,) + parts.shape[1:], kind),
+        in_specs=vmem(1) + [pl.BlockSpec(memory_space=pl.ANY)] * len(after),
+        out_specs=vmem(1)[0],
+        compiler_params=pltpu.CompilerParams(vmem_limit_bytes=8 * 2**20),
+    )(parts, *after)
+
+
+def exchanged(copies, axes):
+    return lax.all_to_all(copies, axes, 0, 0, tiled=True)
 
 
 def end_columns(top, low, high, bottom):
@@ -225,7 +231,7 @@
             pltpu.VMEM((STACK, (height + 2) * breadth), BF16),
             pltpu.VMEM((units * height, breadth), F32),
         ],
-        compiler_params=pltpu.CompilerParams(vmem_limit_bytes=40 * 2**20),
+        compiler_params=pltpu.CompilerParams(vmem_limit_bytes=16 * 2**20),
         cost_estimate=pl.CostEstimate(flops=1_400_000_000, bytes_accessed=6_000_000, transcendentals=700_000),
     )(
         frame.reshape(inputs * height, breadth),
@@ -241,11 +247,17 @@
         grad_cell.reshape(units * height, breadth),
     )
 
+    plane = lax.axis_size(PLANE)
+    low, high = lax.axis_size("z_lo"), lax.axis_size("z_hi")
+    mine = exchanged(terms.reshape(plane, -1, gate_rows), PLANE)
     grad_top, grad_bottom = neighbours(grads[:, :LANES], grads[:, cells - LANES :], NS)
+    mine = exchanged(summed(mine, low, F32, grad_top, grad_bottom), "z_lo")
+    mine = exchanged(summed(mine, high, F32), "z_hi")
     grad_left, grad_right = neighbours(
         *end_columns(grad_top, edges[:, :height], edges[:, height : 2 * height], grad_bottom), EW
     )
-    total = sum_everywhere(terms)
+    mine = summed(mine, plane, BF16, grad_left, grad_right)
+    total = exchanged(mine, PLANE).reshape(3 * STACK, gate_rows)
     grad_frame, grad_hidden_prev = pl.pallas_call(
         backward_kernel,
         out_shape=(shape(inputs * height, breadth, BF16), shape(units * height, breadth, BF16)),
@@ -255,7 +267,7 @@
             pltpu.VMEM((height, 3, channels, breadth), F32),
             pltpu.VMEM((channels * height, breadth), F32),
         ],
-        compiler_params=pltpu.CompilerParams(vmem_limit_bytes=40 * 2**20),
+        compiler_params=pltpu.CompilerParams(vmem_limit_bytes=16 * 2**20),
         cost_estimate=pl.CostEstimate(flops=764_000_000, bytes_accessed=3_000_000, transcendentals=0),
     )(weights_back, grads, grad_top, grad_bottom, grad_left, grad_right)
     kernel_step, bias_step = pl.pallas_call(
@@ -263,7 +275,7 @@
         out_shape=(shape(9 * channels, gate_rows, F32), shape(1, gate_rows, F32)),
         in_specs=vmem(1),
         out_specs=tuple(vmem(2)),
-        compiler_params=pltpu.CompilerParams(vmem_limit_bytes=40 * 2**20),
+        compiler_params=pltpu.CompilerParams(vmem_limit_bytes=16 * 2**20),
     )(total)
     whole = (units, height, breadth)
     return (
@@ -278,7 +290,7 @@
 
 
 def solution(mesh):
-    mesh = Mesh(mesh.devices.reshape(16, 2, 4, 2, 2), EW + NS)
+    mesh = Mesh(mesh.devices.reshape(4, 4, 2, 4, 2, 2), EW + NS)
     grid = P(None, NS, EW)
     return jax.shard_map(
         per_device,

time: 108 us -> 106 us (0.981)
  the two profiles are of different devices: /device:TPU:32 before, /device:TPU:1 now
where the time goes in v3:
time: 106 us; the launch traced here: 105 us
  starting transfers between devices  62.5 us (59%)
  waiting for transfers between devices  25.8 us (24%)
  Pallas kernels  9.65 us (9%)
  local copies, waits for them, and re-layouts  5.73 us (5%)
    all_to_all x4, starting transfers between devices, exchanged(): return lax.all_to_all(copies, axes, 0, 0, tiled=True)  37 us
    all_to_all x4, waiting for transfers between devices, exchanged(): return lax.all_to_all(copies, axes, 0, 0, tiled=True)  17.8 us
    ppermute x4, starting transfers between devices, neighbours(): lax.ppermute(high_side, axes, forward)  15.2 us
    ppermute x4, starting transfers between devices, neighbours(): lax.ppermute(low_side, axes, backward)  10.3 us
    ppermute x4, waiting for transfers between devices, neighbours(): lax.ppermute(low_side, axes, backward)  6.34 us
    pallas_call x1, Pallas kernels, per_device(): pl.pallas_call(forward_kernel, out_shape=(shape(units * height, breadth,...  4.38 us
    unnamed x22, local copies, waits for them, and re-layouts  2.92 us
    pallas_call x3, Pallas kernels, summed(): pl.pallas_call(sum_kernel, out_shape=jax.ShapeDtypeStruct((copies,) + par...  2.14 us
  transfers between devices with their start and end apart: 12, of which 7 were waited for; matrix products, arithmetic and copies ran while one was open for 2% of the time, Pallas kernels for 2%

profile of v3, /device:TPU:1, one launch (start us, length us, event | category | flops | bytes accessed | tf_op | source)
XLA Modules:
  0.0 105.0 jit_solution(7707448304614267942)
XLA Ops:
  0.6 0.0 copy-start
  0.6 0.8 fusion.31
  1.4 1.0 fusion.26
  2.5 4.5 %collective-permute-start = (bf16[72,128]{1,0:T(8,128)(2,1)S(1)}, bf16[72,128]{1,0:T(8,128)(2,1)S(1)}, u32[]{:S(2)}, u32[]{:S(2)}) collective-permute-start(bf16[72,128]{1,0:T(8,128)(2,1)S(1)} %pad_maximum_fusion), channel_id=1, source_target_pairs={{0,1},{1,2},{2,3},{3,4},{4,5},{5,6},{6,7},{7,8},{8,9},{9,10},{10,1... | collective-permute-start | bytes 55304 | tf_op jit(solution)/shard_map/ppermute | solution.py:26
  7.1 5.6 %collective-permute-start.1 = (bf16[72,128]{1,0:T(8,128)(2,1)S(1)}, bf16[72,128]{1,0:T(8,128)(2,1)S(1)}, u32[]{:S(2)}, u32[]{:S(2)}) collective-permute-start(bf16[72,128]{1,0:T(8,128)(2,1)S(1)} %pad_maximum_fusion.1), channel_id=1, source_target_pairs={{1,0},{2,1},{3,2},{4,3},{5,4},{6,5},{7,6},{8,7},{9,8},{10,9},{11,1... | collective-permute-start | bytes 55304 | tf_op jit(solution)/shard_map/ppermute | solution.py:26
  12.6 0.1 fusion.25
  12.8 0.6 copy-done.2
  13.4 0.1 fusion.30
  13.5 0.1 copy.89
  13.6 0.1 copy.87
  13.7 0.5 copy.90
  14.2 0.5 copy.88
  14.7 0.1 fusion.33
  14.8 0.1 fusion.32
  14.9 0.1 fusion.19
  15.0 1.8 %collective-permute-start.2 = (bf16[72,128]{1,0:T(8,128)(2,1)S(1)}, bf16[72,128]{1,0:T(8,128)(2,1)S(1)}, u32[]{:S(2)}, u32[]{:S(2)}) collective-permute-start(bf16[72,128]{1,0:T(8,128)(2,1)S(1)} %fusion.19), channel_id=1, source_target_pairs={{0,16},{16,32},{32,48},{48,64},{64,80},{80,96},{96,112},{112,128},... | collective-permute-start | bytes 55304 | tf_op jit(solution)/shard_map/ppermute | solution.py:26
  16.7 0.1 fusion.22
  16.8 0.0 copy-start.6
  16.9 1.3 %collective-permute-start.3 = (bf16[72,128]{1,0:T(8,128)(2,1)S(1)}, bf16[72,128]{1,0:T(8,128)(2,1)S(1)}, u32[]{:S(2)}, u32[]{:S(2)}) collective-permute-start(bf16[72,128]{1,0:T(8,128)(2,1)S(1)} %fusion.22), channel_id=1, source_target_pairs={{16,0},{32,16},{48,32},{64,48},{80,64},{96,80},{112,96},{128,112},... | collective-permute-start | bytes 55304 | tf_op jit(solution)/shard_map/ppermute | solution.py:26
  18.2 0.1 copy.82.bias
  18.4 0.2 copy.81.weights
  18.6 4.3 %collective-permute-done.3.right = bf16[72,128]{1,0:T(8,128)(2,1)S(1)} collective-permute-done((bf16[72,128]{1,0:T(8,128)(2,1)S(1)}, bf16[72,128]{1,0:T(8,128)(2,1)S(1)}, u32[]{:S(2)}, u32[]{:S(2)}) %collective-permute-start.3) | collective-permute-done | bytes 18464 | tf_op jit(solution)/shard_map/ppermute | solution.py:26
  22.9 1.0 copy-done.5
  23.9 4.4 %shard_map.126 = (bf16[1024,128]{1,0:T(8,128)(2,1)}, f32[1024,128]{1,0:T(8,128)}, f32[1024,128]{1,0:T(8,128)}, bf16[256,2048]{1,0:T(8,128)(2,1)S(1)}, bf16[256,1...) custom-call(bf16[128,128]{1,0:T(8,128)(2,1)S(1)} %bitcast.38, bf16[1024,128]{1,0:T(8,128)(2,1)S(1)} %bitcast.35, ...), custom_call_target="tpu_custom_call" | custom-call | flops 1400000000 | bytes 6000000 | tf_op jit(solution)/shard_map/pallas_call | solution.py:217
  28.3 9.0 %all-to-all-start = ((bf16[32,24,256]{2,1,0:T(8,128)(2,1)}), bf16[32,24,256]{2,1,0:T(8,128)(2,1)S(1)}, u32[]{:S(2)}, u32[]{:S(2)}) async-start(bf16[32,24,256]{2,1,0:T(8,128)(2,1)} %bitcast.22), calls=%async_computation | async-start | bytes 786432 | tf_op jit(solution)/shard_map/all_to_all | solution.py:186
  37.4 2.1 %collective-permute-start.5 = (bf16[256,128]{1,0:T(8,128)(2,1)S(1)}, bf16[256,128]{1,0:T(8,128)(2,1)S(1)}, u32[]{:S(2)}, u32[]{:S(2)}) collective-permute-start(bf16[256,128]{1,0:T(8,128)(2,1)S(1)} %get-tuple-element.27), channel_id=1, source_target_pairs={{1,0},{2,1},{3,2},{4,3},{5,4},{6,5},{7,6},{8,7},{9,8},{10,9},{11,1... | collective-permute-start | bytes 196616 | tf_op jit(solution)/shard_map/ppermute | solution.py:26
  39.5 3.4 %collective-permute-start.4 = (bf16[256,128]{1,0:T(8,128)(2,1)S(1)}, bf16[256,128]{1,0:T(8,128)(2,1)S(1)}, u32[]{:S(2)}, u32[]{:S(2)}) collective-permute-start(bf16[256,128]{1,0:T(8,128)(2,1)S(1)} %get-tuple-element.28), channel_id=1, source_target_pairs={{0,1},{1,2},{2,3},{3,4},{4,5},{5,6},{6,7},{7,8},{8,9},{9,10},{10,1... | collective-permute-start | bytes 196616 | tf_op jit(solution)/shard_map/ppermute | solution.py:26
  42.9 2.0 %collective-permute-done.5.bottom.rest_1_ = bf16[256,128]{1,0:T(8,128)(2,1)S(1)} collective-permute-done((bf16[256,128]{1,0:T(8,128)(2,1)S(1)}, bf16[256,128]{1,0:T(8,128)(2,1)S(1)}, u32[]{:S(2)}, u32[]{:S(2)}) %collective-permute-start.5) | collective-permute-done | bytes 65568 | tf_op jit(solution)/shard_map/ppermute | solution.py:26
  45.0 2.2 %all-to-all-done.parts = bf16[32,24,256]{2,1,0:T(8,128)(2,1)S(1)} async-done(((bf16[32,24,256]{2,1,0:T(8,128)(2,1)}), bf16[32,24,256]{2,1,0:T(8,128)(2,1)S(1)}, u32[]{:S(2)}, u32[]{:S(2)}) %all-to-all-start) | async-done | bytes 393248 | tf_op jit(solution)/shard_map/all_to_all | solution.py:186
  47.2 0.7 shard_map.128
  47.9 8.0 %all-to-all-start.1 = ((f32[4,24,256]{2,1,0:T(8,128)}), f32[4,24,256]{2,1,0:T(8,128)S(1)}, u32[]{:S(2)}, u32[]{:S(2)}) async-start(f32[4,24,256]{2,1,0:T(8,128)} %shard_map.128), calls=%async_computation.1 | async-start | bytes 196608 | tf_op jit(solution)/shard_map/all_to_all | solution.py:186
  55.9 0.1 fusion.28
  56.0 0.1 fusion.27
  56.1 4.6 %all-to-all-done.1.parts = f32[4,24,256]{2,1,0:T(8,128)S(1)} async-done(((f32[4,24,256]{2,1,0:T(8,128)}), f32[4,24,256]{2,1,0:T(8,128)S(1)}, u32[]{:S(2)}, u32[]{:S(2)}) %all-to-all-start.1) | async-done | bytes 98336 | tf_op jit(solution)/shard_map/all_to_all | solution.py:186
  60.7 0.7 shard_map.129
  61.4 10.0 %all-to-all-start.2 = ((f32[4,24,256]{2,1,0:T(8,128)}), f32[4,24,256]{2,1,0:T(8,128)S(1)}, u32[]{:S(2)}, u32[]{:S(2)}) async-start(f32[4,24,256]{2,1,0:T(8,128)} %shard_map.129), calls=%async_computation.2 | async-start | bytes 196608 | tf_op jit(solution)/shard_map/all_to_all | solution.py:186
  71.4 0.1 fusion.29
  71.5 0.1 fusion.9
  71.6 1.3 %collective-permute-start.7 = (bf16[256,128]{1,0:T(8,128)(2,1)S(1)}, bf16[256,128]{1,0:T(8,128)(2,1)S(1)}, u32[]{:S(2)}, u32[]{:S(2)}) collective-permute-start(bf16[256,128]{1,0:T(8,128)(2,1)S(1)} %fusion.9), channel_id=1, source_target_pairs={{16,0},{32,16},{48,32},{64,48},{80,64},{96,80},{112,96},{128,112},... | collective-permute-start | bytes 196616 | tf_op jit(solution)/shard_map/ppermute | solution.py:26
  72.9 0.1 fusion.7
  73.0 5.5 %collective-permute-start.6 = (bf16[256,128]{1,0:T(8,128)(2,1)S(1)}, bf16[256,128]{1,0:T(8,128)(2,1)S(1)}, u32[]{:S(2)}, u32[]{:S(2)}) collective-permute-start(bf16[256,128]{1,0:T(8,128)(2,1)S(1)} %fusion.7), channel_id=1, source_target_pairs={{0,16},{16,32},{32,48},{48,64},{64,80},{80,96},{96,112},{112,128},... | collective-permute-start | bytes 196616 | tf_op jit(solution)/shard_map/ppermute | solution.py:26
  78.5 1.7 %collective-permute-done.6.left.rest_0_ = bf16[256,128]{1,0:T(8,128)(2,1)S(1)} collective-permute-done((bf16[256,128]{1,0:T(8,128)(2,1)S(1)}, bf16[256,128]{1,0:T(8,128)(2,1)S(1)}, u32[]{:S(2)}, u32[]{:S(2)}) %collective-permute-start.6) | collective-permute-done | bytes 65568 | tf_op jit(solution)/shard_map/ppermute | solution.py:26
  80.2 3.1 %all-to-all-done.2.parts = f32[4,24,256]{2,1,0:T(8,128)S(1)} async-done(((f32[4,24,256]{2,1,0:T(8,128)}), f32[4,24,256]{2,1,0:T(8,128)S(1)}, u32[]{:S(2)}, u32[]{:S(2)}) %all-to-all-start.2) | async-done | bytes 98336 | tf_op jit(solution)/shard_map/all_to_all | solution.py:186
  83.2 0.8 shard_map.130
  84.0 9.9 %all-to-all-start.3 = ((bf16[32,24,256]{2,1,0:T(8,128)(2,1)}), bf16[32,24,256]{2,1,0:T(8,128)(2,1)S(1)}, u32[]{:S(2)}, u32[]{:S(2)}) async-start(bf16[32,24,256]{2,1,0:T(8,128)(2,1)} %shard_map.130), calls=%async_computation.3 | async-start | bytes 786432 | tf_op jit(solution)/shard_map/all_to_all | solution.py:186
  94.0 2.0 %shard_map.127 = (bf16[128,128]{1,0:T(8,128)(2,1)}, bf16[1024,128]{1,0:T(8,128)(2,1)}) custom-call(bf16[648,256]{1,0:T(8,128)(2,1)S(1)} %bitcast.37, bf16[256,2048]{1,0:T(8,128)(2,1)S(1)} %get-tuple-element.19.grads, bf16[256,128]{1,0:T(8,128)(2,1)S(1)} %collective-permute-done.4.top.rest_0_, bf16[256,128]{1,0:T(8,128)(2,1)S(1)} %collective-permute-done.5.bottom.rest_1_, ...), custom_call_target="tpu_custom_call" | custom-call | flops 764000000 | bytes 3000000 | tf_op jit(solution)/shard_map/pallas_call | solution.py:261
  95.9 7.9 %all-to-all-done.3 = bf16[32,24,256]{2,1,0:T(8,128)(2,1)S(1)} async-done(((bf16[32,24,256]{2,1,0:T(8,128)(2,1)}), bf16[32,24,256]{2,1,0:T(8,128)(2,1)S(1)}, u32[]{:S(2)}, u32[]{:S(2)}) %all-to-all-start.3) | async-done | bytes 393248 | tf_op jit(solution)/shard_map/all_to_all | solution.py:186
  103.8 1.2 %shard_map.131 = (f32[648,256]{1,0:T(8,128)}, f32[1,256]{1,0:T(1,128)}) custom-call(bf16[768,256]{1,0:T(8,128)(2,1)S(1)} %bitcast.34), custom_call_target="tpu_custom_call" | custom-call | tf_op jit(solution)/shard_map/pallas_call | solution.py:273
  (23 shorter events, 0.1 us)
Async XLA Ops:
  0.6 12.0 %copy-start = (bf16[64,16,128]{2,1,0:T(8,128)(2,1)S(1)}, bf16[64,16,128]{2,1,0:T(8,128)(2,1)}, u32[]{:S(2)}) copy-start(bf16[64,16,128]{2,1,0:T(8,128)(2,1)} %param.8) | copy-start | bytes 786436
  2.5 12.3 %collective-permute-start = (bf16[72,128]{1,0:T(8,128)(2,1)S(1)}, bf16[72,128]{1,0:T(8,128)(2,1)S(1)}, u32[]{:S(2)}, u32[]{:S(2)}) collective-permute-start(bf16[72,128]{1,0:T(8,128)(2,1)S(1)} %pad_maximum_fusion), channel_id=1, source_target_pairs={{0,1},{1,2},{2,3},{3,4},{4,5},{5,6},{6,7},{7,8},{8,9},{9,10},{10,1... | collective-permute-start | bytes 55304 | tf_op jit(solution)/shard_map/ppermute | solution.py:26
  7.1 7.7 %collective-permute-start.1 = (bf16[72,128]{1,0:T(8,128)(2,1)S(1)}, bf16[72,128]{1,0:T(8,128)(2,1)S(1)}, u32[]{:S(2)}, u32[]{:S(2)}) collective-permute-start(bf16[72,128]{1,0:T(8,128)(2,1)S(1)} %pad_maximum_fusion.1), channel_id=1, source_target_pairs={{1,0},{2,1},{3,2},{4,3},{5,4},{6,5},{7,6},{8,7},{9,8},{10,9},{11,1... | collective-permute-start | bytes 55304 | tf_op jit(solution)/shard_map/ppermute | solution.py:26
  12.6 0.8 copy-start.2
  14.2 4.1 %copy-start.1 = (bf16[256,648]{0,1:T(8,128)(2,1)S(1)}, bf16[256,648]{0,1:T(8,128)(2,1)}, u32[]{:S(2)}) copy-start(bf16[256,648]{0,1:T(8,128)(2,1)} %param.10) | copy-start | bytes 995332
  15.0 3.6 %collective-permute-start.2 = (bf16[72,128]{1,0:T(8,128)(2,1)S(1)}, bf16[72,128]{1,0:T(8,128)(2,1)S(1)}, u32[]{:S(2)}, u32[]{:S(2)}) collective-permute-start(bf16[72,128]{1,0:T(8,128)(2,1)S(1)} %fusion.19), channel_id=1, source_target_pairs={{0,16},{16,32},{32,48},{48,64},{64,80},{80,96},{96,112},{112,128},... | collective-permute-start | bytes 55304 | tf_op jit(solution)/shard_map/ppermute | solution.py:26
  16.8 1.3 %copy-start.6 = (f32[256]{0:T(256)S(1)}, f32[256]{0:T(256)}, u32[]{:S(2)}) copy-start(f32[256]{0:T(256)} %param.11) | copy-start | bytes 3076
  16.9 6.0 %collective-permute-start.3 = (bf16[72,128]{1,0:T(8,128)(2,1)S(1)}, bf16[72,128]{1,0:T(8,128)(2,1)S(1)}, u32[]{:S(2)}, u32[]{:S(2)}) collective-permute-start(bf16[72,128]{1,0:T(8,128)(2,1)S(1)} %fusion.22), channel_id=1, source_target_pairs={{16,0},{32,16},{48,32},{64,48},{80,64},{96,80},{112,96},{128,112},... | collective-permute-start | bytes 55304 | tf_op jit(solution)/shard_map/ppermute | solution.py:26
  18.3 4.6 %copy-start.4 = (f32[64,16,128]{2,1,0:T(8,128)S(1)}, f32[64,16,128]{2,1,0:T(8,128)}, u32[]{:S(2)}) copy-start(f32[64,16,128]{2,1,0:T(8,128)} %param.12) | copy-start | bytes 1572868
  18.4 4.5 %copy-start.3 = (f32[64,16,128]{2,1,0:T(8,128)S(1)}, f32[64,16,128]{2,1,0:T(8,128)}, u32[]{:S(2)}) copy-start(f32[64,16,128]{2,1,0:T(8,128)} %param.9) | copy-start | bytes 1572868
  22.9 1.0 copy-start.5
  28.3 18.9 %all-to-all-start = ((bf16[32,24,256]{2,1,0:T(8,128)(2,1)}), bf16[32,24,256]{2,1,0:T(8,128)(2,1)S(1)}, u32[]{:S(2)}, u32[]{:S(2)}) async-start(bf16[32,24,256]{2,1,0:T(8,128)(2,1)} %bitcast.22), calls=%async_computation | async-start | bytes 786432 | tf_op jit(solution)/shard_map/all_to_all | solution.py:186
  37.4 7.6 %collective-permute-start.5 = (bf16[256,128]{1,0:T(8,128)(2,1)S(1)}, bf16[256,128]{1,0:T(8,128)(2,1)S(1)}, u32[]{:S(2)}, u32[]{:S(2)}) collective-permute-start(bf16[256,128]{1,0:T(8,128)(2,1)S(1)} %get-tuple-element.27), channel_id=1, source_target_pairs={{1,0},{2,1},{3,2},{4,3},{5,4},{6,5},{7,6},{8,7},{9,8},{10,9},{11,1... | collective-permute-start | bytes 196616 | tf_op jit(solution)/shard_map/ppermute | solution.py:26
  39.5 5.5 %collective-permute-start.4 = (bf16[256,128]{1,0:T(8,128)(2,1)S(1)}, bf16[256,128]{1,0:T(8,128)(2,1)S(1)}, u32[]{:S(2)}, u32[]{:S(2)}) collective-permute-start(bf16[256,128]{1,0:T(8,128)(2,1)S(1)} %get-tuple-element.28), channel_id=1, source_target_pairs={{0,1},{1,2},{2,3},{3,4},{4,5},{5,6},{6,7},{7,8},{8,9},{9,10},{10,1... | collective-permute-start | bytes 196616 | tf_op jit(solution)/shard_map/ppermute | solution.py:26
  47.9 12.8 %all-to-all-start.1 = ((f32[4,24,256]{2,1,0:T(8,128)}), f32[4,24,256]{2,1,0:T(8,128)S(1)}, u32[]{:S(2)}, u32[]{:S(2)}) async-start(f32[4,24,256]{2,1,0:T(8,128)} %shard_map.128), calls=%async_computation.1 | async-start | bytes 196608 | tf_op jit(solution)/shard_map/all_to_all | solution.py:186
  61.4 21.9 %all-to-all-start.2 = ((f32[4,24,256]{2,1,0:T(8,128)}), f32[4,24,256]{2,1,0:T(8,128)S(1)}, u32[]{:S(2)}, u32[]{:S(2)}) async-start(f32[4,24,256]{2,1,0:T(8,128)} %shard_map.129), calls=%async_computation.2 | async-start | bytes 196608 | tf_op jit(solution)/shard_map/all_to_all | solution.py:186
  71.6 6.9 %collective-permute-start.7 = (bf16[256,128]{1,0:T(8,128)(2,1)S(1)}, bf16[256,128]{1,0:T(8,128)(2,1)S(1)}, u32[]{:S(2)}, u32[]{:S(2)}) collective-permute-start(bf16[256,128]{1,0:T(8,128)(2,1)S(1)} %fusion.9), channel_id=1, source_target_pairs={{16,0},{32,16},{48,32},{64,48},{80,64},{96,80},{112,96},{128,112},... | collective-permute-start | bytes 196616 | tf_op jit(solution)/shard_map/ppermute | solution.py:26
  73.0 7.2 %collective-permute-start.6 = (bf16[256,128]{1,0:T(8,128)(2,1)S(1)}, bf16[256,128]{1,0:T(8,128)(2,1)S(1)}, u32[]{:S(2)}, u32[]{:S(2)}) collective-permute-start(bf16[256,128]{1,0:T(8,128)(2,1)S(1)} %fusion.7), channel_id=1, source_target_pairs={{0,16},{16,32},{32,48},{48,64},{64,80},{80,96},{96,112},{112,128},... | collective-permute-start | bytes 196616 | tf_op jit(solution)/shard_map/ppermute | solution.py:26
  84.0 19.8 %all-to-all-start.3 = ((bf16[32,24,256]{2,1,0:T(8,128)(2,1)}), bf16[32,24,256]{2,1,0:T(8,128)(2,1)S(1)}, u32[]{:S(2)}, u32[]{:S(2)}) async-start(bf16[32,24,256]{2,1,0:T(8,128)(2,1)} %shard_map.130), calls=%async_computation.3 | async-start | bytes 786432 | tf_op jit(solution)/shard_map/all_to_all | solution.py:186

commit v4 on v3

v4 whole, which is shorter than its diff:
```python
import functools

import jax
import jax.numpy as jnp
from jax import lax
from jax.experimental import pallas as pl
from jax.experimental.pallas import tpu as pltpu
from jax.sharding import Mesh, PartitionSpec as P

CLIP_NORM = 100.0
EW = ("z_hi", "z_lo", "x_hi")
NS = ("y", "x_lo", "core")
PLANE = ("x_hi", "y", "x_lo", "core")
LANES = 128
STACK = 256
BF16 = jnp.bfloat16
F32 = jnp.float32


def vmem(count):
    return [pl.BlockSpec(memory_space=pltpu.VMEM)] * count


def neighbours(to_before, to_after, axes):
    count = lax.axis_size(axes)
    forward = [(i, i + 1) for i in range(count - 1)]
    backward = [(target, source) for source, target in forward]
    return lax.ppermute(to_after, axes, forward), lax.ppermute(to_before, axes, backward)


def sigmoid(x):
    return 0.5 * jnp.tanh(0.5 * x) + 0.5


def rows_kernel(frame, hidden_prev, cell_prev, grad_hidden, grad_cell, joined, up, down, *, height):
    inputs = frame.shape[0]
    joined[:inputs] = frame[...].astype(F32)
    joined[inputs:] = hidden_prev[...].astype(F32)
    channels = joined.shape[0] // height
    units = cell_prev.shape[0] // height
    for out, rows, state_row in ((up, (0, 1), 0), (down, (height - 2, height - 1), height - 1)):
        for i, n in enumerate(rows):
            out[i * channels : (i + 1) * channels] = joined[pl.ds(n, channels, stride=height), :]
        for i, state in enumerate((cell_prev, grad_hidden, grad_cell)):
            start = 2 * channels + i * units
            out[start : start + units] = state[pl.ds(state_row, units, stride=height), :]


def put_channels(tile, row, place):
    lane = lax.broadcasted_iota(jnp.int32, tile.shape, 1)
    return jnp.where(lane // 4 == place, pltpu.roll(row, (4 * place + 2) % LANES, 1), tile)


def put_state(tile, row, place, slot):
    lane = lax.broadcasted_iota(jnp.int32, tile.shape, 1)
    return jnp.where(lane // 2 == 2 * place + slot // 2, pltpu.roll(row, (4 * place + slot + 1) % LANES, 1), tile)


def columns_kernel(joined, cell_prev, grad_hidden, grad_cell, columns, *, height):
    channels = joined.shape[0] // height
    units = cell_prev.shape[0] // height
    tile = jnp.zeros((channels, LANES), F32)
    pairs = jnp.zeros((units, LANES), F32)
    single = jnp.zeros((units, LANES), F32)
    for n in range(height):
        at = pl.ds(n, units, stride=height)
        tile = put_channels(tile, joined[pl.ds(n, channels, stride=height), :], n + 2)
        pairs = put_state(pairs, cell_prev[at, :], n + 1, 0)
        pairs = put_state(pairs, grad_hidden[at, :], n + 1, 2)
        single = put_state(single, grad_cell[at, :], n + 1, 0)
    columns[:channels] = tile
    columns[channels : channels + units] = pairs
    columns[channels + units :] = single


def corners_kernel(columns, top, bottom, out, *, height, units):
    channels = columns.shape[0] - 2 * units
    tile = columns[:channels]
    pairs = columns[channels : channels + units]
    single = columns[channels + units :]
    for rows, place, state_place in ((top, 0, 0), (bottom, height + 2, height + 1)):
        for i in range(2):
            tile = put_channels(tile, rows[i * channels : (i + 1) * channels], place + i)
        states = [rows[2 * channels + i * units : 2 * channels + (i + 1) * units] for i in range(3)]
        pairs = put_state(pairs, states[0], state_place, 0)
        pairs = put_state(pairs, states[1], state_place, 2)
        single = put_state(single, states[2], state_place, 0)
    out[:channels] = tile
    out[channels : channels + units] = pairs
    out[channels + units :] = single


def gate_step(gates, old, down, grad_cell):
    units = old.shape[0]
    input_gate = sigmoid(gates[:units])
    forget_gate = sigmoid(gates[units : 2 * units])
    cand_gate = jnp.tanh(gates[2 * units : 3 * units])
    output_gate = sigmoid(gates[3 * units :])
    new = forget_gate * old + input_gate * cand_gate
    new_tanh = jnp.tanh(new)
    cell_grad = grad_cell + down * output_gate * (1.0 - new_tanh * new_tanh)
    grads = jnp.concatenate(
        [
            cell_grad * cand_gate * input_gate * (1.0 - input_gate),
            cell_grad * old * forget_gate * (1.0 - forget_gate),
            cell_grad * input_gate * (1.0 - cand_gate * cand_gate),
            down * new_tanh * output_gate * (1.0 - output_gate),
        ],
        0,
    ).astype(BF16)
    return output_gate * new_tanh, new, cell_grad * forget_gate, grads


def forward_kernel(
    joined, columns, left, right, top, bottom, weights, bias, cell_prev, grad_hidden, grad_cell,
    hidden, cell, grad_cell_prev, grads, side_grads, terms,
    stacked, hidden_rows,
):
    units = bias.shape[0] // 4
    height = cell_prev.shape[0] // units
    channels = joined.shape[0] // height
    lane = lax.broadcasted_iota(jnp.int32, (channels, LANES), 1)
    spare = STACK - 3 * channels
    ones_row = (lax.broadcasted_iota(jnp.int32, (spare, LANES), 0) == 0).astype(F32)
    own = columns[:channels]
    outer = jnp.where(lane % 4 < 2, left[:channels], right[:channels])
    for place in range(height + 4):
        if place < 2:
            row = top[place * channels : (place + 1) * channels]
        elif place >= height + 2:
            row = bottom[(place - height - 2) * channels : (place - height - 1) * channels]
        else:
            row = joined[pl.ds(place - 2, channels, stride=height), :]
        west = pltpu.roll(outer, (LANES - 4 * place - 1) % LANES, 1)
        east = pltpu.roll(outer, (LANES - 4 * place - 3) % LANES, 1)
        before = jnp.where(lane == 0, west, pltpu.roll(row, 1, 1))
        after = jnp.where(lane == LANES - 1, east, pltpu.roll(row, LANES - 1, 1))
        stacked[:, place * LANES : (place + 1) * LANES] = jnp.concatenate([before, row, after, ones_row], 0).astype(
            BF16
        )
    bias_cells = jnp.broadcast_to(bias[...], (4 * units, LANES))

    side = jnp.concatenate(
        [
            jnp.where(lane % 4 == 0, outer, own),
            pltpu.roll(outer, LANES - 1, 1),
            pltpu.roll(jnp.where(lane % 4 == 2, own, outer), LANES - 2, 1),
        ],
        0,
    )
    gates = bias_cells
    for row_off in range(3):
        moved = pltpu.roll(side, LANES - 4 * row_off, 1) if row_off else side
        gates = gates + jnp.dot(
            weights[:, row_off * STACK : (row_off + 1) * STACK],
            jnp.concatenate([moved, ones_row], 0).astype(BF16),
            preferred_element_type=F32,
        )
    lane = lax.broadcasted_iota(jnp.int32, (units, LANES), 1)
    pairs = slice(channels, channels + units)
    single = slice(channels + units, channels + 2 * units)
    pairs = jnp.where(lane % 2 == 0, left[pairs], right[pairs])
    single = jnp.where(lane % 2 == 0, left[single], right[single])
    side_grads[...] = gate_step(gates, pairs, pltpu.roll(pairs, LANES - 2, 1), single)[3]

    for pair in range(height // 2 + 1):
        sums = jnp.zeros((4 * units, 2 * LANES), F32)
        for row_off in range(3):
            start = (2 * pair + row_off) * LANES
            sums = sums + jnp.dot(
                weights[:, row_off * STACK : (row_off + 1) * STACK],
                stacked[:, start : start + 2 * LANES],
                preferred_element_type=F32,
            )
        for half in range(2):
            place = 2 * pair + half
            gates = sums[:, half * LANES : (half + 1) * LANES] + bias_cells
            inside = 0 < place <= height
            if inside:
                at = pl.ds(place - 1, units, stride=height)
                states = [cell_prev[at, :], grad_hidden[at, :], grad_cell[at, :]]
            else:
                rows = bottom if place else top
                states = [rows[2 * channels + i * units : 2 * channels + (i + 1) * units] for i in range(3)]
            new_hidden, new, down, row_grads = gate_step(gates, *states)
            grads[:, place * LANES : (place + 1) * LANES] = row_grads
            if inside:
                hidden_rows[at, :] = new_hidden
                cell[at, :] = new
                grad_cell_prev[at, :] = down
    hidden[...] = hidden_rows[...].astype(BF16)
    for row_off in range(3):
        terms[row_off * STACK : (row_off + 1) * STACK] = lax.dot_general(
            stacked[:, (row_off + 1) * LANES : (row_off + 1 + height) * LANES],
            grads[:, LANES : (height + 1) * LANES],
            (((1,), (1,)), ((), ())),
            preferred_element_type=F32,
        ).astype(BF16)


def backward_kernel(weights, grads, side_grads, grad_frame, grad_hidden_prev, sums, rows):
    height = grads.shape[1] // LANES - 2
    inputs = grad_frame.shape[0] // height
    channels = rows.shape[0] // height
    lane = lax.broadcasted_iota(jnp.int32, (channels, LANES), 1)
    outer = jnp.dot(weights[...], side_grads[...], preferred_element_type=F32)
    first = jnp.zeros((channels, LANES), F32)
    last = jnp.zeros((channels, LANES), F32)
    for row_off in range(3):
        low, high = 3 * row_off * channels, (3 * row_off + 2) * channels
        back = (LANES - 4 * (2 - row_off)) % LANES
        first = first + pltpu.roll(outer[high : high + channels], back, 1)
        last = last + pltpu.roll(outer[low : low + channels], back, 1)
    for place in range(0, height + 2, 2):
        cells = grads[:, place * LANES : (place + 2) * LANES]
        product = jnp.dot(weights[...], cells, preferred_element_type=F32)
        for half in range(2):
            for row_off in range(3):
                n = place + half + row_off - 2
                if not 0 <= n < height:
                    continue
                for col_off in range(3):
                    start = (3 * row_off + col_off) * channels
                    piece = product[start : start + channels, half * LANES : (half + 1) * LANES]
                    if row_off == 2:
                        sums[n, col_off] = piece
                    else:
                        sums[n, col_off] = sums[n, col_off] + piece
    for n in range(height):
        west = pltpu.roll(first, (LANES - 4 * n) % LANES, 1)
        east = pltpu.roll(last, LANES - 2 - 4 * n, 1)
        total = sums[n, 1]
        total = total + jnp.where(lane == LANES - 1, east, pltpu.roll(sums[n, 0], LANES - 1, 1))
        total = total + jnp.where(lane == 0, west, pltpu.roll(sums[n, 2], 1, 1))
        rows[pl.ds(n, channels, stride=height), :] = total
    grad_frame[...] = rows[: inputs * height].astype(BF16)
    grad_hidden_prev[...] = rows[inputs * height :].astype(BF16)


def finish_kernel(total, kernel_step, bias_step):
    block = kernel_step.shape[0] // 3
    parts = [total[i * STACK : i * STACK + block].astype(F32) for i in range(3)]
    bias_grad = total[block : block + 8].astype(F32)[:1]
    norm = jnp.sqrt(sum(jnp.sum(part * part) for part in parts) + jnp.sum(bias_grad * bias_grad))
    factor = jnp.minimum(1.0, CLIP_NORM / norm)
    for i, part in enumerate(parts):
        kernel_step[i * block : (i + 1) * block] = part * factor
    bias_step[...] = bias_grad * factor


def sum_kernel(parts, *rest):
    copies = rest[-1]
    total = jnp.sum(parts[...].astype(F32), 0).astype(copies.dtype)
    copies[...] = jnp.broadcast_to(total[None], copies.shape)


def summed(parts, copies, kind, *after):
    return pl.pallas_call(
        sum_kernel,
        out_shape=jax.ShapeDtypeStruct((copies,) + parts.shape[1:], kind),
        in_specs=vmem(1) + [pl.BlockSpec(memory_space=pl.ANY)] * len(after),
        out_specs=vmem(1)[0],
        compiler_params=pltpu.CompilerParams(vmem_limit_bytes=8 * 2**20),
    )(parts, *after)


def exchanged(copies, axes):
    return lax.all_to_all(copies, axes, 0, 0, tiled=True)


def shape(rows, columns, kind):
    return jax.ShapeDtypeStruct((rows, columns), kind)


def called(kernel, outs, scratch, cost, *args, mebibytes=16):
    return pl.pallas_call(
        kernel,
        out_shape=tuple(outs),
        in_specs=vmem(len(args)),
        out_specs=tuple(vmem(len(outs))),
        scratch_shapes=scratch,
        compiler_params=pltpu.CompilerParams(vmem_limit_bytes=mebibytes * 2**20),
        cost_estimate=pl.CostEstimate(flops=cost, bytes_accessed=2 * cost // 1000, transcendentals=0),
    )(*args)


def per_device(frame, hidden_prev, cell_prev, kernel, bias, grad_hidden, grad_cell):
    inputs, height, breadth = frame.shape
    units = hidden_prev.shape[0]
    channels = inputs + units
    gate_rows = kernel.shape[0]
    weights = kernel.reshape(gate_rows, 3, 3 * channels)
    weights = jnp.pad(weights, ((0, 0), (0, 0), (0, STACK - 3 * channels))).reshape(gate_rows, 3 * STACK)
    flat = (units * height, breadth)
    states = (cell_prev.reshape(flat), grad_hidden.reshape(flat), grad_cell.reshape(flat))

    strip = shape(2 * channels + 3 * units, breadth, F32)
    joined, up, down = called(
        functools.partial(rows_kernel, height=height),
        [shape(channels * height, breadth, F32), strip, strip],
        [],
        1_000_000,
        frame.reshape(inputs * height, breadth),
        hidden_prev.reshape(flat),
        *states,
    )
    edge = shape(channels + 2 * units, LANES, F32)
    (columns,) = called(functools.partial(columns_kernel, height=height), [edge], [], 1_000_000, joined, *states)
    top, bottom = neighbours(up, down, NS)
    (columns,) = called(functools.partial(corners_kernel, height=height, units=units), [edge], [], 100_000, columns, top, bottom)
    left, right = neighbours(columns, columns, EW)

    hidden, cell, grad_cell_prev, grads, side_grads, terms = called(
        forward_kernel,
        [
            shape(*flat, BF16),
            shape(*flat, F32),
            shape(*flat, F32),
            shape(gate_rows, (height + 2) * breadth, BF16),
            shape(gate_rows, LANES, BF16),
            shape(3 * STACK, gate_rows, BF16),
        ],
        [pltpu.VMEM((STACK, (height + 4) * breadth), BF16), pltpu.VMEM(flat, F32)],
        1_400_000_000,
        joined,
        columns,
        left,
        right,
        top,
        bottom,
        weights,
        bias[:, None],
        *states,
    )

    plane = lax.axis_size(PLANE)
    low, high = lax.axis_size("z_lo"), lax.axis_size("z_hi")
    mine = exchanged(terms.reshape(plane, -1, gate_rows), PLANE)
    mine = exchanged(summed(mine, low, F32), "z_lo")
    mine = exchanged(summed(mine, high, F32), "z_hi")
    mine = summed(mine, plane, BF16)
    total = exchanged(mine, PLANE).reshape(3 * STACK, gate_rows)
    grad_frame, grad_hidden_prev = called(
        backward_kernel,
        [shape(inputs * height, breadth, BF16), shape(*flat, BF16)],
        [pltpu.VMEM((height, 3, channels, breadth), F32), pltpu.VMEM((channels * height, breadth), F32)],
        764_000_000,
        kernel.T,
        grads,
        side_grads,
    )
    kernel_step, bias_step = called(
        finish_kernel, [shape(9 * channels, gate_rows, F32), shape(1, gate_rows, F32)], [], 1_000_000, total
    )
    whole = (units, height, breadth)
    return (
        hidden.reshape(whole),
        cell.reshape(whole),
        grad_frame.reshape(frame.shape),
        grad_hidden_prev.reshape(whole),
        grad_cell_prev.reshape(whole),
        kernel_step.T,
        bias_step.reshape(gate_rows),
    )


def solution(mesh):
    mesh = Mesh(mesh.devices.reshape(4, 4, 2, 4, 2, 2), EW + NS)
    grid = P(None, NS, EW)
    return jax.shard_map(
        per_device,
        mesh=mesh,
        in_specs=(grid, grid, grid, P(), P(), grid, grid),
        out_specs=(grid, grid, grid, grid, grid, P(), P()),
        check_vma=False,
    )
```

time: 106 us -> 106 us (level)
  blocking collectives: 0 us -> 53.8 us
  starting transfers between devices: 62.5 us -> 25 us
  waiting for transfers between devices: 25.8 us -> 6.71 us
  local copies, waits for them, and re-layouts: 5.73 us -> 8.18 us
  Pallas kernels: 9.65 us -> 10.9 us
    all_to_all x0 -> x3, blocking collectives: none -> 53.8 us  [exchanged(): return lax.all_to_all(copies, axes, 0, 0, tiled=True)]
    all_to_all x4 -> x1, starting transfers between devices: 37 us -> 7.36 us  [exchanged(): return lax.all_to_all(copies, axes, 0, 0, tiled=True)]
    all_to_all x4 -> x1, waiting for transfers between devices: 17.8 us -> 6.7 us  [exchanged(): return lax.all_to_all(copies, axes, 0, 0, tiled=True)]
    ppermute x8 -> x4, waiting for transfers between devices: 8 us -> 0.01 us  [the longest x2 0.01 us: neighbours(): lax.ppermute(to_before, axes, backward)]
    ppermute x8 -> x4, starting transfers between devices: 25.5 us -> 17.7 us  [the longest x2 10.8 us: neighbours(): lax.ppermute(to_after, axes, forward)]
    unnamed x22 -> x24, local copies, waits for them, and re-layouts: 2.92 us -> 6.11 us
    pallas_call x3 -> x6, Pallas kernels: 7.51 us -> 10 us  [called(): pl.pallas_call(kernel, out_shape=tuple(outs), in_specs=vmem(len(args)), o...]
    slice x10 -> x0, local copies, waits for them, and re-layouts: 2.48 us -> none  [the longest x2 1.81 us: per_device(): row = jnp.concatenate([frame[:, 0], hidden_prev[:, 0]], 0)]
  transfers between devices with their start and end apart: 12 -> 5, of which waited for: 7 -> 1; matrix products, arithmetic and copies ran while one was open for 2% -> 2% of each run, Pallas kernels for 2% -> 3%
where the time goes in v4:
time: 106 us; the launch traced here: 105 us
  blocking collectives  53.8 us (51%)
  starting transfers between devices  25 us (24%)
  Pallas kernels  10.9 us (10%)
  local copies, waits for them, and re-layouts  8.18 us (8%)
  waiting for transfers between devices  6.71 us (6%)
    all_to_all x3, blocking collectives, exchanged(): return lax.all_to_all(copies, axes, 0, 0, tiled=True)  53.8 us
    ppermute x2, starting transfers between devices, neighbours(): lax.ppermute(to_after, axes, forward)  10.8 us
    pallas_call x6, Pallas kernels, called(): pl.pallas_call(kernel, out_shape=tuple(outs), in_specs=vmem(len(args)), o...  10 us
    all_to_all x1, starting transfers between devices, exchanged(): return lax.all_to_all(copies, axes, 0, 0, tiled=True)  7.36 us
    ppermute x2, starting transfers between devices, neighbours(): lax.ppermute(to_before, axes, backward)  6.87 us
    all_to_all x1, waiting for transfers between devices, exchanged(): return lax.all_to_all(copies, axes, 0, 0, tiled=True)  6.7 us
    unnamed x24, local copies, waits for them, and re-layouts  6.11 us
  transfers between devices with their start and end apart: 5, of which 1 were waited for; matrix products, arithmetic and copies ran while one was open for 2% of the time, Pallas kernels for 3%

profile of v4, /device:TPU:1, one launch (start us, length us, event | category | flops | bytes accessed | tf_op | source)
XLA Modules:
  0.0 105.4 jit_solution(16163100802501267331)
XLA Ops:
  0.6 0.0 copy-start
  0.6 1.0 copy-done
  1.7 0.0 copy-start.2
  1.7 1.0 copy-done.2
  2.7 0.0 copy-start.4
  2.7 1.0 copy-done.4
  3.8 0.0 copy-start.7
  3.8 0.9 copy-done.7
  4.7 0.0 copy-start.8
  4.7 0.8 copy-done.8
  5.5 0.0 copy-start.1
  5.5 0.0 copy-start.3
  5.5 0.0 copy-start.5
  5.5 0.2 shard_map.126
  5.7 4.6 %collective-permute-start = (f32[336,128]{1,0:T(8,128)S(1)}, f32[336,128]{1,0:T(8,128)S(1)}, u32[]{:S(2)}, u32[]{:S(2)}) collective-permute-start(f32[336,128]{1,0:T(8,128)S(1)} %get-tuple-element.21), channel_id=1, source_target_pairs={{0,1},{1,2},{2,3},{3,4},{4,5},{5,6},{6,7},{7,8},{8,9},{9,10},{10,1... | collective-permute-start | bytes 516104 | tf_op jit(solution)/shard_map/ppermute | solution.py:28
  10.3 5.6 %collective-permute-start.1 = (f32[336,128]{1,0:T(8,128)S(1)}, f32[336,128]{1,0:T(8,128)S(1)}, u32[]{:S(2)}, u32[]{:S(2)}) collective-permute-start(f32[336,128]{1,0:T(8,128)S(1)} %get-tuple-element.22), channel_id=1, source_target_pairs={{1,0},{2,1},{3,2},{4,3},{5,4},{6,5},{7,6},{8,7},{9,8},{10,9},{11,1... | collective-permute-start | bytes 516104 | tf_op jit(solution)/shard_map/ppermute | solution.py:28
  15.9 0.0 copy-done.1
  15.9 0.0 copy-done.3
  15.9 0.0 copy-done.5
  15.9 0.0 copy-start.11
  15.9 0.0 copy-start.6
  15.9 1.2 %shard_map.127.columns = f32[200,128]{1,0:T(8,128)S(1)} custom-call(f32[1152,128]{1,0:T(8,128)S(1)} %get-tuple-element.20.joined, f32[1024,128]{1,0:T(8,128)S(1)} %bitcast.19, f32[1024,128]{1,0:T(8,128)S(1)} %bitcast.22, f32[1024,128]{1,0:T(8,128)S(1)} %bitcast.25), custom_call_target="tpu_custom_call" | custom-call | flops 1000000 | bytes 2000 | tf_op jit(solution)/shard_map/pallas_call | solution.py:276
  17.1 0.0 collective-permute-done.top
  17.1 0.0 collective-permute-done.1.bottom
  17.1 0.2 shard_map.128.columns
  17.3 1.3 %collective-permute-start.3 = (f32[200,128]{1,0:T(8,128)S(1)}, f32[200,128]{1,0:T(8,128)}, u32[]{:S(2)}, u32[]{:S(2)}) collective-permute-start(f32[200,128]{1,0:T(8,128)S(1)} %shard_map.128.columns), channel_id=1, source_target_pairs={{16,0},{32,16},{48,32},{64,48},{80,64},{96,80},{112,96},{128,112},... | collective-permute-start | bytes 307208 | tf_op jit(solution)/shard_map/ppermute | solution.py:28
  18.6 6.1 %collective-permute-start.2 = (f32[200,128]{1,0:T(8,128)S(1)}, f32[200,128]{1,0:T(8,128)}, u32[]{:S(2)}, u32[]{:S(2)}) collective-permute-start(f32[200,128]{1,0:T(8,128)S(1)} %shard_map.128.columns), channel_id=1, source_target_pairs={{0,16},{16,32},{32,48},{48,64},{64,80},{80,96},{96,112},{112,128},... | collective-permute-start | bytes 307208 | tf_op jit(solution)/shard_map/ppermute | solution.py:28
  24.7 0.0 copy-done.11
  24.7 0.1 copy.16.bias
  24.9 0.0 copy-done.6
  24.9 0.8 pad.4
  25.7 1.2 %copy.15.weights = bf16[256,768]{1,0:T(8,128)(2,1)S(1)} copy(bf16[256,768]{0,1:T(8,128)(2,1)} %bitcast.33) | data formatting | bytes 786432 | tf_op jit(solution)/shard_map/reshape | solution.py:293
  26.8 0.0 collective-permute-done.3.right
  26.9 0.0 collective-permute-done.2.left
  26.9 5.3 %shard_map.129 = (bf16[1024,128]{1,0:T(8,128)(2,1)}, f32[1024,128]{1,0:T(8,128)}, f32[1024,128]{1,0:T(8,128)}, bf16[256,2304]{1,0:T(8,128)(2,1)S(1)}, bf16[256,1...) custom-call(f32[1152,128]{1,0:T(8,128)S(1)} %get-tuple-element.20.joined, f32[200,128]{1,0:T(8,128)S(1)} %shard_map.128.columns, ...), custom_call_target="tpu_custom_call" | custom-call | flops 1400000000 | bytes 2800000 | tf_op jit(solution)/shard_map/pallas_call | solution.py:276
  32.2 0.0 copy-start.9
  32.2 18.6 %all_to_all.20.parts = bf16[32,24,256]{2,1,0:T(8,128)(2,1)S(1)} all-to-all(bf16[32,24,256]{2,1,0:T(8,128)(2,1)S(1)} %bitcast.28), channel_id=1, replica_groups=mesh['z_hi'=4,'z_lo'=4,'x_hi'=2,'y'=4,'x_lo'=2,'core'=2] {'x_hi','y','x_..., dimensions={0} | all-to-all | bytes 786432 | tf_op jit(solution)/shard_map/all_to_all | solution.py:268
  50.9 0.1 shard_map.131
  50.9 11.4 %all_to_all.21.parts = f32[4,24,256]{2,1,0:T(8,128)S(1)} all-to-all(f32[4,24,256]{2,1,0:T(8,128)S(1)} %shard_map.131), channel_id=1, replica_groups=mesh['z_hi'=4,'z_lo'=4,'x_hi'=2,'y'=4,'x_lo'=2,'core'=2] {'z_lo'}, dimensions={0} | all-to-all | bytes 196608 | tf_op jit(solution)/shard_map/all_to_all | solution.py:268
  62.4 23.8 %all_to_all.22.parts = f32[4,24,256]{2,1,0:T(8,128)S(1)} all-to-all(f32[4,24,256]{2,1,0:T(8,128)S(1)} %shard_map.132), channel_id=1, replica_groups=mesh['z_hi'=4,'z_lo'=4,'x_hi'=2,'y'=4,'x_lo'=2,'core'=2] {'z_hi'}, dimensions={0} | all-to-all | bytes 196608 | tf_op jit(solution)/shard_map/all_to_all | solution.py:268
  86.1 0.0 copy-done.9
  86.1 0.8 shard_map.133
  86.9 7.4 %all-to-all-start.3 = ((bf16[32,24,256]{2,1,0:T(8,128)(2,1)}), bf16[32,24,256]{2,1,0:T(8,128)(2,1)S(1)}, u32[]{:S(2)}, u32[]{:S(2)}) async-start(bf16[32,24,256]{2,1,0:T(8,128)(2,1)} %shard_map.133), calls=%async_computation.3 | async-start | bytes 786432 | tf_op jit(solution)/shard_map/all_to_all | solution.py:268
  94.3 0.0 copy-start.10
  94.3 1.3 %copy-done.10 = bf16[256,2304]{1,0:T(8,128)(2,1)S(1)} copy-done((bf16[256,2304]{1,0:T(8,128)(2,1)S(1)}, bf16[256,2304]{1,0:T(8,128)(2,1)}, u32[]{:S(2)}) %copy-start.10) | copy-done | bytes 1179672
  95.5 2.0 %shard_map.130 = (bf16[128,128]{1,0:T(8,128)(2,1)}, bf16[1024,128]{1,0:T(8,128)(2,1)}) custom-call(bf16[648,256]{1,0:T(8,128)(2,1)S(1)} %bitcast.30, bf16[256,2304]{1,0:T(8,128)(2,1)S(1)} %copy-done.10, bf16[256,128]{1,0:T(8,128)(2,1)S(1)} %get-tuple-element.26.side_grads), custom_call_target="tpu_custom_call" | custom-call | flops 764000000 | bytes 1528000 | tf_op jit(solution)/shard_map/pallas_call | solution.py:276
  97.5 6.7 %all-to-all-done.3 = bf16[32,24,256]{2,1,0:T(8,128)(2,1)S(1)} async-done(((bf16[32,24,256]{2,1,0:T(8,128)(2,1)}), bf16[32,24,256]{2,1,0:T(8,128)(2,1)S(1)}, u32[]{:S(2)}, u32[]{:S(2)}) %all-to-all-start.3) | async-done | bytes 393248 | tf_op jit(solution)/shard_map/all_to_all | solution.py:268
  104.2 1.2 %shard_map.134 = (f32[648,256]{1,0:T(8,128)}, f32[1,256]{1,0:T(1,128)}) custom-call(bf16[768,256]{1,0:T(8,128)(2,1)S(1)} %bitcast.27), custom_call_target="tpu_custom_call" | custom-call | flops 1000000 | bytes 2000 | tf_op jit(solution)/shard_map/pallas_call | solution.py:276
  (1 shorter events, 0.0 us)
Async XLA Ops:
  0.6 1.0 copy-start
  1.7 1.0 copy-start.2
  2.7 1.0 copy-start.4
  3.8 0.9 copy-start.7
  4.7 0.8 copy-start.8
  5.5 10.4 %copy-start.1 = (f32[64,16,128]{2,1,0:T(8,128)S(1)}, f32[64,16,128]{2,1,0:T(8,128)}, u32[]{:S(2)}) copy-start(f32[64,16,128]{2,1,0:T(8,128)} %param.9) | copy-start | bytes 1572868
  5.5 10.4 %copy-start.3 = (f32[64,16,128]{2,1,0:T(8,128)S(1)}, f32[64,16,128]{2,1,0:T(8,128)}, u32[]{:S(2)}) copy-start(f32[64,16,128]{2,1,0:T(8,128)} %param.12) | copy-start | bytes 1572868
  5.5 10.4 %copy-start.5 = (f32[64,16,128]{2,1,0:T(8,128)S(1)}, f32[64,16,128]{2,1,0:T(8,128)}, u32[]{:S(2)}) copy-start(f32[64,16,128]{2,1,0:T(8,128)} %param.13) | copy-start | bytes 1572868
  5.7 11.5 %collective-permute-start = (f32[336,128]{1,0:T(8,128)S(1)}, f32[336,128]{1,0:T(8,128)S(1)}, u32[]{:S(2)}, u32[]{:S(2)}) collective-permute-start(f32[336,128]{1,0:T(8,128)S(1)} %get-tuple-element.21), channel_id=1, source_target_pairs={{0,1},{1,2},{2,3},{3,4},{4,5},{5,6},{6,7},{7,8},{8,9},{9,10},{10,1... | collective-permute-start | bytes 516104 | tf_op jit(solution)/shard_map/ppermute | solution.py:28
  10.3 6.8 %collective-permute-start.1 = (f32[336,128]{1,0:T(8,128)S(1)}, f32[336,128]{1,0:T(8,128)S(1)}, u32[]{:S(2)}, u32[]{:S(2)}) collective-permute-start(f32[336,128]{1,0:T(8,128)S(1)} %get-tuple-element.22), channel_id=1, source_target_pairs={{1,0},{2,1},{3,2},{4,3},{5,4},{6,5},{7,6},{8,7},{9,8},{10,9},{11,1... | collective-permute-start | bytes 516104 | tf_op jit(solution)/shard_map/ppermute | solution.py:28
  15.9 8.8 %copy-start.11 = (f32[256]{0:T(256)S(1)}, f32[256]{0:T(256)}, u32[]{:S(2)}) copy-start(f32[256]{0:T(256)} %param.11) | copy-start | bytes 3076
  15.9 9.0 %copy-start.6 = (bf16[256,648]{0,1:T(8,128)(2,1)S(1)}, bf16[256,648]{0,1:T(8,128)(2,1)}, u32[]{:S(2)}) copy-start(bf16[256,648]{0,1:T(8,128)(2,1)} %param.10) | copy-start | bytes 995332
  17.3 9.5 %collective-permute-start.3 = (f32[200,128]{1,0:T(8,128)S(1)}, f32[200,128]{1,0:T(8,128)}, u32[]{:S(2)}, u32[]{:S(2)}) collective-permute-start(f32[200,128]{1,0:T(8,128)S(1)} %shard_map.128.columns), channel_id=1, source_target_pairs={{16,0},{32,16},{48,32},{64,48},{80,64},{96,80},{112,96},{128,112},... | collective-permute-start | bytes 307208 | tf_op jit(solution)/shard_map/ppermute | solution.py:28
  18.6 8.3 %collective-permute-start.2 = (f32[200,128]{1,0:T(8,128)S(1)}, f32[200,128]{1,0:T(8,128)}, u32[]{:S(2)}, u32[]{:S(2)}) collective-permute-start(f32[200,128]{1,0:T(8,128)S(1)} %shard_map.128.columns), channel_id=1, source_target_pairs={{0,16},{16,32},{32,48},{48,64},{64,80},{80,96},{96,112},{112,128},... | collective-permute-start | bytes 307208 | tf_op jit(solution)/shard_map/ppermute | solution.py:28
  32.2 53.9 %copy-start.9 = (bf16[256,2304]{1,0:T(8,128)(2,1)}, bf16[256,2304]{1,0:T(8,128)(2,1)S(1)}, u32[]{:S(2)}) copy-start(bf16[256,2304]{1,0:T(8,128)(2,1)S(1)} %get-tuple-element.25.grads) | copy-start | bytes 3538948
  86.9 17.3 %all-to-all-start.3 = ((bf16[32,24,256]{2,1,0:T(8,128)(2,1)}), bf16[32,24,256]{2,1,0:T(8,128)(2,1)S(1)}, u32[]{:S(2)}, u32[]{:S(2)}) async-start(bf16[32,24,256]{2,1,0:T(8,128)(2,1)} %shard_map.133), calls=%async_computation.3 | async-start | bytes 786432 | tf_op jit(solution)/shard_map/all_to_all | solution.py:268
  94.3 1.3 %copy-start.10 = (bf16[256,2304]{1,0:T(8,128)(2,1)S(1)}, bf16[256,2304]{1,0:T(8,128)(2,1)}, u32[]{:S(2)}) copy-start(bf16[256,2304]{1,0:T(8,128)(2,1)} %copy-done.9) | copy-start | bytes 3538948

commit v5 on v4

--- a/solution.py
+++ b/solution.py
@@ -32,18 +32,34 @@
     return 0.5 * jnp.tanh(0.5 * x) + 0.5
 
 
-def rows_kernel(frame, hidden_prev, cell_prev, grad_hidden, grad_cell, joined, up, down, *, height):
-    inputs = frame.shape[0]
-    joined[:inputs] = frame[...].astype(F32)
-    joined[inputs:] = hidden_prev[...].astype(F32)
+def rows_kernel(
+    frame, hidden_prev, cell_prev, grad_hidden, grad_cell, up, down, joined, frame_here, hidden_here, *rest, height
+):
+    *here, sems = rest
+    copies = [
+        pltpu.make_async_copy(source, target, sems.at[i])
+        for i, (source, target) in enumerate(
+            zip((frame, hidden_prev, cell_prev, grad_hidden, grad_cell), (frame_here, hidden_here, *here))
+        )
+    ]
+    for copy in copies:
+        copy.start()
+    inputs = frame_here.shape[0]
     channels = joined.shape[0] // height
-    units = cell_prev.shape[0] // height
-    for out, rows, state_row in ((up, (0, 1), 0), (down, (height - 2, height - 1), height - 1)):
+    units = here[0].shape[0] // height
+    sides = ((up, (0, 1), 0), (down, (height - 2, height - 1), height - 1))
+    copies[0].wait()
+    joined[:inputs] = frame_here[...].astype(F32)
+    copies[1].wait()
+    joined[inputs:] = hidden_here[...].astype(F32)
+    for out, rows, _ in sides:
         for i, n in enumerate(rows):
             out[i * channels : (i + 1) * channels] = joined[pl.ds(n, channels, stride=height), :]
-        for i, state in enumerate((cell_prev, grad_hidden, grad_cell)):
-            start = 2 * channels + i * units
-            out[start : start + units] = state[pl.ds(state_row, units, stride=height), :]
+    for i, state in enumerate(here):
+        copies[2 + i].wait()
+        start = 2 * channels + i * units
+        for out, _, n in sides:
+            out[start : start + units] = state[pl.ds(n, units, stride=height), :]
 
 
 def put_channels(tile, row, place):
@@ -56,7 +72,16 @@
     return jnp.where(lane // 2 == 2 * place + slot // 2, pltpu.roll(row, (4 * place + slot + 1) % LANES, 1), tile)
 
 
-def columns_kernel(joined, cell_prev, grad_hidden, grad_cell, columns, *, height):
+def columns_kernel(
+    frame, hidden_prev, cell_prev, grad_hidden, grad_cell, kernel, columns, weights, joined, *, height
+):
+    joined[: frame.shape[0]] = frame[...].astype(F32)
+    joined[frame.shape[0] :] = hidden_prev[...].astype(F32)
+    depth = kernel.shape[0] // 3
+    blank = jnp.zeros((STACK - depth, kernel.shape[1]), F32)
+    for row_off in range(3):
+        part = kernel[...].astype(F32)[row_off * depth : (row_off + 1) * depth]
+        weights[:, row_off * STACK : (row_off + 1) * STACK] = jnp.concatenate([part, blank], 0).T.astype(BF16)
     channels = joined.shape[0] // height
     units = cell_prev.shape[0] // height
     tile = jnp.zeros((channels, LANES), F32)
@@ -99,31 +124,25 @@
     new = forget_gate * old + input_gate * cand_gate
     new_tanh = jnp.tanh(new)
     cell_grad = grad_cell + down * output_gate * (1.0 - new_tanh * new_tanh)
-    grads = jnp.concatenate(
-        [
-            cell_grad * cand_gate * input_gate * (1.0 - input_gate),
-            cell_grad * old * forget_gate * (1.0 - forget_gate),
-            cell_grad * input_gate * (1.0 - cand_gate * cand_gate),
-            down * new_tanh * output_gate * (1.0 - output_gate),
-        ],
-        0,
-    ).astype(BF16)
-    return output_gate * new_tanh, new, cell_grad * forget_gate, grads
+    grads = [
+        cell_grad * cand_gate * input_gate * (1.0 - input_gate),
+        cell_grad * old * forget_gate * (1.0 - forget_gate),
+        cell_grad * input_gate * (1.0 - cand_gate * cand_gate),
+        down * new_tanh * output_gate * (1.0 - output_gate),
+    ]
+    return output_gate * new_tanh, new, cell_grad * forget_gate, jnp.concatenate(grads, 0)
 
 
 def forward_kernel(
-    joined, columns, left, right, top, bottom, weights, bias, cell_prev, grad_hidden, grad_cell,
-    hidden, cell, grad_cell_prev, grads, side_grads, terms,
-    stacked, hidden_rows,
+    joined, top, bottom, weights, bias, cell_prev, grad_hidden, grad_cell,
+    hidden, cell, grad_cell_prev, grads, terms,
+    stacked,
 ):
     units = bias.shape[0] // 4
     height = cell_prev.shape[0] // units
     channels = joined.shape[0] // height
-    lane = lax.broadcasted_iota(jnp.int32, (channels, LANES), 1)
     spare = STACK - 3 * channels
     ones_row = (lax.broadcasted_iota(jnp.int32, (spare, LANES), 0) == 0).astype(F32)
-    own = columns[:channels]
-    outer = jnp.where(lane % 4 < 2, left[:channels], right[:channels])
     for place in range(height + 4):
         if place < 2:
             row = top[place * channels : (place + 1) * channels]
@@ -131,38 +150,12 @@
             row = bottom[(place - height - 2) * channels : (place - height - 1) * channels]
         else:
             row = joined[pl.ds(place - 2, channels, stride=height), :]
-        west = pltpu.roll(outer, (LANES - 4 * place - 1) % LANES, 1)
-        east = pltpu.roll(outer, (LANES - 4 * place - 3) % LANES, 1)
-        before = jnp.where(lane == 0, west, pltpu.roll(row, 1, 1))
-        after = jnp.where(lane == LANES - 1, east, pltpu.roll(row, LANES - 1, 1))
-        stacked[:, place * LANES : (place + 1) * LANES] = jnp.concatenate([before, row, after, ones_row], 0).astype(
-            BF16
-        )
+        stacked[:, place * LANES : (place + 1) * LANES] = jnp.concatenate(
+            [pltpu.roll(row, 1, 1), row, pltpu.roll(row, LANES - 1, 1), ones_row], 0
+        ).astype(BF16)
     bias_cells = jnp.broadcast_to(bias[...], (4 * units, LANES))
-
-    side = jnp.concatenate(
-        [
-            jnp.where(lane % 4 == 0, outer, own),
-            pltpu.roll(outer, LANES - 1, 1),
-            pltpu.roll(jnp.where(lane % 4 == 2, own, outer), LANES - 2, 1),
-        ],
-        0,
-    )
-    gates = bias_cells
-    for row_off in range(3):
-        moved = pltpu.roll(side, LANES - 4 * row_off, 1) if row_off else side
-        gates = gates + jnp.dot(
-            weights[:, row_off * STACK : (row_off + 1) * STACK],
-            jnp.concatenate([moved, ones_row], 0).astype(BF16),
-            preferred_element_type=F32,
-        )
-    lane = lax.broadcasted_iota(jnp.int32, (units, LANES), 1)
-    pairs = slice(channels, channels + units)
-    single = slice(channels + units, channels + 2 * units)
-    pairs = jnp.where(lane % 2 == 0, left[pairs], right[pairs])
-    single = jnp.where(lane % 2 == 0, left[single], right[single])
-    side_grads[...] = gate_step(gates, pairs, pltpu.roll(pairs, LANES - 2, 1), single)[3]
-
+    lane = lax.broadcasted_iota(jnp.int32, (4 * units, LANES), 1)
+    middle = (lane > 0) & (lane < LANES - 1)
     for pair in range(height // 2 + 1):
         sums = jnp.zeros((4 * units, 2 * LANES), F32)
         for row_off in range(3):
@@ -183,34 +176,112 @@
                 rows = bottom if place else top
                 states = [rows[2 * channels + i * units : 2 * channels + (i + 1) * units] for i in range(3)]
             new_hidden, new, down, row_grads = gate_step(gates, *states)
-            grads[:, place * LANES : (place + 1) * LANES] = row_grads
+            grads[:, place * LANES : (place + 1) * LANES] = jnp.where(middle, row_grads, 0.0).astype(BF16)
             if inside:
-                hidden_rows[at, :] = new_hidden
+                hidden[at, :] = new_hidden
                 cell[at, :] = new
                 grad_cell_prev[at, :] = down
-    hidden[...] = hidden_rows[...].astype(BF16)
     for row_off in range(3):
         terms[row_off * STACK : (row_off + 1) * STACK] = lax.dot_general(
             stacked[:, (row_off + 1) * LANES : (row_off + 1 + height) * LANES],
             grads[:, LANES : (height + 1) * LANES],
             (((1,), (1,)), ((), ())),
             preferred_element_type=F32,
+        )
+
+
+def sides_kernel(columns, left, right, weights, bias, inner_terms, side_grads, side_cells, terms, *, height):
+    units = bias.shape[0] // 4
+    channels = columns.shape[0] - 2 * units
+    spare = STACK - 3 * channels
+
+    def moved(x, lanes):
+        return pltpu.roll(x, lanes % LANES, 1)
+
+    slot = lax.broadcasted_iota(jnp.int32, (channels, LANES), 1) % 4
+    own = columns[:channels]
+    outer = jnp.where(slot < 2, left[:channels], right[:channels])
+    before = jnp.where(
+        slot == 0, outer, jnp.where(slot == 1, moved(own, 1), jnp.where(slot == 2, moved(outer, 1), moved(own, 2)))
+    )
+    at = jnp.where(slot == 0, moved(outer, -1), jnp.where(slot == 3, moved(outer, 1), own))
+    after = jnp.where(
+        slot == 0, moved(own, -2), jnp.where(slot == 1, moved(outer, -1), jnp.where(slot == 2, moved(own, -1), outer))
+    )
+    patches = jnp.concatenate([before, at, after], 0)
+    ones_row = (lax.broadcasted_iota(jnp.int32, (spare, LANES), 0) == 0).astype(F32)
+    stacks = [
+        jnp.concatenate([moved(patches, -4 * row_off) if row_off else patches, ones_row], 0).astype(BF16)
+        for row_off in range(3)
+    ]
+    gates = jnp.broadcast_to(bias[...], (4 * units, LANES))
+    for row_off in range(3):
+        gates = gates + jnp.dot(
+            weights[:, row_off * STACK : (row_off + 1) * STACK], stacks[row_off], preferred_element_type=F32
+        )
+    slot = slot[:units]
+    rows = slice(channels, channels + units)
+    here, west, east = columns[rows], left[rows], right[rows]
+    old = jnp.where(slot == 0, west, jnp.where(slot == 3, moved(east, 2), moved(here, 1)))
+    down = jnp.where(slot == 0, moved(west, -2), jnp.where(slot == 3, east, moved(here, -1)))
+    rows = slice(channels + units, channels + 2 * units)
+    here, west, east = columns[rows], left[rows], right[rows]
+    grad_cell = jnp.where(slot == 0, west, jnp.where(slot == 3, moved(east, 2), moved(here, 1)))
+    new_hidden, new, back, grads = gate_step(gates, old, down, grad_cell)
+    side_cells[:units] = new_hidden
+    side_cells[units : 2 * units] = new
+    side_cells[2 * units :] = back
+    side_grads[...] = grads.astype(BF16)
+    lane = lax.broadcasted_iota(jnp.int32, grads.shape, 1)
+    inside = (lane >= 4) & (lane < 4 * (height + 1)) & ((lane % 4 == 1) | (lane % 4 == 2))
+    grads = jnp.where(inside, grads, 0.0).astype(BF16)
+    for row_off in range(3):
+        part = slice(row_off * STACK, (row_off + 1) * STACK)
+        terms[part] = (
+            inner_terms[part]
+            + lax.dot_general(
+                stacks[row_off], grads, (((1,), (1,)), ((), ())), preferred_element_type=F32
+            )
         ).astype(BF16)
 
 
-def backward_kernel(weights, grads, side_grads, grad_frame, grad_hidden_prev, sums, rows):
+def backward_kernel(
+    weights, grads, side_grads, side_cells, inner_hidden, inner_cell, inner_back,
+    hidden, cell, grad_cell_prev, grad_frame, grad_hidden_prev,
+    sums, rows,
+):
     height = grads.shape[1] // LANES - 2
+    units = hidden.shape[0] // height
     inputs = grad_frame.shape[0] // height
-    channels = rows.shape[0] // height
+    channels = inputs + units
     lane = lax.broadcasted_iota(jnp.int32, (channels, LANES), 1)
+    ends = (lane[:units] == 0) | (lane[:units] == LANES - 1)
+    for n in range(height):
+        at = pl.ds(n, units, stride=height)
+        for i, (inner, out) in enumerate(((inner_hidden, rows), (inner_cell, cell), (inner_back, grad_cell_prev))):
+            side = pltpu.roll(side_cells[i * units : (i + 1) * units], LANES - 4 * (n + 1) - 2, 1)
+            out[at, :] = jnp.where(ends, side, inner[at, :])
+    hidden[...] = rows[: units * height].astype(BF16)
+
     outer = jnp.dot(weights[...], side_grads[...], preferred_element_type=F32)
-    first = jnp.zeros((channels, LANES), F32)
-    last = jnp.zeros((channels, LANES), F32)
-    for row_off in range(3):
-        low, high = 3 * row_off * channels, (3 * row_off + 2) * channels
-        back = (LANES - 4 * (2 - row_off)) % LANES
-        first = first + pltpu.roll(outer[high : high + channels], back, 1)
-        last = last + pltpu.roll(outer[low : low + channels], back, 1)
+    parts = []
+    for col_off in range(3):
+        part = jnp.zeros((channels, LANES), F32)
+        for row_off in range(3):
+            start = (3 * row_off + col_off) * channels
+            piece = outer[start : start + channels]
+            part = part + (pltpu.roll(piece, LANES - 4 * (2 - row_off), 1) if row_off < 2 else piece)
+        parts.append(part)
+    slot = lane % 4
+    sides = jnp.where((slot == 1) | (slot == 2), parts[1], 0.0) + jnp.where(
+        slot == 0,
+        pltpu.roll(parts[0], LANES - 1, 1),
+        jnp.where(
+            slot == 1,
+            pltpu.roll(parts[0], LANES - 2, 1),
+            jnp.where(slot == 2, pltpu.roll(parts[2], 2, 1), pltpu.roll(parts[2], 1, 1)),
+        ),
+    )
     for place in range(0, height + 2, 2):
         cells = grads[:, place * LANES : (place + 2) * LANES]
         product = jnp.dot(weights[...], cells, preferred_element_type=F32)
@@ -226,12 +297,10 @@
                         sums[n, col_off] = piece
                     else:
                         sums[n, col_off] = sums[n, col_off] + piece
+    edge = (lane < 2) | (lane >= LANES - 2)
     for n in range(height):
-        west = pltpu.roll(first, (LANES - 4 * n) % LANES, 1)
-        east = pltpu.roll(last, LANES - 2 - 4 * n, 1)
-        total = sums[n, 1]
-        total = total + jnp.where(lane == LANES - 1, east, pltpu.roll(sums[n, 0], LANES - 1, 1))
-        total = total + jnp.where(lane == 0, west, pltpu.roll(sums[n, 2], 1, 1))
+        total = sums[n, 1] + pltpu.roll(sums[n, 0], LANES - 1, 1) + pltpu.roll(sums[n, 2], 1, 1)
+        total = total + jnp.where(edge, pltpu.roll(sides, LANES - 4 * n - 2, 1), 0.0)
         rows[pl.ds(n, channels, stride=height), :] = total
     grad_frame[...] = rows[: inputs * height].astype(BF16)
     grad_hidden_prev[...] = rows[inputs * height :].astype(BF16)
@@ -289,48 +358,68 @@
     units = hidden_prev.shape[0]
     channels = inputs + units
     gate_rows = kernel.shape[0]
-    weights = kernel.reshape(gate_rows, 3, 3 * channels)
-    weights = jnp.pad(weights, ((0, 0), (0, 0), (0, STACK - 3 * channels))).reshape(gate_rows, 3 * STACK)
     flat = (units * height, breadth)
     states = (cell_prev.reshape(flat), grad_hidden.reshape(flat), grad_cell.reshape(flat))
 
     strip = shape(2 * channels + 3 * units, breadth, F32)
-    joined, up, down = called(
+    blocks = (frame.reshape(inputs * height, breadth), hidden_prev.reshape(flat), *states)
+    channel_rows = (channels * height, breadth)
+    up, down = pl.pallas_call(
         functools.partial(rows_kernel, height=height),
-        [shape(channels * height, breadth, F32), strip, strip],
+        out_shape=(strip, strip),
+        in_specs=[pl.BlockSpec(memory_space=pl.ANY)] * 5,
+        out_specs=tuple(vmem(2)),
+        scratch_shapes=[pltpu.VMEM(channel_rows, F32)]
+        + [pltpu.VMEM(x.shape, x.dtype) for x in blocks]
+        + [pltpu.SemaphoreType.DMA((5,))],
+        compiler_params=pltpu.CompilerParams(vmem_limit_bytes=60 * 2**20),
+        cost_estimate=pl.CostEstimate(flops=1_000_000, bytes_accessed=3_000_000, transcendentals=0),
+    )(*blocks)
+    edge = shape(channels + 2 * units, LANES, F32)
+    columns, weights, joined = called(
+        functools.partial(columns_kernel, height=height),
+        [edge, shape(gate_rows, 3 * STACK, BF16), shape(*channel_rows, F32)],
         [],
         1_000_000,
-        frame.reshape(inputs * height, breadth),
-        hidden_prev.reshape(flat),
-        *states,
-    )
-    edge = shape(channels + 2 * units, LANES, F32)
-    (columns,) = called(functools.partial(columns_kernel, height=height), [edge], [], 1_000_000, joined, *states)
+        *blocks,
+        kernel.T,
+    )
     top, bottom = neighbours(up, down, NS)
-    (columns,) = called(functools.partial(corners_kernel, height=height, units=units), [edge], [], 100_000, columns, top, bottom)
+    (columns,) = called(
+        functools.partial(corners_kernel, height=height, units=units), [edge], [], 100_000, columns, top, bottom
+    )
     left, right = neighbours(columns, columns, EW)
-
-    hidden, cell, grad_cell_prev, grads, side_grads, terms = called(
+    bias = bias[:, None]
+    field = shape(*flat, F32)
+    inner_hidden, inner_cell, inner_back, grads, inner_terms = called(
         forward_kernel,
         [
-            shape(*flat, BF16),
-            shape(*flat, F32),
-            shape(*flat, F32),
+            field,
+            field,
+            field,
             shape(gate_rows, (height + 2) * breadth, BF16),
-            shape(gate_rows, LANES, BF16),
-            shape(3 * STACK, gate_rows, BF16),
+            shape(3 * STACK, gate_rows, F32),
         ],
-        [pltpu.VMEM((STACK, (height + 4) * breadth), BF16), pltpu.VMEM(flat, F32)],
+        [pltpu.VMEM((STACK, (height + 4) * breadth), BF16)],
         1_400_000_000,
         joined,
+        top,
+        bottom,
+        weights,
+        bias,
+        *states,
+    )
+    side_grads, side_cells, terms = called(
+        functools.partial(sides_kernel, height=height),
+        [shape(gate_rows, LANES, BF16), shape(3 * units, LANES, F32), shape(3 * STACK, gate_rows, BF16)],
+        [],
+        100_000_000,
         columns,
         left,
         right,
-        top,
-        bottom,
         weights,
-        bias[:, None],
-        *states,
+        bias,
+        inner_terms,
     )
 
     plane = lax.axis_size(PLANE)
@@ -340,14 +429,18 @@
     mine = exchanged(summed(mine, high, F32), "z_hi")
     mine = summed(mine, plane, BF16)
     total = exchanged(mine, PLANE).reshape(3 * STACK, gate_rows)
-    grad_frame, grad_hidden_prev = called(
+    hidden, cell, grad_cell_prev, grad_frame, grad_hidden_prev = called(
         backward_kernel,
-        [shape(inputs * height, breadth, BF16), shape(*flat, BF16)],
+        [shape(*flat, BF16), field, field, shape(inputs * height, breadth, BF16), shape(*flat, BF16)],
         [pltpu.VMEM((height, 3, channels, breadth), F32), pltpu.VMEM((channels * height, breadth), F32)],
         764_000_000,
         kernel.T,
         grads,
         side_grads,
+        side_cells,
+        inner_hidden,
+        inner_cell,
+        inner_back,
     )
     kernel_step, bias_step = called(
         finish_kernel, [shape(9 * channels, gate_rows, F32), shape(1, gate_rows, F32)], [], 1_000_000, total

time: 106 us -> 99.6 us (0.940)
  local copies, waits for them, and re-layouts: 8.18 us -> 3.86 us
  starting transfers between devices: 25 us -> 22.1 us
  Pallas kernels: 10.9 us -> 12.9 us
    ppermute x2, starting transfers between devices: 10.8 us -> 7.84 us  [neighbours(): lax.ppermute(to_after, axes, forward)]
    unnamed x24 -> x30, local copies, waits for them, and re-layouts: 6.11 us -> 3.73 us
    pallas_call x0 -> x1, Pallas kernels: none -> 2.37 us  [per_device(): pl.pallas_call(functools.partial(rows_kernel, height=height), out_shape=(...]
    reshape x1 -> x0, local copies, waits for them, and re-layouts: 1.16 us -> none  [per_device(): jnp.pad(weights, ((0, 0), (0, 0), (0, STACK - 3 * channels)))]
  transfers between devices with their start and end apart: 5 -> 5, of which waited for: 1 -> 2; matrix products, arithmetic and copies ran while one was open for 2% -> 0% of each run, Pallas kernels for 3% -> 8%
where the time goes in v5:
time: 99.6 us; the launch traced here: 99.1 us
  blocking collectives  53 us (53%)
  starting transfers between devices  22.1 us (22%)
  Pallas kernels  12.9 us (13%)
  waiting for transfers between devices  6.4 us (6%)
  local copies, waits for them, and re-layouts  3.86 us (4%)
    all_to_all x3, blocking collectives, exchanged(): return lax.all_to_all(copies, axes, 0, 0, tiled=True)  53 us
    pallas_call x6, Pallas kernels, called(): pl.pallas_call(kernel, out_shape=tuple(outs), in_specs=vmem(len(args)), o...  9.68 us
    ppermute x2, starting transfers between devices, neighbours(): lax.ppermute(to_after, axes, forward)  7.84 us
    all_to_all x1, starting transfers between devices, exchanged(): return lax.all_to_all(copies, axes, 0, 0, tiled=True)  7.36 us
    ppermute x2, starting transfers between devices, neighbours(): lax.ppermute(to_before, axes, backward)  6.87 us
    all_to_all x1, waiting for transfers between devices, exchanged(): return lax.all_to_all(copies, axes, 0, 0, tiled=True)  5.83 us
    unnamed x30, local copies, waits for them, and re-layouts  3.73 us
    pallas_call x1, Pallas kernels, per_device(): pl.pallas_call(functools.partial(rows_kernel, height=height), out_shape=(...  2.37 us
  transfers between devices with their start and end apart: 5, of which 2 were waited for; matrix products, arithmetic and copies ran while one was open for 0% of the time, Pallas kernels for 8%

profile of v5, /device:TPU:1, one launch (start us, length us, event | category | flops | bytes accessed | tf_op | source)
XLA Modules:
  0.0 99.1 jit_solution(10944089211838806457)
XLA Ops:
  0.6 0.0 copy-start
  0.6 0.0 copy-start.1
  0.7 0.0 copy-start.2
  0.7 0.0 copy-start.13
  0.7 0.0 copy-start.14
  0.7 0.0 copy-start.3
  0.7 2.4 %shard_map.127 = (f32[336,128]{1,0:T(8,128)}, f32[336,128]{1,0:T(8,128)}) custom-call(bf16[128,128]{1,0:T(8,128)(2,1)} %bitcast.31, bf16[1024,128]{1,0:T(8,128)(2,1)} %bitcast.28, f32[1024,128]{1,0:T(8,128)} %bitcast.16, f32[1024,128]{1,0:T(8,128)} %bitcast.19, f32[1024,128]{1,0:T(8,128)} %bitcast.22), custom_call_target="tpu_custom_call" | custom-call | flops 1000000 | bytes 3000000 | tf_op jit(solution)/shard_map/pallas_call | solution.py:367
  3.1 4.5 %collective-permute-start = (f32[336,128]{1,0:T(8,128)}, f32[336,128]{1,0:T(8,128)S(1)}, u32[]{:S(2)}, u32[]{:S(2)}) collective-permute-start(f32[336,128]{1,0:T(8,128)} %get-tuple-element.28), channel_id=1, source_target_pairs={{0,1},{1,2},{2,3},{3,4},{4,5},{5,6},{6,7},{7,8},{8,9},{9,10},{10,1... | collective-permute-start | bytes 516104 | tf_op jit(solution)/shard_map/ppermute | solution.py:28
  7.6 5.6 %collective-permute-start.1 = (f32[336,128]{1,0:T(8,128)}, f32[336,128]{1,0:T(8,128)S(1)}, u32[]{:S(2)}, u32[]{:S(2)}) collective-permute-start(f32[336,128]{1,0:T(8,128)} %get-tuple-element.29), channel_id=1, source_target_pairs={{1,0},{2,1},{3,2},{4,3},{5,4},{6,5},{7,6},{8,7},{9,8},{10,9},{11,1... | collective-permute-start | bytes 516104 | tf_op jit(solution)/shard_map/ppermute | solution.py:28
  13.2 0.0 copy-done.14
  13.2 0.1 copy.14.bias
  13.3 0.0 copy-done
  13.3 0.0 copy-done.1
  13.3 0.0 copy-done.2
  13.4 0.0 copy-done.13
  13.4 0.0 copy-done.3
  13.4 0.0 copy-start.4
  13.4 0.9 copy-done.4
  14.3 1.2 %shard_map.126 = (f32[200,128]{1,0:T(8,128)S(1)}, bf16[256,768]{1,0:T(8,128)(2,1)S(1)}, f32[1152,128]{1,0:T(8,128)S(1)}) custom-call(bf16[128,128]{1,0:T(8,128)(2,1)S(1)} %bitcast.32, bf16[1024,128]{1,0:T(8,128)(2,1)S(1)} %bitcast.29, f32[1024,128]{1,0:T(8,128)S(1)} %bitcast.17, f32[1024,128]{1,0:T(8,128)S(1)} %bitcast.20, f32[1024,128]{1,0:T(8,128)S(1)} %bitcast.23, ...), custom_call_target="tpu_custom_call" | custom-call | flops 1000000 | bytes 2000 | tf_op jit(solution)/shard_map/pallas_call | solution.py:345
  15.5 0.0 collective-permute-done.top
  15.5 0.0 collective-permute-done.1.bottom
  15.5 0.0 copy-start.11
  15.6 0.2 shard_map.129.columns
  15.7 3.3 %collective-permute-start.2 = (f32[200,128]{1,0:T(8,128)S(1)}, f32[200,128]{1,0:T(8,128)S(1)}, u32[]{:S(2)}, u32[]{:S(2)}) collective-permute-start(f32[200,128]{1,0:T(8,128)S(1)} %shard_map.129.columns), channel_id=1, source_target_pairs={{0,16},{16,32},{32,48},{48,64},{64,80},{80,96},{96,112},{112,128},... | collective-permute-start | bytes 307208 | tf_op jit(solution)/shard_map/ppermute | solution.py:28
  19.1 1.3 %collective-permute-start.3 = (f32[200,128]{1,0:T(8,128)S(1)}, f32[200,128]{1,0:T(8,128)S(1)}, u32[]{:S(2)}, u32[]{:S(2)}) collective-permute-start(f32[200,128]{1,0:T(8,128)S(1)} %shard_map.129.columns), channel_id=1, source_target_pairs={{16,0},{32,16},{48,32},{64,48},{80,64},{96,80},{112,96},{128,112},... | collective-permute-start | bytes 307208 | tf_op jit(solution)/shard_map/ppermute | solution.py:28
  20.4 0.0 copy-done.11
  20.4 0.0 copy-start.12
  20.4 0.9 copy-done.12
  21.3 3.3 %shard_map.128 = (f32[1024,128]{1,0:T(8,128)S(1)}, f32[1024,128]{1,0:T(8,128)S(1)}, f32[1024,128]{1,0:T(8,128)S(1)}, bf16[256,2304]{1,0:T(8,128)(2,1)S(1)}, f32[768,256]{1,0:T(8,128)S(1)}) custom-call(f32[1152,128]{1,0:T(8,128)S(1)} %get-tuple-element.27.joined, f32[336,128]{1,0:T(8,128)S(1)} %collective-permute-done.top, f32[336,128]{1,0:T(8,128)S(1)} %copy-done.12, ...), custom_call_target="tpu_custom_call" | custom-call | flops 1400000000 | bytes 2800000 | tf_op jit(solution)/shard_map/pallas_call | solution.py:345
  24.6 0.0 copy-start.5
  24.6 0.8 copy-done.5
  25.4 0.0 collective-permute-done.2.left
  25.4 0.6 collective-permute-done.3.right
  26.0 0.8 shard_map.130
  26.8 18.6 %all_to_all.20.parts = bf16[32,24,256]{2,1,0:T(8,128)(2,1)S(1)} all-to-all(bf16[32,24,256]{2,1,0:T(8,128)(2,1)S(1)} %bitcast.30), channel_id=1, replica_groups=mesh['z_hi'=4,'z_lo'=4,'x_hi'=2,'y'=4,'x_lo'=2,'core'=2] {'x_hi','y','x_..., dimensions={0} | all-to-all | bytes 786432 | tf_op jit(solution)/shard_map/all_to_all | solution.py:337
  45.3 0.0 copy-done.7
  45.3 0.0 copy-done.9
  45.3 0.1 shard_map.132
  45.4 12.8 %all_to_all.21.parts = f32[4,24,256]{2,1,0:T(8,128)S(1)} all-to-all(f32[4,24,256]{2,1,0:T(8,128)S(1)} %shard_map.132), channel_id=1, replica_groups=mesh['z_hi'=4,'z_lo'=4,'x_hi'=2,'y'=4,'x_lo'=2,'core'=2] {'z_lo'}, dimensions={0} | all-to-all | bytes 196608 | tf_op jit(solution)/shard_map/all_to_all | solution.py:337
  58.2 21.7 %all_to_all.22.parts = f32[4,24,256]{2,1,0:T(8,128)S(1)} all-to-all(f32[4,24,256]{2,1,0:T(8,128)S(1)} %shard_map.133), channel_id=1, replica_groups=mesh['z_hi'=4,'z_lo'=4,'x_hi'=2,'y'=4,'x_lo'=2,'core'=2] {'z_hi'}, dimensions={0} | all-to-all | bytes 196608 | tf_op jit(solution)/shard_map/all_to_all | solution.py:337
  79.8 0.8 shard_map.134
  80.6 7.4 %all-to-all-start.3 = ((bf16[32,24,256]{2,1,0:T(8,128)(2,1)}), bf16[32,24,256]{2,1,0:T(8,128)(2,1)S(1)}, u32[]{:S(2)}, u32[]{:S(2)}) async-start(bf16[32,24,256]{2,1,0:T(8,128)(2,1)} %shard_map.134), calls=%async_computation.3 | async-start | bytes 786432 | tf_op jit(solution)/shard_map/all_to_all | solution.py:337
  88.0 0.0 copy-done.6
  88.0 0.0 copy-start.10
  88.0 1.0 %copy-done.10 = f32[1024,128]{1,0:T(8,128)S(1)} copy-done((f32[1024,128]{1,0:T(8,128)S(1)}, f32[1024,128]{1,0:T(8,128)}, u32[]{:S(2)}) %copy-start.10) | copy-done | bytes 524312
  89.0 3.1 %shard_map.131 = (bf16[1024,128]{1,0:T(8,128)(2,1)}, f32[1024,128]{1,0:T(8,128)}, f32[1024,128]{1,0:T(8,128)}, bf16[128,128]{1,0:T(8,128)(2,1)}, bf16[1024,128]{1,0:T(8,128)(2,1)}) custom-call(bf16[648,256]{1,0:T(8,128)(2,1)S(1)} %bitcast.27, bf16[256,2304]{1,0:T(8,128)(2,1)S(1)} %get-tuple-element.31.grads, ...), custom_call_target="tpu_custom_call" | custom-call | flops 764000000 | bytes 1528000 | tf_op jit(solution)/shard_map/pallas_call | solution.py:345
  92.1 5.8 %all-to-all-done.3 = bf16[32,24,256]{2,1,0:T(8,128)(2,1)S(1)} async-done(((bf16[32,24,256]{2,1,0:T(8,128)(2,1)}), bf16[32,24,256]{2,1,0:T(8,128)(2,1)S(1)}, u32[]{:S(2)}, u32[]{:S(2)}) %all-to-all-start.3) | async-done | bytes 393248 | tf_op jit(solution)/shard_map/all_to_all | solution.py:337
  97.9 1.2 %shard_map.135 = (f32[648,256]{1,0:T(8,128)}, f32[1,256]{1,0:T(1,128)}) custom-call(bf16[768,256]{1,0:T(8,128)(2,1)S(1)} %bitcast.25), custom_call_target="tpu_custom_call" | custom-call | flops 1000000 | bytes 2000 | tf_op jit(solution)/shard_map/pallas_call | solution.py:345
  (6 shorter events, 0.0 us)
Async XLA Ops:
  0.6 12.7 %copy-start = (f32[64,16,128]{2,1,0:T(8,128)S(1)}, f32[64,16,128]{2,1,0:T(8,128)}, u32[]{:S(2)}) copy-start(f32[64,16,128]{2,1,0:T(8,128)} %param.9) | copy-start | bytes 1572868
  0.6 12.7 %copy-start.1 = (f32[64,16,128]{2,1,0:T(8,128)S(1)}, f32[64,16,128]{2,1,0:T(8,128)}, u32[]{:S(2)}) copy-start(f32[64,16,128]{2,1,0:T(8,128)} %param.12) | copy-start | bytes 1572868
  0.7 12.7 %copy-start.2 = (f32[64,16,128]{2,1,0:T(8,128)S(1)}, f32[64,16,128]{2,1,0:T(8,128)}, u32[]{:S(2)}) copy-start(f32[64,16,128]{2,1,0:T(8,128)} %param.13) | copy-start | bytes 1572868
  0.7 12.7 %copy-start.13 = (bf16[8,16,128]{2,1,0:T(8,128)(2,1)S(1)}, bf16[8,16,128]{2,1,0:T(8,128)(2,1)}, u32[]{:S(2)}) copy-start(bf16[8,16,128]{2,1,0:T(8,128)(2,1)} %param.7) | copy-start | bytes 98308
  0.7 12.5 %copy-start.14 = (f32[256]{0:T(256)S(1)}, f32[256]{0:T(256)}, u32[]{:S(2)}) copy-start(f32[256]{0:T(256)} %param.11) | copy-start | bytes 3076
  0.7 12.7 %copy-start.3 = (bf16[256,648]{0,1:T(8,128)(2,1)S(1)}, bf16[256,648]{0,1:T(8,128)(2,1)}, u32[]{:S(2)}) copy-start(bf16[256,648]{0,1:T(8,128)(2,1)} %param.10) | copy-start | bytes 995332
  3.1 12.5 %collective-permute-start = (f32[336,128]{1,0:T(8,128)}, f32[336,128]{1,0:T(8,128)S(1)}, u32[]{:S(2)}, u32[]{:S(2)}) collective-permute-start(f32[336,128]{1,0:T(8,128)} %get-tuple-element.28), channel_id=1, source_target_pairs={{0,1},{1,2},{2,3},{3,4},{4,5},{5,6},{6,7},{7,8},{8,9},{9,10},{10,1... | collective-permute-start | bytes 516104 | tf_op jit(solution)/shard_map/ppermute | solution.py:28
  7.6 8.0 %collective-permute-start.1 = (f32[336,128]{1,0:T(8,128)}, f32[336,128]{1,0:T(8,128)S(1)}, u32[]{:S(2)}, u32[]{:S(2)}) collective-permute-start(f32[336,128]{1,0:T(8,128)} %get-tuple-element.29), channel_id=1, source_target_pairs={{1,0},{2,1},{3,2},{4,3},{5,4},{6,5},{7,6},{8,7},{9,8},{10,9},{11,1... | collective-permute-start | bytes 516104 | tf_op jit(solution)/shard_map/ppermute | solution.py:28
  13.4 1.0 copy-start.4
  15.5 4.8 %copy-start.11 = (f32[336,128]{1,0:T(8,128)}, f32[336,128]{1,0:T(8,128)S(1)}, u32[]{:S(2)}) copy-start(f32[336,128]{1,0:T(8,128)S(1)} %collective-permute-done.1.bottom) | copy-start | bytes 516100
  15.7 9.7 %collective-permute-start.2 = (f32[200,128]{1,0:T(8,128)S(1)}, f32[200,128]{1,0:T(8,128)S(1)}, u32[]{:S(2)}, u32[]{:S(2)}) collective-permute-start(f32[200,128]{1,0:T(8,128)S(1)} %shard_map.129.columns), channel_id=1, source_target_pairs={{0,16},{16,32},{32,48},{48,64},{64,80},{80,96},{96,112},{112,128},... | collective-permute-start | bytes 307208 | tf_op jit(solution)/shard_map/ppermute | solution.py:28
  19.1 6.9 %collective-permute-start.3 = (f32[200,128]{1,0:T(8,128)S(1)}, f32[200,128]{1,0:T(8,128)S(1)}, u32[]{:S(2)}, u32[]{:S(2)}) collective-permute-start(f32[200,128]{1,0:T(8,128)S(1)} %shard_map.129.columns), channel_id=1, source_target_pairs={{16,0},{32,16},{48,32},{64,48},{80,64},{96,80},{112,96},{128,112},... | collective-permute-start | bytes 307208 | tf_op jit(solution)/shard_map/ppermute | solution.py:28
  20.4 0.9 copy-start.12
  24.6 0.8 copy-start.5
  25.4 19.9 %copy-start.7 = (f32[1024,128]{1,0:T(8,128)}, f32[1024,128]{1,0:T(8,128)S(1)}, u32[]{:S(2)}) copy-start(f32[1024,128]{1,0:T(8,128)S(1)} %get-tuple-element.37.inner_cell) | copy-start | bytes 1572868
  25.4 19.9 %copy-start.9 = (f32[1024,128]{1,0:T(8,128)}, f32[1024,128]{1,0:T(8,128)S(1)}, u32[]{:S(2)}) copy-start(f32[1024,128]{1,0:T(8,128)S(1)} %get-tuple-element.38.inner_back) | copy-start | bytes 1572868
  45.3 42.7 %copy-start.6 = (f32[1024,128]{1,0:T(8,128)S(1)}, f32[1024,128]{1,0:T(8,128)}, u32[]{:S(2)}) copy-start(f32[1024,128]{1,0:T(8,128)} %copy-done.5) | copy-start | bytes 1572868
  45.4 42.6 %copy-start.8 = (f32[1024,128]{1,0:T(8,128)S(1)}, f32[1024,128]{1,0:T(8,128)}, u32[]{:S(2)}) copy-start(f32[1024,128]{1,0:T(8,128)} %copy-done.7) | copy-start | bytes 1572868
  80.6 17.3 %all-to-all-start.3 = ((bf16[32,24,256]{2,1,0:T(8,128)(2,1)}), bf16[32,24,256]{2,1,0:T(8,128)(2,1)S(1)}, u32[]{:S(2)}, u32[]{:S(2)}) async-start(bf16[32,24,256]{2,1,0:T(8,128)(2,1)} %shard_map.134), calls=%async_computation.3 | async-start | bytes 786432 | tf_op jit(solution)/shard_map/all_to_all | solution.py:337
  88.0 1.0 %copy-start.10 = (f32[1024,128]{1,0:T(8,128)S(1)}, f32[1024,128]{1,0:T(8,128)}, u32[]{:S(2)}) copy-start(f32[1024,128]{1,0:T(8,128)} %copy-done.9) | copy-start | bytes 1572868

commit v6 on v5

--- a/solution.py
+++ b/solution.py
@@ -33,33 +33,28 @@
 
 
 def rows_kernel(
-    frame, hidden_prev, cell_prev, grad_hidden, grad_cell, up, down, joined, frame_here, hidden_here, *rest, height
+    frame, hidden_prev, cell_prev, grad_hidden, grad_cell, up, down, joined, frame_here, hidden_here, ends, sems
 ):
-    *here, sems = rest
+    inputs, height, _ = frame_here.shape
     copies = [
-        pltpu.make_async_copy(source, target, sems.at[i])
-        for i, (source, target) in enumerate(
-            zip((frame, hidden_prev, cell_prev, grad_hidden, grad_cell), (frame_here, hidden_here, *here))
-        )
+        pltpu.make_async_copy(frame, frame_here, sems.at[0]),
+        pltpu.make_async_copy(hidden_prev, hidden_here, sems.at[1]),
     ]
+    for i, state in enumerate((cell_prev, grad_hidden, grad_cell)):
+        for j, n in enumerate((0, height - 1)):
+            copies.append(pltpu.make_async_copy(state.at[:, n, :], ends.at[j, i], sems.at[2 + 2 * i + j]))
     for copy in copies:
         copy.start()
-    inputs = frame_here.shape[0]
     channels = joined.shape[0] // height
-    units = here[0].shape[0] // height
-    sides = ((up, (0, 1), 0), (down, (height - 2, height - 1), height - 1))
     copies[0].wait()
-    joined[:inputs] = frame_here[...].astype(F32)
+    joined[: inputs * height] = frame_here[...].astype(F32).reshape(-1, LANES)
     copies[1].wait()
-    joined[inputs:] = hidden_here[...].astype(F32)
-    for out, rows, _ in sides:
-        for i, n in enumerate(rows):
-            out[i * channels : (i + 1) * channels] = joined[pl.ds(n, channels, stride=height), :]
-    for i, state in enumerate(here):
-        copies[2 + i].wait()
-        start = 2 * channels + i * units
-        for out, _, n in sides:
-            out[start : start + units] = state[pl.ds(n, units, stride=height), :]
+    joined[inputs * height :] = hidden_here[...].astype(F32).reshape(-1, LANES)
+    for copy in copies[2:]:
+        copy.wait()
+    for j, (out, rows) in enumerate(((up, (0, 1)), (down, (height - 2, height - 1)))):
+        parts = [joined[pl.ds(n, channels, stride=height), :] for n in rows]
+        out[...] = jnp.concatenate(parts + [ends[j, i] for i in range(3)], 0).astype(BF16)
 
 
 def put_channels(tile, row, place):
@@ -98,8 +93,10 @@
     columns[channels + units :] = single
 
 
-def corners_kernel(columns, top, bottom, out, *, height, units):
+def corners_kernel(columns, top, bottom, out, sent, *, height, units):
     channels = columns.shape[0] - 2 * units
+    top = top[...].astype(F32)
+    bottom = bottom[...].astype(F32)
     tile = columns[:channels]
     pairs = columns[channels : channels + units]
     single = columns[channels + units :]
@@ -110,9 +107,10 @@
         pairs = put_state(pairs, states[0], state_place, 0)
         pairs = put_state(pairs, states[1], state_place, 2)
         single = put_state(single, states[2], state_place, 0)
-    out[:channels] = tile
-    out[channels : channels + units] = pairs
-    out[channels + units :] = single
+    whole = jnp.concatenate([tile, pairs, single], 0)
+    out[...] = whole
+    spare = jnp.zeros((sent.shape[0] - out.shape[0], LANES), F32)
+    sent[...] = jnp.concatenate([whole, spare], 0).astype(BF16)
 
 
 def gate_step(gates, old, down, grad_cell):
@@ -136,8 +134,10 @@
 def forward_kernel(
     joined, top, bottom, weights, bias, cell_prev, grad_hidden, grad_cell,
     hidden, cell, grad_cell_prev, grads, terms,
-    stacked,
+    stacked, hidden_rows, hidden_here, cell_here, back_here, sems,
 ):
+    top = top[...].astype(F32)
+    bottom = bottom[...].astype(F32)
     units = bias.shape[0] // 4
     height = cell_prev.shape[0] // units
     channels = joined.shape[0] // height
@@ -178,9 +178,18 @@
             new_hidden, new, down, row_grads = gate_step(gates, *states)
             grads[:, place * LANES : (place + 1) * LANES] = jnp.where(middle, row_grads, 0.0).astype(BF16)
             if inside:
-                hidden[at, :] = new_hidden
-                cell[at, :] = new
-                grad_cell_prev[at, :] = down
+                hidden_rows[at, :] = new_hidden
+                cell_here[at, :] = new
+                back_here[at, :] = down
+    hidden_here[...] = hidden_rows[...].astype(BF16)
+    copies = [
+        pltpu.make_async_copy(source, target, sems.at[i])
+        for i, (source, target) in enumerate(
+            ((hidden_here, hidden), (cell_here, cell), (back_here, grad_cell_prev))
+        )
+    ]
+    for copy in copies:
+        copy.start()
     for row_off in range(3):
         terms[row_off * STACK : (row_off + 1) * STACK] = lax.dot_general(
             stacked[:, (row_off + 1) * LANES : (row_off + 1 + height) * LANES],
@@ -188,12 +197,16 @@
             (((1,), (1,)), ((), ())),
             preferred_element_type=F32,
         )
+    for copy in copies:
+        copy.wait()
 
 
 def sides_kernel(columns, left, right, weights, bias, inner_terms, side_grads, side_cells, terms, *, height):
     units = bias.shape[0] // 4
     channels = columns.shape[0] - 2 * units
     spare = STACK - 3 * channels
+    left = left[...].astype(F32)
+    right = right[...].astype(F32)
 
     def moved(x, lanes):
         return pltpu.roll(x, lanes % LANES, 1)
@@ -256,9 +269,10 @@
     channels = inputs + units
     lane = lax.broadcasted_iota(jnp.int32, (channels, LANES), 1)
     ends = (lane[:units] == 0) | (lane[:units] == LANES - 1)
+    rows[: units * height] = inner_hidden[...].astype(F32)
     for n in range(height):
         at = pl.ds(n, units, stride=height)
-        for i, (inner, out) in enumerate(((inner_hidden, rows), (inner_cell, cell), (inner_back, grad_cell_prev))):
+        for i, (inner, out) in enumerate(((rows, rows), (inner_cell, cell), (inner_back, grad_cell_prev))):
             side = pltpu.roll(side_cells[i * units : (i + 1) * units], LANES - 4 * (n + 1) - 2, 1)
             out[at, :] = jnp.where(ends, side, inner[at, :])
     hidden[...] = rows[: units * height].astype(BF16)
@@ -341,14 +355,15 @@
     return jax.ShapeDtypeStruct((rows, columns), kind)
 
 
-def called(kernel, outs, scratch, cost, *args, mebibytes=16):
+def called(kernel, outs, scratch, cost, *args, aliases={}):
     return pl.pallas_call(
         kernel,
         out_shape=tuple(outs),
         in_specs=vmem(len(args)),
         out_specs=tuple(vmem(len(outs))),
         scratch_shapes=scratch,
-        compiler_params=pltpu.CompilerParams(vmem_limit_bytes=mebibytes * 2**20),
+        input_output_aliases=aliases,
+        compiler_params=pltpu.CompilerParams(vmem_limit_bytes=16 * 2**20),
         cost_estimate=pl.CostEstimate(flops=cost, bytes_accessed=2 * cost // 1000, transcendentals=0),
     )(*args)
 
@@ -361,20 +376,25 @@
     flat = (units * height, breadth)
     states = (cell_prev.reshape(flat), grad_hidden.reshape(flat), grad_cell.reshape(flat))
 
-    strip = shape(2 * channels + 3 * units, breadth, F32)
+    strip = shape(2 * channels + 3 * units, breadth, BF16)
     blocks = (frame.reshape(inputs * height, breadth), hidden_prev.reshape(flat), *states)
     channel_rows = (channels * height, breadth)
+    arrays = (frame, hidden_prev, cell_prev, grad_hidden, grad_cell)
     up, down = pl.pallas_call(
-        functools.partial(rows_kernel, height=height),
+        rows_kernel,
         out_shape=(strip, strip),
         in_specs=[pl.BlockSpec(memory_space=pl.ANY)] * 5,
         out_specs=tuple(vmem(2)),
-        scratch_shapes=[pltpu.VMEM(channel_rows, F32)]
-        + [pltpu.VMEM(x.shape, x.dtype) for x in blocks]
-        + [pltpu.SemaphoreType.DMA((5,))],
+        scratch_shapes=[
+            pltpu.VMEM(channel_rows, F32),
+            pltpu.VMEM(frame.shape, BF16),
+            pltpu.VMEM(hidden_prev.shape, BF16),
+            pltpu.VMEM((2, 3, units, breadth), F32),
+            pltpu.SemaphoreType.DMA((8,)),
+        ],
         compiler_params=pltpu.CompilerParams(vmem_limit_bytes=60 * 2**20),
-        cost_estimate=pl.CostEstimate(flops=1_000_000, bytes_accessed=3_000_000, transcendentals=0),
-    )(*blocks)
+        cost_estimate=pl.CostEstimate(flops=1_000_000, bytes_accessed=1_000_000, transcendentals=0),
+    )(*arrays)
     edge = shape(channels + 2 * units, LANES, F32)
     columns, weights, joined = called(
         functools.partial(columns_kernel, height=height),
@@ -385,30 +405,30 @@
         kernel.T,
     )
     top, bottom = neighbours(up, down, NS)
-    (columns,) = called(
-        functools.partial(corners_kernel, height=height, units=units), [edge], [], 100_000, columns, top, bottom
-    )
-    left, right = neighbours(columns, columns, EW)
+    sent = shape(-(-(channels + 2 * units) // 16) * 16, LANES, BF16)
+    columns, sent = called(
+        functools.partial(corners_kernel, height=height, units=units), [edge, sent], [], 100_000, columns, top, bottom
+    )
+    left, right = neighbours(sent, sent, EW)
     bias = bias[:, None]
     field = shape(*flat, F32)
-    inner_hidden, inner_cell, inner_back, grads, inner_terms = called(
+    inner_hidden, inner_cell, inner_back, grads, inner_terms = pl.pallas_call(
         forward_kernel,
-        [
-            field,
+        out_shape=(
+            shape(*flat, BF16),
             field,
             field,
             shape(gate_rows, (height + 2) * breadth, BF16),
             shape(3 * STACK, gate_rows, F32),
-        ],
-        [pltpu.VMEM((STACK, (height + 4) * breadth), BF16)],
-        1_400_000_000,
-        joined,
-        top,
-        bottom,
-        weights,
-        bias,
-        *states,
-    )
+        ),
+        in_specs=vmem(8),
+        out_specs=tuple([pl.BlockSpec(memory_space=pl.ANY)] * 3 + vmem(2)),
+        scratch_shapes=[pltpu.VMEM((STACK, (height + 4) * breadth), BF16)]
+        + [pltpu.VMEM(flat, kind) for kind in (F32, BF16, F32, F32)]
+        + [pltpu.SemaphoreType.DMA((3,))],
+        compiler_params=pltpu.CompilerParams(vmem_limit_bytes=16 * 2**20),
+        cost_estimate=pl.CostEstimate(flops=1_400_000_000, bytes_accessed=4_000_000, transcendentals=700_000),
+    )(joined, top, bottom, weights, bias, *states)
     side_grads, side_cells, terms = called(
         functools.partial(sides_kernel, height=height),
         [shape(gate_rows, LANES, BF16), shape(3 * units, LANES, F32), shape(3 * STACK, gate_rows, BF16)],
@@ -441,6 +461,7 @@
         inner_hidden,
         inner_cell,
         inner_back,
+        aliases={4: 0, 5: 1, 6: 2},
     )
     kernel_step, bias_step = called(
         finish_kernel, [shape(9 * channels, gate_rows, F32), shape(1, gate_rows, F32)], [], 1_000_000, total

time: 99.6 us -> 97.1 us (0.975)
  local copies, waits for them, and re-layouts: 3.86 us -> 1.1 us
  Pallas kernels: 12.9 us -> 14.6 us
    pallas_call x1 -> x2, Pallas kernels: 2.37 us -> 6.15 us  [the longest x1 4.24 us: per_device(): pl.pallas_call(forward_kernel, out_shape=(shape(*flat, BF16), field, fiel...]
    unnamed x30 -> x14, local copies, waits for them, and re-layouts: 3.73 us -> 0.97 us
    pallas_call x6 -> x5, Pallas kernels: 9.68 us -> 7.58 us  [called(): pl.pallas_call(kernel, out_shape=tuple(outs), in_specs=vmem(len(args)), o...]
  transfers between devices with their start and end apart: 5 -> 5, of which waited for: 2 -> 2; matrix products, arithmetic and copies ran while one was open for 0% -> 0% of each run, Pallas kernels for 8% -> 10%
where the time goes in v6:
time: 97.1 us; the launch traced here: 96.6 us
  blocking collectives  52.5 us (54%)
  starting transfers between devices  21.2 us (22%)
  Pallas kernels  14.6 us (15%)
  waiting for transfers between devices  6.48 us (7%)
  local copies, waits for them, and re-layouts  1.1 us (1%)
    all_to_all x3, blocking collectives, exchanged(): return lax.all_to_all(copies, axes, 0, 0, tiled=True)  52.5 us
    pallas_call x5, Pallas kernels, called(): pl.pallas_call(kernel, out_shape=tuple(outs), in_specs=vmem(len(args)), o...  7.58 us
    all_to_all x1, starting transfers between devices, exchanged(): return lax.all_to_all(copies, axes, 0, 0, tiled=True)  7.36 us
    ppermute x2, starting transfers between devices, neighbours(): lax.ppermute(to_after, axes, forward)  6.92 us
    ppermute x2, starting transfers between devices, neighbours(): lax.ppermute(to_before, axes, backward)  6.86 us
    all_to_all x1, waiting for transfers between devices, exchanged(): return lax.all_to_all(copies, axes, 0, 0, tiled=True)  5.65 us
    pallas_call x1, Pallas kernels, per_device(): pl.pallas_call(forward_kernel, out_shape=(shape(*flat, BF16), field, fiel...  4.24 us
  transfers between devices with their start and end apart: 5, of which 2 were waited for; matrix products, arithmetic and copies ran while one was open for 0% of the time, Pallas kernels for 10%

profile of v6, /device:TPU:1, one launch (start us, length us, event | category | flops | bytes accessed | tf_op | source)
XLA Modules:
  0.0 96.6 jit_solution(5517320789257779364)
XLA Ops:
  0.6 0.0 copy-start
  0.6 0.0 copy-start.1
  0.7 0.0 copy-start.2
  0.7 0.0 copy-start.5
  0.7 0.0 copy-start.6
  0.7 0.0 copy-start.3
  0.7 1.9 %shard_map.127 = (bf16[336,128]{1,0:T(8,128)(2,1)}, bf16[336,128]{1,0:T(8,128)(2,1)}) custom-call(bf16[8,16,128]{2,1,0:T(8,128)(2,1)} %frame.1, bf16[64,16,128]{2,1,0:T(8,128)(2,1)} %hidden_prev.1, f32[64,16,128]{2,1,0:T(8,128)} %cell_prev.1, f32[64,16,128]{2,1,0:T(8,128)} %grad_hidden.1, f32[64,16,128]{2,1,0:T(8,128)} %grad_cell.1), custom_call_target="tpu_custom_call" | custom-call | flops 1000000 | bytes 1000000 | tf_op jit(solution)/shard_map/pallas_call | solution.py:383
  2.6 4.5 %collective-permute-start = (bf16[336,128]{1,0:T(8,128)(2,1)}, bf16[336,128]{1,0:T(8,128)(2,1)S(1)}, u32[]{:S(2)}, u32[]{:S(2)}) collective-permute-start(bf16[336,128]{1,0:T(8,128)(2,1)} %get-tuple-element.30), channel_id=1, source_target_pairs={{0,1},{1,2},{2,3},{3,4},{4,5},{5,6},{6,7},{7,8},{8,9},{9,10},{10,1... | collective-permute-start | bytes 258056 | tf_op jit(solution)/shard_map/ppermute | solution.py:28
  7.1 5.6 %collective-permute-start.1 = (bf16[336,128]{1,0:T(8,128)(2,1)}, bf16[336,128]{1,0:T(8,128)(2,1)S(1)}, u32[]{:S(2)}, u32[]{:S(2)}) collective-permute-start(bf16[336,128]{1,0:T(8,128)(2,1)} %get-tuple-element.31), channel_id=1, source_target_pairs={{1,0},{2,1},{3,2},{4,3},{5,4},{6,5},{7,6},{8,7},{9,8},{10,9},{11,1... | collective-permute-start | bytes 258056 | tf_op jit(solution)/shard_map/ppermute | solution.py:28
  12.7 0.0 copy-done.6
  12.7 0.1 copy.17.bias
  12.9 0.0 copy-done
  12.9 0.0 copy-done.1
  12.9 0.0 copy-done.2
  12.9 0.0 copy-done.5
  12.9 0.0 copy-done.3
  12.9 0.0 copy-start.4
  12.9 0.9 copy-done.4
  13.9 1.2 %shard_map.126 = (f32[200,128]{1,0:T(8,128)S(1)}, bf16[256,768]{1,0:T(8,128)(2,1)S(1)}, f32[1152,128]{1,0:T(8,128)S(1)}) custom-call(bf16[128,128]{1,0:T(8,128)(2,1)S(1)} %bitcast.27, bf16[1024,128]{1,0:T(8,128)(2,1)S(1)} %bitcast.25, f32[1024,128]{1,0:T(8,128)S(1)} %bitcast.16, f32[1024,128]{1,0:T(8,128)S(1)} %bitcast.18, f32[1024,128]{1,0:T(8,128)S(1)} %bitcast.20, ...), custom_call_target="tpu_custom_call" | custom-call | flops 1000000 | bytes 2000 | tf_op jit(solution)/shard_map/pallas_call | solution.py:359
  15.1 0.0 collective-permute-done.top
  15.1 0.0 collective-permute-done.1.bottom
  15.1 0.1 shard_map.129
  15.2 2.4 %collective-permute-start.2 = (bf16[208,128]{1,0:T(8,128)(2,1)S(1)}, bf16[208,128]{1,0:T(8,128)(2,1)S(1)}, u32[]{:S(2)}, u32[]{:S(2)}) collective-permute-start(bf16[208,128]{1,0:T(8,128)(2,1)S(1)} %get-tuple-element.36), channel_id=1, source_target_pairs={{0,16},{16,32},{32,48},{48,64},{64,80},{80,96},{96,112},{112,128},... | collective-permute-start | bytes 159752 | tf_op jit(solution)/shard_map/ppermute | solution.py:28
  17.6 1.3 %collective-permute-start.3 = (bf16[208,128]{1,0:T(8,128)(2,1)S(1)}, bf16[208,128]{1,0:T(8,128)(2,1)S(1)}, u32[]{:S(2)}, u32[]{:S(2)}) collective-permute-start(bf16[208,128]{1,0:T(8,128)(2,1)S(1)} %get-tuple-element.36), channel_id=1, source_target_pairs={{16,0},{32,16},{48,32},{64,48},{80,64},{96,80},{112,96},{128,112},... | collective-permute-start | bytes 159752 | tf_op jit(solution)/shard_map/ppermute | solution.py:28
  18.9 4.2 %shard_map.128 = (bf16[1024,128]{1,0:T(8,128)(2,1)}, f32[1024,128]{1,0:T(8,128)}, f32[1024,128]{1,0:T(8,128)}, bf16[256,2304]{1,0:T(8,128)(2,1)S(1)}, f32[768,256]{1,0:T(8,128)S(1)}) custom-call(f32[1152,128]{1,0:T(8,128)S(1)} %get-tuple-element.29.joined, bf16[336,128]{1,0:T(8,128)(2,1)S(1)} %collective-permute-done.top, ...), custom_call_target="tpu_custom_call" | custom-call | flops 1400000000 | bytes 4000000 | tf_op jit(solution)/shard_map/pallas_call | solution.py:415
  23.2 0.0 collective-permute-done.2.left
  23.2 0.8 collective-permute-done.3.right
  24.0 0.8 shard_map.130
  24.8 18.2 %all_to_all.20.parts = bf16[32,24,256]{2,1,0:T(8,128)(2,1)S(1)} all-to-all(bf16[32,24,256]{2,1,0:T(8,128)(2,1)S(1)} %bitcast.26), channel_id=1, replica_groups=mesh['z_hi'=4,'z_lo'=4,'x_hi'=2,'y'=4,'x_lo'=2,'core'=2] {'x_hi','y','x_..., dimensions={0} | all-to-all | bytes 786432 | tf_op jit(solution)/shard_map/all_to_all | solution.py:351
  43.0 0.1 shard_map.132
  43.1 12.6 %all_to_all.21.parts = f32[4,24,256]{2,1,0:T(8,128)S(1)} all-to-all(f32[4,24,256]{2,1,0:T(8,128)S(1)} %shard_map.132), channel_id=1, replica_groups=mesh['z_hi'=4,'z_lo'=4,'x_hi'=2,'y'=4,'x_lo'=2,'core'=2] {'z_lo'}, dimensions={0} | all-to-all | bytes 196608 | tf_op jit(solution)/shard_map/all_to_all | solution.py:351
  55.7 21.7 %all_to_all.22.parts = f32[4,24,256]{2,1,0:T(8,128)S(1)} all-to-all(f32[4,24,256]{2,1,0:T(8,128)S(1)} %shard_map.133), channel_id=1, replica_groups=mesh['z_hi'=4,'z_lo'=4,'x_hi'=2,'y'=4,'x_lo'=2,'core'=2] {'z_hi'}, dimensions={0} | all-to-all | bytes 196608 | tf_op jit(solution)/shard_map/all_to_all | solution.py:351
  77.3 0.8 shard_map.134
  78.1 7.4 %all-to-all-start.3 = ((bf16[32,24,256]{2,1,0:T(8,128)(2,1)}), bf16[32,24,256]{2,1,0:T(8,128)(2,1)S(1)}, u32[]{:S(2)}, u32[]{:S(2)}) async-start(bf16[32,24,256]{2,1,0:T(8,128)(2,1)} %shard_map.134), calls=%async_computation.3 | async-start | bytes 786432 | tf_op jit(solution)/shard_map/all_to_all | solution.py:351
  85.5 4.3 %shard_map.131 = (bf16[1024,128]{1,0:T(8,128)(2,1)}, f32[1024,128]{1,0:T(8,128)}, f32[1024,128]{1,0:T(8,128)}, bf16[128,128]{1,0:T(8,128)(2,1)}, bf16[1024,128]{1,0:T(8,128)(2,1)}) custom-call(bf16[648,256]{1,0:T(8,128)(2,1)S(1)} %bitcast.24, ...), custom_call_target="tpu_custom_call", output_to_operand_aliasing={{0}: (4, {}), {1}: (5, {}), {2}: (6, {})} | custom-call | flops 764000000 | bytes 1528000 | tf_op jit(solution)/shard_map/pallas_call | solution.py:359
  89.8 5.7 %all-to-all-done.3 = bf16[32,24,256]{2,1,0:T(8,128)(2,1)S(1)} async-done(((bf16[32,24,256]{2,1,0:T(8,128)(2,1)}), bf16[32,24,256]{2,1,0:T(8,128)(2,1)S(1)}, u32[]{:S(2)}, u32[]{:S(2)}) %all-to-all-start.3) | async-done | bytes 393248 | tf_op jit(solution)/shard_map/all_to_all | solution.py:351
  95.5 1.2 %shard_map.135 = (f32[648,256]{1,0:T(8,128)}, f32[1,256]{1,0:T(1,128)}) custom-call(bf16[768,256]{1,0:T(8,128)(2,1)S(1)} %bitcast.22), custom_call_target="tpu_custom_call" | custom-call | flops 1000000 | bytes 2000 | tf_op jit(solution)/shard_map/pallas_call | solution.py:359
  (1 shorter events, 0.0 us)
Async XLA Ops:
  0.6 12.2 %copy-start = (f32[64,16,128]{2,1,0:T(8,128)S(1)}, f32[64,16,128]{2,1,0:T(8,128)}, u32[]{:S(2)}) copy-start(f32[64,16,128]{2,1,0:T(8,128)} %cell_prev.1) | copy-start | bytes 1572868
  0.6 12.2 %copy-start.1 = (f32[64,16,128]{2,1,0:T(8,128)S(1)}, f32[64,16,128]{2,1,0:T(8,128)}, u32[]{:S(2)}) copy-start(f32[64,16,128]{2,1,0:T(8,128)} %grad_hidden.1) | copy-start | bytes 1572868
  0.7 12.2 %copy-start.2 = (f32[64,16,128]{2,1,0:T(8,128)S(1)}, f32[64,16,128]{2,1,0:T(8,128)}, u32[]{:S(2)}) copy-start(f32[64,16,128]{2,1,0:T(8,128)} %grad_cell.1) | copy-start | bytes 1572868
  0.7 12.2 %copy-start.5 = (bf16[8,16,128]{2,1,0:T(8,128)(2,1)S(1)}, bf16[8,16,128]{2,1,0:T(8,128)(2,1)}, u32[]{:S(2)}) copy-start(bf16[8,16,128]{2,1,0:T(8,128)(2,1)} %frame.1) | copy-start | bytes 98308
  0.7 12.0 %copy-start.6 = (f32[256]{0:T(256)S(1)}, f32[256]{0:T(256)}, u32[]{:S(2)}) copy-start(f32[256]{0:T(256)} %param.11) | copy-start | bytes 3076
  0.7 12.2 %copy-start.3 = (bf16[256,648]{0,1:T(8,128)(2,1)S(1)}, bf16[256,648]{0,1:T(8,128)(2,1)}, u32[]{:S(2)}) copy-start(bf16[256,648]{0,1:T(8,128)(2,1)} %param.10) | copy-start | bytes 995332
  2.6 12.5 %collective-permute-start = (bf16[336,128]{1,0:T(8,128)(2,1)}, bf16[336,128]{1,0:T(8,128)(2,1)S(1)}, u32[]{:S(2)}, u32[]{:S(2)}) collective-permute-start(bf16[336,128]{1,0:T(8,128)(2,1)} %get-tuple-element.30), channel_id=1, source_target_pairs={{0,1},{1,2},{2,3},{3,4},{4,5},{5,6},{6,7},{7,8},{8,9},{9,10},{10,1... | collective-permute-start | bytes 258056 | tf_op jit(solution)/shard_map/ppermute | solution.py:28
  7.1 7.9 %collective-permute-start.1 = (bf16[336,128]{1,0:T(8,128)(2,1)}, bf16[336,128]{1,0:T(8,128)(2,1)S(1)}, u32[]{:S(2)}, u32[]{:S(2)}) collective-permute-start(bf16[336,128]{1,0:T(8,128)(2,1)} %get-tuple-element.31), channel_id=1, source_target_pairs={{1,0},{2,1},{3,2},{4,3},{5,4},{6,5},{7,6},{8,7},{9,8},{10,9},{11,1... | collective-permute-start | bytes 258056 | tf_op jit(solution)/shard_map/ppermute | solution.py:28
  12.9 1.0 copy-start.4
  15.2 8.0 %collective-permute-start.2 = (bf16[208,128]{1,0:T(8,128)(2,1)S(1)}, bf16[208,128]{1,0:T(8,128)(2,1)S(1)}, u32[]{:S(2)}, u32[]{:S(2)}) collective-permute-start(bf16[208,128]{1,0:T(8,128)(2,1)S(1)} %get-tuple-element.36), channel_id=1, source_target_pairs={{0,16},{16,32},{32,48},{48,64},{64,80},{80,96},{96,112},{112,128},... | collective-permute-start | bytes 159752 | tf_op jit(solution)/shard_map/ppermute | solution.py:28
  17.6 6.4 %collective-permute-start.3 = (bf16[208,128]{1,0:T(8,128)(2,1)S(1)}, bf16[208,128]{1,0:T(8,128)(2,1)S(1)}, u32[]{:S(2)}, u32[]{:S(2)}) collective-permute-start(bf16[208,128]{1,0:T(8,128)(2,1)S(1)} %get-tuple-element.36), channel_id=1, source_target_pairs={{16,0},{32,16},{48,32},{64,48},{80,64},{96,80},{112,96},{128,112},... | collective-permute-start | bytes 159752 | tf_op jit(solution)/shard_map/ppermute | solution.py:28
  78.1 17.3 %all-to-all-start.3 = ((bf16[32,24,256]{2,1,0:T(8,128)(2,1)}), bf16[32,24,256]{2,1,0:T(8,128)(2,1)S(1)}, u32[]{:S(2)}, u32[]{:S(2)}) async-start(bf16[32,24,256]{2,1,0:T(8,128)(2,1)} %shard_map.134), calls=%async_computation.3 | async-start | bytes 786432 | tf_op jit(solution)/shard_map/all_to_all | solution.py:351

commit v7 on v6

--- a/solution.py
+++ b/solution.py
@@ -21,11 +21,19 @@
     return [pl.BlockSpec(memory_space=pltpu.VMEM)] * count
 
 
-def neighbours(to_before, to_after, axes):
+def swapped(to_pair, to_next, axes):
     count = lax.axis_size(axes)
-    forward = [(i, i + 1) for i in range(count - 1)]
-    backward = [(target, source) for source, target in forward]
-    return lax.ppermute(to_after, axes, forward), lax.ppermute(to_before, axes, backward)
+    pairs = [(i, i ^ 1) for i in range(count) if i ^ 1 < count]
+    across = [(i, (i + 1 ^ 1) - 1) for i in range(1, count - 1)]
+    other = lax.ppermute(to_next, axes, across)
+    return other, lax.ppermute(to_pair, axes, pairs)
+
+
+def in_order(from_next, from_pair, axis):
+    first = lax.axis_index(axis) == 0
+    from_pair = from_pair[...].astype(F32)
+    from_next = from_next[...].astype(F32)
+    return jnp.where(first, from_next, from_pair), jnp.where(first, from_pair, from_next)
 
 
 def sigmoid(x):
@@ -33,7 +41,7 @@
 
 
 def rows_kernel(
-    frame, hidden_prev, cell_prev, grad_hidden, grad_cell, up, down, joined, frame_here, hidden_here, ends, sems
+    frame, hidden_prev, cell_prev, grad_hidden, grad_cell, to_pair, to_next, joined, frame_here, hidden_here, ends, sems
 ):
     inputs, height, _ = frame_here.shape
     copies = [
@@ -52,9 +60,13 @@
     joined[inputs * height :] = hidden_here[...].astype(F32).reshape(-1, LANES)
     for copy in copies[2:]:
         copy.wait()
-    for j, (out, rows) in enumerate(((up, (0, 1)), (down, (height - 2, height - 1)))):
+    strips = []
+    for j, rows in enumerate(((0, 1), (height - 2, height - 1))):
         parts = [joined[pl.ds(n, channels, stride=height), :] for n in rows]
-        out[...] = jnp.concatenate(parts + [ends[j, i] for i in range(3)], 0).astype(BF16)
+        strips.append(jnp.concatenate(parts + [ends[j, i] for i in range(3)], 0))
+    first = lax.axis_index(NS[-1]) == 0
+    to_pair[...] = jnp.where(first, strips[1], strips[0]).astype(BF16)
+    to_next[...] = jnp.where(first, strips[0], strips[1]).astype(BF16)
 
 
 def put_channels(tile, row, place):
@@ -67,8 +79,14 @@
     return jnp.where(lane // 2 == 2 * place + slot // 2, pltpu.roll(row, (4 * place + slot + 1) % LANES, 1), tile)
 
 
+def stack_of(row):
+    spare = STACK - 3 * row.shape[0]
+    ones_row = (lax.broadcasted_iota(jnp.int32, (spare, LANES), 0) == 0).astype(F32)
+    return jnp.concatenate([pltpu.roll(row, 1, 1), row, pltpu.roll(row, LANES - 1, 1), ones_row], 0).astype(BF16)
+
+
 def columns_kernel(
-    frame, hidden_prev, cell_prev, grad_hidden, grad_cell, kernel, columns, weights, joined, *, height
+    frame, hidden_prev, cell_prev, grad_hidden, grad_cell, kernel, columns, weights, stacked, joined, *, height
 ):
     joined[: frame.shape[0]] = frame[...].astype(F32)
     joined[frame.shape[0] :] = hidden_prev[...].astype(F32)
@@ -84,7 +102,9 @@
     single = jnp.zeros((units, LANES), F32)
     for n in range(height):
         at = pl.ds(n, units, stride=height)
-        tile = put_channels(tile, joined[pl.ds(n, channels, stride=height), :], n + 2)
+        row = joined[pl.ds(n, channels, stride=height), :]
+        stacked[:, n * LANES : (n + 1) * LANES] = stack_of(row)
+        tile = put_channels(tile, row, n + 2)
         pairs = put_state(pairs, cell_prev[at, :], n + 1, 0)
         pairs = put_state(pairs, grad_hidden[at, :], n + 1, 2)
         single = put_state(single, grad_cell[at, :], n + 1, 0)
@@ -93,10 +113,9 @@
     columns[channels + units :] = single
 
 
-def corners_kernel(columns, top, bottom, out, sent, *, height, units):
+def corners_kernel(columns, from_next, from_pair, out, sent, *, height, units):
     channels = columns.shape[0] - 2 * units
-    top = top[...].astype(F32)
-    bottom = bottom[...].astype(F32)
+    top, bottom = in_order(from_next, from_pair, NS[-1])
     tile = columns[:channels]
     pairs = columns[channels : channels + units]
     single = columns[channels + units :]
@@ -132,37 +151,43 @@
 
 
 def forward_kernel(
-    joined, top, bottom, weights, bias, cell_prev, grad_hidden, grad_cell,
+    stacked, from_next, from_pair, weights, bias, cell_prev, grad_hidden, grad_cell,
     hidden, cell, grad_cell_prev, grads, terms,
-    stacked, hidden_rows, hidden_here, cell_here, back_here, sems,
+    hidden_rows, hidden_here, cell_here, back_here, sems,
 ):
-    top = top[...].astype(F32)
-    bottom = bottom[...].astype(F32)
     units = bias.shape[0] // 4
     height = cell_prev.shape[0] // units
-    channels = joined.shape[0] // height
-    spare = STACK - 3 * channels
-    ones_row = (lax.broadcasted_iota(jnp.int32, (spare, LANES), 0) == 0).astype(F32)
-    for place in range(height + 4):
-        if place < 2:
-            row = top[place * channels : (place + 1) * channels]
-        elif place >= height + 2:
-            row = bottom[(place - height - 2) * channels : (place - height - 1) * channels]
-        else:
-            row = joined[pl.ds(place - 2, channels, stride=height), :]
-        stacked[:, place * LANES : (place + 1) * LANES] = jnp.concatenate(
-            [pltpu.roll(row, 1, 1), row, pltpu.roll(row, LANES - 1, 1), ones_row], 0
-        ).astype(BF16)
+    channels = (from_pair.shape[0] - 3 * units) // 2
+    top, bottom = in_order(from_next, from_pair, NS[-1])
+    north = [stack_of(top[i * channels : (i + 1) * channels]) for i in range(2)]
+    south = [stack_of(bottom[i * channels : (i + 1) * channels]) for i in range(2)]
+
+    def two_rows(place):
+        if 2 <= place <= height:
+            return stacked[:, (place - 2) * LANES : place * LANES]
+        outer = [None] * (height + 4)
+        outer[:2], outer[-2:] = north, south
+        outer[2], outer[-3] = stacked[:, :LANES], stacked[:, (height - 1) * LANES :]
+        return jnp.concatenate(outer[place : place + 2], 1)
+
+    def copy_out(half):
+        rows = pl.ds(half * (height // 2), height // 2)
+        return [
+            pltpu.make_async_copy(here.at[:, rows, :], out.at[:, rows, :], sems.at[2 * half + i])
+            for i, (here, out) in enumerate(((cell_here, cell), (back_here, grad_cell_prev)))
+        ]
+
+    cell_rows = cell_here.reshape(units * height, LANES)
+    back_rows = back_here.reshape(units * height, LANES)
     bias_cells = jnp.broadcast_to(bias[...], (4 * units, LANES))
     lane = lax.broadcasted_iota(jnp.int32, (4 * units, LANES), 1)
     middle = (lane > 0) & (lane < LANES - 1)
     for pair in range(height // 2 + 1):
         sums = jnp.zeros((4 * units, 2 * LANES), F32)
         for row_off in range(3):
-            start = (2 * pair + row_off) * LANES
             sums = sums + jnp.dot(
                 weights[:, row_off * STACK : (row_off + 1) * STACK],
-                stacked[:, start : start + 2 * LANES],
+                two_rows(2 * pair + row_off),
                 preferred_element_type=F32,
             )
         for half in range(2):
@@ -179,34 +204,38 @@
             grads[:, place * LANES : (place + 1) * LANES] = jnp.where(middle, row_grads, 0.0).astype(BF16)
             if inside:
                 hidden_rows[at, :] = new_hidden
-                cell_here[at, :] = new
-                back_here[at, :] = down
+                cell_rows[at, :] = new
+                back_rows[at, :] = down
+        if pair == height // 4:
+            for copy in copy_out(0):
+                copy.start()
     hidden_here[...] = hidden_rows[...].astype(BF16)
-    copies = [
-        pltpu.make_async_copy(source, target, sems.at[i])
-        for i, (source, target) in enumerate(
-            ((hidden_here, hidden), (cell_here, cell), (back_here, grad_cell_prev))
-        )
-    ]
-    for copy in copies:
+    hidden_copy = pltpu.make_async_copy(hidden_here, hidden, sems.at[4])
+    copies = copy_out(0) + copy_out(1) + [hidden_copy]
+    for copy in copies[2:]:
         copy.start()
+    own = grads[:, LANES : (height + 1) * LANES]
     for row_off in range(3):
+        if row_off == 0:
+            rows = jnp.concatenate([north[1], stacked[:, : (height - 1) * LANES]], 1)
+        elif row_off == 1:
+            rows = stacked[...]
+        else:
+            rows = jnp.concatenate([stacked[:, LANES:], south[0]], 1)
         terms[row_off * STACK : (row_off + 1) * STACK] = lax.dot_general(
-            stacked[:, (row_off + 1) * LANES : (row_off + 1 + height) * LANES],
-            grads[:, LANES : (height + 1) * LANES],
-            (((1,), (1,)), ((), ())),
-            preferred_element_type=F32,
+            rows, own, (((1,), (1,)), ((), ())), preferred_element_type=F32
         )
     for copy in copies:
         copy.wait()
 
 
-def sides_kernel(columns, left, right, weights, bias, inner_terms, side_grads, side_cells, terms, *, height):
+def sides_kernel(
+    columns, from_next, from_pair, weights, bias, inner_terms, side_grads, side_cells, terms, *, height
+):
     units = bias.shape[0] // 4
     channels = columns.shape[0] - 2 * units
     spare = STACK - 3 * channels
-    left = left[...].astype(F32)
-    right = right[...].astype(F32)
+    left, right = in_order(from_next, from_pair, EW[-1])
 
     def moved(x, lanes):
         return pltpu.roll(x, lanes % LANES, 1)
@@ -380,7 +409,7 @@
     blocks = (frame.reshape(inputs * height, breadth), hidden_prev.reshape(flat), *states)
     channel_rows = (channels * height, breadth)
     arrays = (frame, hidden_prev, cell_prev, grad_hidden, grad_cell)
-    up, down = pl.pallas_call(
+    to_pair, to_next = pl.pallas_call(
         rows_kernel,
         out_shape=(strip, strip),
         in_specs=[pl.BlockSpec(memory_space=pl.ANY)] * 5,
@@ -396,47 +425,51 @@
         cost_estimate=pl.CostEstimate(flops=1_000_000, bytes_accessed=1_000_000, transcendentals=0),
     )(*arrays)
     edge = shape(channels + 2 * units, LANES, F32)
-    columns, weights, joined = called(
+    columns, weights, stacked = called(
         functools.partial(columns_kernel, height=height),
-        [edge, shape(gate_rows, 3 * STACK, BF16), shape(*channel_rows, F32)],
-        [],
+        [edge, shape(gate_rows, 3 * STACK, BF16), shape(STACK, height * breadth, BF16)],
+        [pltpu.VMEM(channel_rows, F32)],
         1_000_000,
         *blocks,
         kernel.T,
     )
-    top, bottom = neighbours(up, down, NS)
+    rows = swapped(to_pair, to_next, NS)
     sent = shape(-(-(channels + 2 * units) // 16) * 16, LANES, BF16)
     columns, sent = called(
-        functools.partial(corners_kernel, height=height, units=units), [edge, sent], [], 100_000, columns, top, bottom
-    )
-    left, right = neighbours(sent, sent, EW)
+        functools.partial(corners_kernel, height=height, units=units), [edge, sent], [], 100_000, columns, *rows
+    )
+    sides = swapped(sent, sent, EW)
     bias = bias[:, None]
     field = shape(*flat, F32)
+    cube = jax.ShapeDtypeStruct((units, height, breadth), F32)
     inner_hidden, inner_cell, inner_back, grads, inner_terms = pl.pallas_call(
         forward_kernel,
         out_shape=(
             shape(*flat, BF16),
-            field,
-            field,
+            cube,
+            cube,
             shape(gate_rows, (height + 2) * breadth, BF16),
             shape(3 * STACK, gate_rows, F32),
         ),
         in_specs=vmem(8),
         out_specs=tuple([pl.BlockSpec(memory_space=pl.ANY)] * 3 + vmem(2)),
-        scratch_shapes=[pltpu.VMEM((STACK, (height + 4) * breadth), BF16)]
-        + [pltpu.VMEM(flat, kind) for kind in (F32, BF16, F32, F32)]
-        + [pltpu.SemaphoreType.DMA((3,))],
+        scratch_shapes=[
+            pltpu.VMEM(flat, F32),
+            pltpu.VMEM(flat, BF16),
+            pltpu.VMEM(cube.shape, F32),
+            pltpu.VMEM(cube.shape, F32),
+            pltpu.SemaphoreType.DMA((5,)),
+        ],
         compiler_params=pltpu.CompilerParams(vmem_limit_bytes=16 * 2**20),
         cost_estimate=pl.CostEstimate(flops=1_400_000_000, bytes_accessed=4_000_000, transcendentals=700_000),
-    )(joined, top, bottom, weights, bias, *states)
+    )(stacked, *rows, weights, bias, *states)
     side_grads, side_cells, terms = called(
         functools.partial(sides_kernel, height=height),
         [shape(gate_rows, LANES, BF16), shape(3 * units, LANES, F32), shape(3 * STACK, gate_rows, BF16)],
         [],
         100_000_000,
         columns,
-        left,
-        right,
+        *sides,
         weights,
         bias,
         inner_terms,
@@ -459,8 +492,8 @@
         side_grads,
         side_cells,
         inner_hidden,
-        inner_cell,
-        inner_back,
+        inner_cell.reshape(flat),
+        inner_back.reshape(flat),
         aliases={4: 0, 5: 1, 6: 2},
     )
     kernel_step, bias_step = called(

time: 97.1 us -> 94.6 us (0.974)
  blocking collectives: 52.5 us -> 50.6 us
    all_to_all x3, blocking collectives: 52.5 us -> 50.6 us  [exchanged(): return lax.all_to_all(copies, axes, 0, 0, tiled=True)]
  transfers between devices with their start and end apart: 5 -> 5, of which waited for: 2 -> 1; matrix products, arithmetic and copies ran while one was open for 0% -> 0% of each run, Pallas kernels for 10% -> 10%
where the time goes in v7:
time: 94.6 us; the launch traced here: 94.1 us
  blocking collectives  50.6 us (53%)
  starting transfers between devices  21.9 us (23%)
  Pallas kernels  13.9 us (15%)
  waiting for transfers between devices  5.67 us (6%)
  local copies, waits for them, and re-layouts  1.1 us (1%)
    all_to_all x3, blocking collectives, exchanged(): return lax.all_to_all(copies, axes, 0, 0, tiled=True)  50.6 us
    ppermute x2, starting transfers between devices, swapped(): return (other, lax.ppermute(to_pair, axes, pairs))  9.4 us
    pallas_call x5, Pallas kernels, called(): pl.pallas_call(kernel, out_shape=tuple(outs), in_specs=vmem(len(args)), o...  7.55 us
    all_to_all x1, starting transfers between devices, exchanged(): return lax.all_to_all(copies, axes, 0, 0, tiled=True)  7.36 us
    all_to_all x1, waiting for transfers between devices, exchanged(): return lax.all_to_all(copies, axes, 0, 0, tiled=True)  5.66 us
    ppermute x2, starting transfers between devices, swapped(): other = lax.ppermute(to_next, axes, across)  5.17 us
    pallas_call x1, Pallas kernels, per_device(): pl.pallas_call(forward_kernel, out_shape=(shape(*flat, BF16), cube, cube,...  3.56 us
    pallas_call x1, Pallas kernels, per_device(): pl.pallas_call(rows_kernel, out_shape=(strip, strip), in_specs=[pl.BlockS...  1.93 us
  transfers between devices with their start and end apart: 5, of which 1 were waited for; matrix products, arithmetic and copies ran while one was open for 0% of the time, Pallas kernels for 10%

profile of v7, /device:TPU:1, one launch (start us, length us, event | category | flops | bytes accessed | tf_op | source)
XLA Modules:
  0.0 94.1 jit_solution(13724064932759745426)
XLA Ops:
  0.6 0.0 copy-start
  0.6 0.0 copy-start.1
  0.7 0.0 copy-start.2
  0.7 0.0 copy-start.5
  0.7 0.0 copy-start.6
  0.7 0.0 copy-start.3
  0.7 1.9 %shard_map.127 = (bf16[336,128]{1,0:T(8,128)(2,1)}, bf16[336,128]{1,0:T(8,128)(2,1)}) custom-call(bf16[8,16,128]{2,1,0:T(8,128)(2,1)} %frame.1, bf16[64,16,128]{2,1,0:T(8,128)(2,1)} %hidden_prev.1, f32[64,16,128]{2,1,0:T(8,128)} %cell_prev.1, f32[64,16,128]{2,1,0:T(8,128)} %grad_hidden.1, f32[64,16,128]{2,1,0:T(8,128)} %grad_cell.1), custom_call_target="tpu_custom_call" | custom-call | flops 1000000 | bytes 1000000 | tf_op jit(solution)/shard_map/pallas_call | solution.py:412
  2.6 4.5 %collective-permute-start = (bf16[336,128]{1,0:T(8,128)(2,1)}, bf16[336,128]{1,0:T(8,128)(2,1)S(1)}, u32[]{:S(2)}, u32[]{:S(2)}) collective-permute-start(bf16[336,128]{1,0:T(8,128)(2,1)} %get-tuple-element.30), channel_id=1, source_target_pairs={{1,2},{2,1},{3,4},{4,3},{5,6},{6,5},{7,8},{8,7},{9,10},{10,9},{11,... | collective-permute-start | bytes 258056 | tf_op jit(solution)/shard_map/ppermute | solution.py:28
  7.1 4.9 %collective-permute-start.1 = (bf16[336,128]{1,0:T(8,128)(2,1)}, bf16[336,128]{1,0:T(8,128)(2,1)S(1)}, u32[]{:S(2)}, u32[]{:S(2)}) collective-permute-start(bf16[336,128]{1,0:T(8,128)(2,1)} %get-tuple-element.31), channel_id=1, source_target_pairs={{0,1},{1,0},{2,3},{3,2},{4,5},{5,4},{6,7},{7,6},{8,9},{9,8},{10,11... | collective-permute-start | bytes 258056 | tf_op jit(solution)/shard_map/ppermute | solution.py:29
  12.1 0.0 copy-done.6
  12.1 0.1 copy.17.bias
  12.2 0.0 copy-done
  12.3 0.0 copy-done.1
  12.3 0.0 copy-done.2
  12.3 0.0 copy-done.5
  12.3 0.0 copy-done.3
  12.3 0.0 copy-start.4
  12.3 0.9 copy-done.4
  13.2 1.1 %shard_map.126 = (f32[200,128]{1,0:T(8,128)S(1)}, bf16[256,768]{1,0:T(8,128)(2,1)S(1)}, bf16[256,2048]{1,0:T(8,128)(2,1)S(1)}) custom-call(bf16[128,128]{1,0:T(8,128)(2,1)S(1)} %bitcast.29, bf16[1024,128]{1,0:T(8,128)(2,1)S(1)} %bitcast.27, f32[1024,128]{1,0:T(8,128)S(1)} %bitcast.18, f32[1024,128]{1,0:T(8,128)S(1)} %bitcast.20, f32[1024,128]{1,0:T(8,128)S(1)} %bitcast.22, ...), custom_call_target="tpu_custom_call" | custom-call | flops 1000000 | bytes 2000 | tf_op jit(solution)/shard_map/pallas_call | solution.py:388
  14.4 0.0 collective-permute-done.from_next
  14.4 0.0 collective-permute-done.1.from_pair
  14.4 0.1 shard_map.129
  14.6 0.7 collective-permute-start.2
  15.2 4.5 %collective-permute-start.3 = (bf16[208,128]{1,0:T(8,128)(2,1)S(1)}, bf16[208,128]{1,0:T(8,128)(2,1)S(1)}, u32[]{:S(2)}, u32[]{:S(2)}) collective-permute-start(bf16[208,128]{1,0:T(8,128)(2,1)S(1)} %get-tuple-element.36), channel_id=1, source_target_pairs={{0,16},{16,0},{32,48},{48,32},{64,80},{80,64},{96,112},{112,96},{1... | collective-permute-start | bytes 159752 | tf_op jit(solution)/shard_map/ppermute | solution.py:29
  19.7 3.6 %shard_map.128 = (bf16[1024,128]{1,0:T(8,128)(2,1)}, f32[64,16,128]{2,1,0:T(8,128)}, f32[64,16,128]{2,1,0:T(8,128)}, bf16[256,2304]{1,0:T(8,128)(2,1)S(1)}, f32[768,256]{1,0:T(8,128)S(1)}) custom-call(bf16[256,2048]{1,0:T(8,128)(2,1)S(1)} %get-tuple-element.29.stacked, bf16[336,128]{1,0:T(8,128)(2,1)S(1)} %collective-permute-done.from_next, ...), custom_call_target="tpu_custom_call" | custom-call | flops 1400000000 | bytes 4000000 | tf_op jit(solution)/shard_map/pallas_call | solution.py:445
  23.3 0.0 collective-permute-done.2.from_next
  23.3 0.0 collective-permute-done.3.from_pair
  23.3 0.8 shard_map.130
  24.1 17.2 %all_to_all.20.parts = bf16[32,24,256]{2,1,0:T(8,128)(2,1)S(1)} all-to-all(bf16[32,24,256]{2,1,0:T(8,128)(2,1)S(1)} %bitcast.28), channel_id=1, replica_groups=mesh['z_hi'=4,'z_lo'=4,'x_hi'=2,'y'=4,'x_lo'=2,'core'=2] {'x_hi','y','x_..., dimensions={0} | all-to-all | bytes 786432 | tf_op jit(solution)/shard_map/all_to_all | solution.py:380
  41.3 0.1 shard_map.132
  41.3 11.4 %all_to_all.21.parts = f32[4,24,256]{2,1,0:T(8,128)S(1)} all-to-all(f32[4,24,256]{2,1,0:T(8,128)S(1)} %shard_map.132), channel_id=1, replica_groups=mesh['z_hi'=4,'z_lo'=4,'x_hi'=2,'y'=4,'x_lo'=2,'core'=2] {'z_lo'}, dimensions={0} | all-to-all | bytes 196608 | tf_op jit(solution)/shard_map/all_to_all | solution.py:380
  52.8 22.0 %all_to_all.22.parts = f32[4,24,256]{2,1,0:T(8,128)S(1)} all-to-all(f32[4,24,256]{2,1,0:T(8,128)S(1)} %shard_map.133), channel_id=1, replica_groups=mesh['z_hi'=4,'z_lo'=4,'x_hi'=2,'y'=4,'x_lo'=2,'core'=2] {'z_hi'}, dimensions={0} | all-to-all | bytes 196608 | tf_op jit(solution)/shard_map/all_to_all | solution.py:380
  74.8 0.8 shard_map.134
  75.6 7.4 %all-to-all-start.3 = ((bf16[32,24,256]{2,1,0:T(8,128)(2,1)}), bf16[32,24,256]{2,1,0:T(8,128)(2,1)S(1)}, u32[]{:S(2)}, u32[]{:S(2)}) async-start(bf16[32,24,256]{2,1,0:T(8,128)(2,1)} %shard_map.134), calls=%async_computation.3 | async-start | bytes 786432 | tf_op jit(solution)/shard_map/all_to_all | solution.py:380
  83.0 4.3 %shard_map.131 = (bf16[1024,128]{1,0:T(8,128)(2,1)}, f32[1024,128]{1,0:T(8,128)}, f32[1024,128]{1,0:T(8,128)}, bf16[128,128]{1,0:T(8,128)(2,1)}, bf16[1024,128]{1,0:T(8,128)(2,1)}) custom-call(bf16[648,256]{1,0:T(8,128)(2,1)S(1)} %bitcast.26, ...), custom_call_target="tpu_custom_call", output_to_operand_aliasing={{0}: (4, {}), {1}: (5, {}), {2}: (6, {})} | custom-call | flops 764000000 | bytes 1528000 | tf_op jit(solution)/shard_map/pallas_call | solution.py:388
  87.3 5.7 %all-to-all-done.3 = bf16[32,24,256]{2,1,0:T(8,128)(2,1)S(1)} async-done(((bf16[32,24,256]{2,1,0:T(8,128)(2,1)}), bf16[32,24,256]{2,1,0:T(8,128)(2,1)S(1)}, u32[]{:S(2)}, u32[]{:S(2)}) %all-to-all-start.3) | async-done | bytes 393248 | tf_op jit(solution)/shard_map/all_to_all | solution.py:380
  92.9 1.2 %shard_map.135 = (f32[648,256]{1,0:T(8,128)}, f32[1,256]{1,0:T(1,128)}) custom-call(bf16[768,256]{1,0:T(8,128)(2,1)S(1)} %bitcast.24), custom_call_target="tpu_custom_call" | custom-call | flops 1000000 | bytes 2000 | tf_op jit(solution)/shard_map/pallas_call | solution.py:388
  (1 shorter events, 0.0 us)
Async XLA Ops:
  0.6 11.6 %copy-start = (f32[64,16,128]{2,1,0:T(8,128)S(1)}, f32[64,16,128]{2,1,0:T(8,128)}, u32[]{:S(2)}) copy-start(f32[64,16,128]{2,1,0:T(8,128)} %cell_prev.1) | copy-start | bytes 1572868
  0.6 11.6 %copy-start.1 = (f32[64,16,128]{2,1,0:T(8,128)S(1)}, f32[64,16,128]{2,1,0:T(8,128)}, u32[]{:S(2)}) copy-start(f32[64,16,128]{2,1,0:T(8,128)} %grad_hidden.1) | copy-start | bytes 1572868
  0.7 11.6 %copy-start.2 = (f32[64,16,128]{2,1,0:T(8,128)S(1)}, f32[64,16,128]{2,1,0:T(8,128)}, u32[]{:S(2)}) copy-start(f32[64,16,128]{2,1,0:T(8,128)} %grad_cell.1) | copy-start | bytes 1572868
  0.7 11.6 %copy-start.5 = (bf16[8,16,128]{2,1,0:T(8,128)(2,1)S(1)}, bf16[8,16,128]{2,1,0:T(8,128)(2,1)}, u32[]{:S(2)}) copy-start(bf16[8,16,128]{2,1,0:T(8,128)(2,1)} %frame.1) | copy-start | bytes 98308
  0.7 11.4 %copy-start.6 = (f32[256]{0:T(256)S(1)}, f32[256]{0:T(256)}, u32[]{:S(2)}) copy-start(f32[256]{0:T(256)} %param.11) | copy-start | bytes 3076
  0.7 11.6 %copy-start.3 = (bf16[256,648]{0,1:T(8,128)(2,1)S(1)}, bf16[256,648]{0,1:T(8,128)(2,1)}, u32[]{:S(2)}) copy-start(bf16[256,648]{0,1:T(8,128)(2,1)} %param.10) | copy-start | bytes 995332
  2.6 11.8 %collective-permute-start = (bf16[336,128]{1,0:T(8,128)(2,1)}, bf16[336,128]{1,0:T(8,128)(2,1)S(1)}, u32[]{:S(2)}, u32[]{:S(2)}) collective-permute-start(bf16[336,128]{1,0:T(8,128)(2,1)} %get-tuple-element.30), channel_id=1, source_target_pairs={{1,2},{2,1},{3,4},{4,3},{5,6},{6,5},{7,8},{8,7},{9,10},{10,9},{11,... | collective-permute-start | bytes 258056 | tf_op jit(solution)/shard_map/ppermute | solution.py:28
  7.1 7.3 %collective-permute-start.1 = (bf16[336,128]{1,0:T(8,128)(2,1)}, bf16[336,128]{1,0:T(8,128)(2,1)S(1)}, u32[]{:S(2)}, u32[]{:S(2)}) collective-permute-start(bf16[336,128]{1,0:T(8,128)(2,1)} %get-tuple-element.31), channel_id=1, source_target_pairs={{0,1},{1,0},{2,3},{3,2},{4,5},{5,4},{6,7},{7,6},{8,9},{9,8},{10,11... | collective-permute-start | bytes 258056 | tf_op jit(solution)/shard_map/ppermute | solution.py:29
  12.3 1.0 %copy-start.4 = (bf16[64,16,128]{2,1,0:T(8,128)(2,1)S(1)}, bf16[64,16,128]{2,1,0:T(8,128)(2,1)}, u32[]{:S(2)}) copy-start(bf16[64,16,128]{2,1,0:T(8,128)(2,1)} %hidden_prev.1) | copy-start | bytes 786436
  14.6 8.7 %collective-permute-start.2 = (bf16[208,128]{1,0:T(8,128)(2,1)S(1)}, bf16[208,128]{1,0:T(8,128)(2,1)S(1)}, u32[]{:S(2)}, u32[]{:S(2)}) collective-permute-start(bf16[208,128]{1,0:T(8,128)(2,1)S(1)} %get-tuple-element.36), channel_id=1, source_target_pairs={{16,32},{32,16},{48,64},{64,48},{80,96},{96,80},{112,128},{128,112... | collective-permute-start | bytes 159752 | tf_op jit(solution)/shard_map/ppermute | solution.py:28
  15.2 8.0 %collective-permute-start.3 = (bf16[208,128]{1,0:T(8,128)(2,1)S(1)}, bf16[208,128]{1,0:T(8,128)(2,1)S(1)}, u32[]{:S(2)}, u32[]{:S(2)}) collective-permute-start(bf16[208,128]{1,0:T(8,128)(2,1)S(1)} %get-tuple-element.36), channel_id=1, source_target_pairs={{0,16},{16,0},{32,48},{48,32},{64,80},{80,64},{96,112},{112,96},{1... | collective-permute-start | bytes 159752 | tf_op jit(solution)/shard_map/ppermute | solution.py:29
  75.6 17.3 %all-to-all-start.3 = ((bf16[32,24,256]{2,1,0:T(8,128)(2,1)}), bf16[32,24,256]{2,1,0:T(8,128)(2,1)S(1)}, u32[]{:S(2)}, u32[]{:S(2)}) async-start(bf16[32,24,256]{2,1,0:T(8,128)(2,1)} %shard_map.134), calls=%async_computation.3 | async-start | bytes 786432 | tf_op jit(solution)/shard_map/all_to_all | solution.py:380

commit v8 on v7

--- a/solution.py
+++ b/solution.py
@@ -13,6 +13,7 @@
 PLANE = ("x_hi", "y", "x_lo", "core")
 LANES = 128
 STACK = 256
+STEP = 6
 BF16 = jnp.bfloat16
 F32 = jnp.float32
 
@@ -71,12 +72,13 @@
 
 def put_channels(tile, row, place):
     lane = lax.broadcasted_iota(jnp.int32, tile.shape, 1)
-    return jnp.where(lane // 4 == place, pltpu.roll(row, (4 * place + 2) % LANES, 1), tile)
+    return jnp.where(lane // STEP == place, pltpu.roll(row, (STEP * place + 2) % LANES, 1), tile)
 
 
 def put_state(tile, row, place, slot):
     lane = lax.broadcasted_iota(jnp.int32, tile.shape, 1)
-    return jnp.where(lane // 2 == 2 * place + slot // 2, pltpu.roll(row, (4 * place + slot + 1) % LANES, 1), tile)
+    start = STEP * place + slot
+    return jnp.where(lane // 2 == start // 2, pltpu.roll(row, (start + 1) % LANES, 1), tile)
 
 
 def stack_of(row):
@@ -85,51 +87,58 @@
     return jnp.concatenate([pltpu.roll(row, 1, 1), row, pltpu.roll(row, LANES - 1, 1), ones_row], 0).astype(BF16)
 
 
-def columns_kernel(
-    frame, hidden_prev, cell_prev, grad_hidden, grad_cell, kernel, columns, weights, stacked, joined, *, height
-):
+def columns_kernel(frame, hidden_prev, cell_prev, grad_hidden, grad_cell, columns, stacked, joined, *, height):
     joined[: frame.shape[0]] = frame[...].astype(F32)
     joined[frame.shape[0] :] = hidden_prev[...].astype(F32)
-    depth = kernel.shape[0] // 3
-    blank = jnp.zeros((STACK - depth, kernel.shape[1]), F32)
-    for row_off in range(3):
-        part = kernel[...].astype(F32)[row_off * depth : (row_off + 1) * depth]
-        weights[:, row_off * STACK : (row_off + 1) * STACK] = jnp.concatenate([part, blank], 0).T.astype(BF16)
     channels = joined.shape[0] // height
     units = cell_prev.shape[0] // height
     tile = jnp.zeros((channels, LANES), F32)
-    pairs = jnp.zeros((units, LANES), F32)
-    single = jnp.zeros((units, LANES), F32)
+    states = jnp.zeros((units, LANES), F32)
     for n in range(height):
         at = pl.ds(n, units, stride=height)
         row = joined[pl.ds(n, channels, stride=height), :]
         stacked[:, n * LANES : (n + 1) * LANES] = stack_of(row)
         tile = put_channels(tile, row, n + 2)
-        pairs = put_state(pairs, cell_prev[at, :], n + 1, 0)
-        pairs = put_state(pairs, grad_hidden[at, :], n + 1, 2)
-        single = put_state(single, grad_cell[at, :], n + 1, 0)
+        for i, state in enumerate((cell_prev, grad_hidden, grad_cell)):
+            states = put_state(states, state[at, :], n + 1, 2 * i)
     columns[:channels] = tile
-    columns[channels : channels + units] = pairs
-    columns[channels + units :] = single
-
-
-def corners_kernel(columns, from_next, from_pair, out, sent, *, height, units):
-    channels = columns.shape[0] - 2 * units
+    columns[channels:] = states
+
+
+def moved(x, lanes):
+    return pltpu.roll(x, lanes % LANES, 1) if lanes else x
+
+
+def by_slot(slot, *choices):
+    out = choices[-1]
+    for i in range(len(choices) - 2, -1, -1):
+        out = jnp.where(slot == i, choices[i], out)
+    return out
+
+
+def corners_kernel(columns, from_next, from_pair, out, to_next, to_pair, *, height, units):
+    channels = columns.shape[0] - units
     top, bottom = in_order(from_next, from_pair, NS[-1])
     tile = columns[:channels]
-    pairs = columns[channels : channels + units]
-    single = columns[channels + units :]
+    states = columns[channels:]
     for rows, place, state_place in ((top, 0, 0), (bottom, height + 2, height + 1)):
         for i in range(2):
             tile = put_channels(tile, rows[i * channels : (i + 1) * channels], place + i)
-        states = [rows[2 * channels + i * units : 2 * channels + (i + 1) * units] for i in range(3)]
-        pairs = put_state(pairs, states[0], state_place, 0)
-        pairs = put_state(pairs, states[1], state_place, 2)
-        single = put_state(single, states[2], state_place, 0)
-    whole = jnp.concatenate([tile, pairs, single], 0)
-    out[...] = whole
-    spare = jnp.zeros((sent.shape[0] - out.shape[0], LANES), F32)
-    sent[...] = jnp.concatenate([whole, spare], 0).astype(BF16)
+        for i in range(3):
+            start = 2 * channels + i * units
+            states = put_state(states, rows[start : start + units], state_place, 2 * i)
+    out[:channels] = tile
+    out[channels:] = states
+    slot = lax.broadcasted_iota(jnp.int32, (channels, LANES), 1) % STEP
+    blank = jnp.zeros((channels - units, LANES), F32)
+    east = [jnp.concatenate([moved(states, k), blank], 0) for k in (2, 1, 0)]
+    west = [jnp.concatenate([moved(states, k), blank], 0) for k in (1, 0, -1)]
+    east = by_slot(slot, tile, tile, *east)
+    west = by_slot(slot, moved(tile, -2), moved(tile, -2), *west)
+    spare = jnp.zeros((to_pair.shape[0] - channels, LANES), F32)
+    first = lax.axis_index(EW[-1]) == 0
+    to_pair[...] = jnp.concatenate([jnp.where(first, east, west), spare], 0).astype(BF16)
+    to_next[...] = jnp.concatenate([jnp.where(first, west, east), spare], 0).astype(BF16)
 
 
 def gate_step(gates, old, down, grad_cell):
@@ -151,10 +160,15 @@
 
 
 def forward_kernel(
-    stacked, from_next, from_pair, weights, bias, cell_prev, grad_hidden, grad_cell,
-    hidden, cell, grad_cell_prev, grads, terms,
+    stacked, from_next, from_pair, kernel, bias, cell_prev, grad_hidden, grad_cell,
+    hidden, cell, grad_cell_prev, grads, terms, weights,
     hidden_rows, hidden_here, cell_here, back_here, sems,
 ):
+    depth = kernel.shape[0] // 3
+    blank = jnp.zeros((STACK - depth, kernel.shape[1]), F32)
+    for row_off in range(3):
+        part = kernel[...].astype(F32)[row_off * depth : (row_off + 1) * depth]
+        weights[:, row_off * STACK : (row_off + 1) * STACK] = jnp.concatenate([part, blank], 0).T.astype(BF16)
     units = bias.shape[0] // 4
     height = cell_prev.shape[0] // units
     channels = (from_pair.shape[0] - 3 * units) // 2
@@ -233,27 +247,20 @@
     columns, from_next, from_pair, weights, bias, inner_terms, side_grads, side_cells, terms, *, height
 ):
     units = bias.shape[0] // 4
-    channels = columns.shape[0] - 2 * units
+    channels = columns.shape[0] - units
     spare = STACK - 3 * channels
-    left, right = in_order(from_next, from_pair, EW[-1])
-
-    def moved(x, lanes):
-        return pltpu.roll(x, lanes % LANES, 1)
-
-    slot = lax.broadcasted_iota(jnp.int32, (channels, LANES), 1) % 4
+    west, east = in_order(from_next, from_pair, EW[-1])
+    west, east = west[:channels], east[:channels]
+    slot = lax.broadcasted_iota(jnp.int32, (channels, LANES), 1) % STEP
     own = columns[:channels]
-    outer = jnp.where(slot < 2, left[:channels], right[:channels])
-    before = jnp.where(
-        slot == 0, outer, jnp.where(slot == 1, moved(own, 1), jnp.where(slot == 2, moved(outer, 1), moved(own, 2)))
-    )
-    at = jnp.where(slot == 0, moved(outer, -1), jnp.where(slot == 3, moved(outer, 1), own))
-    after = jnp.where(
-        slot == 0, moved(own, -2), jnp.where(slot == 1, moved(outer, -1), jnp.where(slot == 2, moved(own, -1), outer))
-    )
+    outer = jnp.where(slot < 2, west, moved(east, 2))
+    before = by_slot(slot, outer, moved(own, 1), moved(outer, 1), moved(own, 2))
+    at = by_slot(slot, moved(outer, -1), own, own, moved(outer, 1))
+    after = by_slot(slot, moved(own, -2), moved(outer, -1), moved(own, -1), outer)
     patches = jnp.concatenate([before, at, after], 0)
     ones_row = (lax.broadcasted_iota(jnp.int32, (spare, LANES), 0) == 0).astype(F32)
     stacks = [
-        jnp.concatenate([moved(patches, -4 * row_off) if row_off else patches, ones_row], 0).astype(BF16)
+        jnp.concatenate([moved(patches, -STEP * row_off), ones_row], 0).astype(BF16)
         for row_off in range(3)
     ]
     gates = jnp.broadcast_to(bias[...], (4 * units, LANES))
@@ -262,20 +269,18 @@
             weights[:, row_off * STACK : (row_off + 1) * STACK], stacks[row_off], preferred_element_type=F32
         )
     slot = slot[:units]
-    rows = slice(channels, channels + units)
-    here, west, east = columns[rows], left[rows], right[rows]
-    old = jnp.where(slot == 0, west, jnp.where(slot == 3, moved(east, 2), moved(here, 1)))
-    down = jnp.where(slot == 0, moved(west, -2), jnp.where(slot == 3, east, moved(here, -1)))
-    rows = slice(channels + units, channels + 2 * units)
-    here, west, east = columns[rows], left[rows], right[rows]
-    grad_cell = jnp.where(slot == 0, west, jnp.where(slot == 3, moved(east, 2), moved(here, 1)))
+    here, west, east = columns[channels:], west[:units], east[:units]
+    old = by_slot(slot, moved(west, -2), moved(here, 1), moved(here, 1), moved(east, 1))
+    down = by_slot(slot, moved(west, -3), moved(here, -1), moved(here, -1), east)
+    grad_cell = by_slot(slot, moved(west, -4), moved(here, -3), moved(here, -3), moved(east, -1))
     new_hidden, new, back, grads = gate_step(gates, old, down, grad_cell)
     side_cells[:units] = new_hidden
     side_cells[units : 2 * units] = new
     side_cells[2 * units :] = back
     side_grads[...] = grads.astype(BF16)
     lane = lax.broadcasted_iota(jnp.int32, grads.shape, 1)
-    inside = (lane >= 4) & (lane < 4 * (height + 1)) & ((lane % 4 == 1) | (lane % 4 == 2))
+    slot = lane % STEP
+    inside = (lane >= STEP) & (lane < STEP * (height + 1)) & ((slot == 1) | (slot == 2))
     grads = jnp.where(inside, grads, 0.0).astype(BF16)
     for row_off in range(3):
         part = slice(row_off * STACK, (row_off + 1) * STACK)
@@ -302,7 +307,7 @@
     for n in range(height):
         at = pl.ds(n, units, stride=height)
         for i, (inner, out) in enumerate(((rows, rows), (inner_cell, cell), (inner_back, grad_cell_prev))):
-            side = pltpu.roll(side_cells[i * units : (i + 1) * units], LANES - 4 * (n + 1) - 2, 1)
+            side = pltpu.roll(side_cells[i * units : (i + 1) * units], LANES - STEP * (n + 1) - 2, 1)
             out[at, :] = jnp.where(ends, side, inner[at, :])
     hidden[...] = rows[: units * height].astype(BF16)
 
@@ -313,9 +318,9 @@
         for row_off in range(3):
             start = (3 * row_off + col_off) * channels
             piece = outer[start : start + channels]
-            part = part + (pltpu.roll(piece, LANES - 4 * (2 - row_off), 1) if row_off < 2 else piece)
+            part = part + moved(piece, -STEP * (2 - row_off))
         parts.append(part)
-    slot = lane % 4
+    slot = lane % STEP
     sides = jnp.where((slot == 1) | (slot == 2), parts[1], 0.0) + jnp.where(
         slot == 0,
         pltpu.roll(parts[0], LANES - 1, 1),
@@ -343,7 +348,7 @@
     edge = (lane < 2) | (lane >= LANES - 2)
     for n in range(height):
         total = sums[n, 1] + pltpu.roll(sums[n, 0], LANES - 1, 1) + pltpu.roll(sums[n, 2], 1, 1)
-        total = total + jnp.where(edge, pltpu.roll(sides, LANES - 4 * n - 2, 1), 0.0)
+        total = total + jnp.where(edge, moved(sides, -STEP * n - 2), 0.0)
         rows[pl.ds(n, channels, stride=height), :] = total
     grad_frame[...] = rows[: inputs * height].astype(BF16)
     grad_hidden_prev[...] = rows[inputs * height :].astype(BF16)
@@ -424,25 +429,24 @@
         compiler_params=pltpu.CompilerParams(vmem_limit_bytes=60 * 2**20),
         cost_estimate=pl.CostEstimate(flops=1_000_000, bytes_accessed=1_000_000, transcendentals=0),
     )(*arrays)
-    edge = shape(channels + 2 * units, LANES, F32)
-    columns, weights, stacked = called(
+    edge = shape(channels + units, LANES, F32)
+    columns, stacked = called(
         functools.partial(columns_kernel, height=height),
-        [edge, shape(gate_rows, 3 * STACK, BF16), shape(STACK, height * breadth, BF16)],
+        [edge, shape(STACK, height * breadth, BF16)],
         [pltpu.VMEM(channel_rows, F32)],
         1_000_000,
         *blocks,
-        kernel.T,
     )
     rows = swapped(to_pair, to_next, NS)
-    sent = shape(-(-(channels + 2 * units) // 16) * 16, LANES, BF16)
-    columns, sent = called(
-        functools.partial(corners_kernel, height=height, units=units), [edge, sent], [], 100_000, columns, *rows
-    )
-    sides = swapped(sent, sent, EW)
+    sent = shape(-(-channels // 16) * 16, LANES, BF16)
+    columns, to_next, to_pair = called(
+        functools.partial(corners_kernel, height=height, units=units), [edge, sent, sent], [], 100_000, columns, *rows
+    )
+    sides = swapped(to_pair, to_next, EW)
     bias = bias[:, None]
     field = shape(*flat, F32)
     cube = jax.ShapeDtypeStruct((units, height, breadth), F32)
-    inner_hidden, inner_cell, inner_back, grads, inner_terms = pl.pallas_call(
+    inner_hidden, inner_cell, inner_back, grads, inner_terms, weights = pl.pallas_call(
         forward_kernel,
         out_shape=(
             shape(*flat, BF16),
@@ -450,9 +454,10 @@
             cube,
             shape(gate_rows, (height + 2) * breadth, BF16),
             shape(3 * STACK, gate_rows, F32),
+            shape(gate_rows, 3 * STACK, BF16),
         ),
         in_specs=vmem(8),
-        out_specs=tuple([pl.BlockSpec(memory_space=pl.ANY)] * 3 + vmem(2)),
+        out_specs=tuple([pl.BlockSpec(memory_space=pl.ANY)] * 3 + vmem(3)),
         scratch_shapes=[
             pltpu.VMEM(flat, F32),
             pltpu.VMEM(flat, BF16),
@@ -462,7 +467,7 @@
         ],
         compiler_params=pltpu.CompilerParams(vmem_limit_bytes=16 * 2**20),
         cost_estimate=pl.CostEstimate(flops=1_400_000_000, bytes_accessed=4_000_000, transcendentals=700_000),
-    )(stacked, *rows, weights, bias, *states)
+    )(stacked, *rows, kernel.T, bias, *states)
     side_grads, side_cells, terms = called(
         functools.partial(sides_kernel, height=height),
         [shape(gate_rows, LANES, BF16), shape(3 * units, LANES, F32), shape(3 * STACK, gate_rows, BF16)],

time: 94.6 us -> 94.3 us (level)
  no operation moved by 1% of the time
where the time goes in v8:
time: 94.3 us; the launch traced here: 93.9 us
  blocking collectives  50.9 us (54%)
  starting transfers between devices  22.2 us (24%)
  Pallas kernels  14 us (15%)
  waiting for transfers between devices  5.69 us (6%)
    all_to_all x3, blocking collectives, exchanged(): return lax.all_to_all(copies, axes, 0, 0, tiled=True)  50.9 us
    ppermute x2, starting transfers between devices, swapped(): return (other, lax.ppermute(to_pair, axes, pairs))  9.58 us
    pallas_call x5, Pallas kernels, called(): pl.pallas_call(kernel, out_shape=tuple(outs), in_specs=vmem(len(args)), o...  7.59 us
    all_to_all x1, starting transfers between devices, exchanged(): return lax.all_to_all(copies, axes, 0, 0, tiled=True)  7.36 us
    all_to_all x1, waiting for transfers between devices, exchanged(): return lax.all_to_all(copies, axes, 0, 0, tiled=True)  5.68 us
    ppermute x2, starting transfers between devices, swapped(): other = lax.ppermute(to_next, axes, across)  5.3 us
    pallas_call x1, Pallas kernels, per_device(): pl.pallas_call(forward_kernel, out_shape=(shape(*flat, BF16), cube, cube,...  3.66 us
    pallas_call x1, Pallas kernels, per_device(): pl.pallas_call(rows_kernel, out_shape=(strip, strip), in_specs=[pl.BlockS...  1.93 us
  transfers between devices with their start and end apart: 5, of which 1 were waited for; matrix products, arithmetic and copies ran while one was open for 0% of the time, Pallas kernels for 10%

profile of v8, /device:TPU:1, one launch (start us, length us, event | category | flops | bytes accessed | tf_op | source)
XLA Modules:
  0.0 93.9 jit_solution(476870312314391182)
XLA Ops:
  0.6 0.0 copy-start
  0.6 0.0 copy-start.1
  0.7 0.0 copy-start.2
  0.7 0.0 copy-start.5
  0.7 0.0 copy-start.3
  0.7 0.0 copy-start.6
  0.7 1.9 %shard_map.127 = (bf16[336,128]{1,0:T(8,128)(2,1)}, bf16[336,128]{1,0:T(8,128)(2,1)}) custom-call(bf16[8,16,128]{2,1,0:T(8,128)(2,1)} %frame.1, bf16[64,16,128]{2,1,0:T(8,128)(2,1)} %hidden_prev.1, f32[64,16,128]{2,1,0:T(8,128)} %cell_prev.1, f32[64,16,128]{2,1,0:T(8,128)} %grad_hidden.1, f32[64,16,128]{2,1,0:T(8,128)} %grad_cell.1), custom_call_target="tpu_custom_call" | custom-call | flops 1000000 | bytes 1000000 | tf_op jit(solution)/shard_map/pallas_call | solution.py:417
  2.6 0.0 copy-start.4
  2.6 4.6 %collective-permute-start = (bf16[336,128]{1,0:T(8,128)(2,1)}, bf16[336,128]{1,0:T(8,128)(2,1)S(1)}, u32[]{:S(2)}, u32[]{:S(2)}) collective-permute-start(bf16[336,128]{1,0:T(8,128)(2,1)} %get-tuple-element.31), channel_id=1, source_target_pairs={{1,2},{2,1},{3,4},{4,3},{5,6},{6,5},{7,8},{8,7},{9,10},{10,9},{11,... | collective-permute-start | bytes 258056 | tf_op jit(solution)/shard_map/ppermute | solution.py:29
  7.3 4.9 %collective-permute-start.1 = (bf16[336,128]{1,0:T(8,128)(2,1)}, bf16[336,128]{1,0:T(8,128)(2,1)S(1)}, u32[]{:S(2)}, u32[]{:S(2)}) collective-permute-start(bf16[336,128]{1,0:T(8,128)(2,1)} %get-tuple-element.32), channel_id=1, source_target_pairs={{0,1},{1,0},{2,3},{3,2},{4,5},{5,4},{6,7},{7,6},{8,9},{9,8},{10,11... | collective-permute-start | bytes 258056 | tf_op jit(solution)/shard_map/ppermute | solution.py:30
  12.2 0.0 copy-done.6
  12.3 0.1 copy.17.bias
  12.4 0.0 copy-done
  12.4 0.0 copy-done.1
  12.4 0.0 copy-done.2
  12.4 0.0 copy-done.5
  12.4 0.0 copy-done.3
  12.4 1.0 %shard_map.126 = (f32[136,128]{1,0:T(8,128)S(1)}, bf16[256,2048]{1,0:T(8,128)(2,1)S(1)}) custom-call(bf16[128,128]{1,0:T(8,128)(2,1)S(1)} %bitcast.29, bf16[1024,128]{1,0:T(8,128)(2,1)S(1)} %bitcast.25, f32[1024,128]{1,0:T(8,128)S(1)} %bitcast.18, f32[1024,128]{1,0:T(8,128)S(1)} %bitcast.20, f32[1024,128]{1,0:T(8,128)S(1)} %bitcast.22), custom_call_target="tpu_custom_call" | custom-call | flops 1000000 | bytes 2000 | tf_op jit(solution)/shard_map/pallas_call | solution.py:393
  13.5 0.0 collective-permute-done.from_next
  13.5 0.0 collective-permute-done.1.from_pair
  13.5 0.2 shard_map.129
  13.7 0.7 collective-permute-start.2
  14.4 4.6 %collective-permute-start.3 = (bf16[80,128]{1,0:T(8,128)(2,1)S(1)}, bf16[80,128]{1,0:T(8,128)(2,1)S(1)}, u32[]{:S(2)}, u32[]{:S(2)}) collective-permute-start(bf16[80,128]{1,0:T(8,128)(2,1)S(1)} %get-tuple-element.37), channel_id=1, source_target_pairs={{0,16},{16,0},{32,48},{48,32},{64,80},{80,64},{96,112},{112,96},{1... | collective-permute-start | bytes 61448 | tf_op jit(solution)/shard_map/ppermute | solution.py:30
  19.1 0.0 copy-done.4
  19.1 3.7 %shard_map.128 = (bf16[1024,128]{1,0:T(8,128)(2,1)}, f32[64,16,128]{2,1,0:T(8,128)}, f32[64,16,128]{2,1,0:T(8,128)}, bf16[256,2304]{1,0:T(8,128)(2,1)S(1)}, f32[...) custom-call(bf16[256,2048]{1,0:T(8,128)(2,1)S(1)} %get-tuple-element.30.stacked, ...), custom_call_target="tpu_custom_call" | custom-call | flops 1400000000 | bytes 4000000 | tf_op jit(solution)/shard_map/pallas_call | solution.py:449
  22.7 0.0 collective-permute-done.2.from_next
  22.7 0.0 collective-permute-done.3.from_pair
  22.8 0.9 shard_map.130
  23.6 16.9 %all_to_all.20.parts = bf16[32,24,256]{2,1,0:T(8,128)(2,1)S(1)} all-to-all(bf16[32,24,256]{2,1,0:T(8,128)(2,1)S(1)} %bitcast.26), channel_id=1, replica_groups=mesh['z_hi'=4,'z_lo'=4,'x_hi'=2,'y'=4,'x_lo'=2,'core'=2] {'x_hi','y','x_..., dimensions={0} | all-to-all | bytes 786432 | tf_op jit(solution)/shard_map/all_to_all | solution.py:385
  40.5 0.1 shard_map.132
  40.6 11.4 %all_to_all.21.parts = f32[4,24,256]{2,1,0:T(8,128)S(1)} all-to-all(f32[4,24,256]{2,1,0:T(8,128)S(1)} %shard_map.132), channel_id=1, replica_groups=mesh['z_hi'=4,'z_lo'=4,'x_hi'=2,'y'=4,'x_lo'=2,'core'=2] {'z_lo'}, dimensions={0} | all-to-all | bytes 196608 | tf_op jit(solution)/shard_map/all_to_all | solution.py:385
  52.0 22.6 %all_to_all.22.parts = f32[4,24,256]{2,1,0:T(8,128)S(1)} all-to-all(f32[4,24,256]{2,1,0:T(8,128)S(1)} %shard_map.133), channel_id=1, replica_groups=mesh['z_hi'=4,'z_lo'=4,'x_hi'=2,'y'=4,'x_lo'=2,'core'=2] {'z_hi'}, dimensions={0} | all-to-all | bytes 196608 | tf_op jit(solution)/shard_map/all_to_all | solution.py:385
  74.6 0.8 shard_map.134
  75.4 7.4 %all-to-all-start.3 = ((bf16[32,24,256]{2,1,0:T(8,128)(2,1)}), bf16[32,24,256]{2,1,0:T(8,128)(2,1)S(1)}, u32[]{:S(2)}, u32[]{:S(2)}) async-start(bf16[32,24,256]{2,1,0:T(8,128)(2,1)} %shard_map.134), calls=%async_computation.3 | async-start | bytes 786432 | tf_op jit(solution)/shard_map/all_to_all | solution.py:385
  82.8 4.3 %shard_map.131 = (bf16[1024,128]{1,0:T(8,128)(2,1)}, f32[1024,128]{1,0:T(8,128)}, f32[1024,128]{1,0:T(8,128)}, bf16[128,128]{1,0:T(8,128)(2,1)}, bf16[1024,128]{1,0:T(8,128)(2,1)}) custom-call(bf16[648,256]{1,0:T(8,128)(2,1)S(1)} %bitcast.28, ...), custom_call_target="tpu_custom_call", output_to_operand_aliasing={{0}: (4, {}), {1}: (5, {}), {2}: (6, {})} | custom-call | flops 764000000 | bytes 1528000 | tf_op jit(solution)/shard_map/pallas_call | solution.py:393
  87.1 5.7 %all-to-all-done.3 = bf16[32,24,256]{2,1,0:T(8,128)(2,1)S(1)} async-done(((bf16[32,24,256]{2,1,0:T(8,128)(2,1)}), bf16[32,24,256]{2,1,0:T(8,128)(2,1)S(1)}, u32[]{:S(2)}, u32[]{:S(2)}) %all-to-all-start.3) | async-done | bytes 393248 | tf_op jit(solution)/shard_map/all_to_all | solution.py:385
  92.7 1.2 %shard_map.135 = (f32[648,256]{1,0:T(8,128)}, f32[1,256]{1,0:T(1,128)}) custom-call(bf16[768,256]{1,0:T(8,128)(2,1)S(1)} %bitcast.24), custom_call_target="tpu_custom_call" | custom-call | flops 1000000 | bytes 2000 | tf_op jit(solution)/shard_map/pallas_call | solution.py:393
  (1 shorter events, 0.0 us)
Async XLA Ops:
  0.6 11.8 %copy-start = (f32[64,16,128]{2,1,0:T(8,128)S(1)}, f32[64,16,128]{2,1,0:T(8,128)}, u32[]{:S(2)}) copy-start(f32[64,16,128]{2,1,0:T(8,128)} %cell_prev.1) | copy-start | bytes 1572868
  0.6 11.8 %copy-start.1 = (f32[64,16,128]{2,1,0:T(8,128)S(1)}, f32[64,16,128]{2,1,0:T(8,128)}, u32[]{:S(2)}) copy-start(f32[64,16,128]{2,1,0:T(8,128)} %grad_hidden.1) | copy-start | bytes 1572868
  0.7 11.8 %copy-start.2 = (f32[64,16,128]{2,1,0:T(8,128)S(1)}, f32[64,16,128]{2,1,0:T(8,128)}, u32[]{:S(2)}) copy-start(f32[64,16,128]{2,1,0:T(8,128)} %grad_cell.1) | copy-start | bytes 1572868
  0.7 11.8 %copy-start.5 = (bf16[8,16,128]{2,1,0:T(8,128)(2,1)S(1)}, bf16[8,16,128]{2,1,0:T(8,128)(2,1)}, u32[]{:S(2)}) copy-start(bf16[8,16,128]{2,1,0:T(8,128)(2,1)} %frame.1) | copy-start | bytes 98308
  0.7 11.8 %copy-start.3 = (bf16[64,16,128]{2,1,0:T(8,128)(2,1)S(1)}, bf16[64,16,128]{2,1,0:T(8,128)(2,1)}, u32[]{:S(2)}) copy-start(bf16[64,16,128]{2,1,0:T(8,128)(2,1)} %hidden_prev.1) | copy-start | bytes 786436
  0.7 11.6 %copy-start.6 = (f32[256]{0:T(256)S(1)}, f32[256]{0:T(256)}, u32[]{:S(2)}) copy-start(f32[256]{0:T(256)} %param.11) | copy-start | bytes 3076
  2.6 16.4 %copy-start.4 = (bf16[256,648]{0,1:T(8,128)(2,1)S(1)}, bf16[256,648]{0,1:T(8,128)(2,1)}, u32[]{:S(2)}) copy-start(bf16[256,648]{0,1:T(8,128)(2,1)} %param.10) | copy-start | bytes 995332
  2.6 10.9 %collective-permute-start = (bf16[336,128]{1,0:T(8,128)(2,1)}, bf16[336,128]{1,0:T(8,128)(2,1)S(1)}, u32[]{:S(2)}, u32[]{:S(2)}) collective-permute-start(bf16[336,128]{1,0:T(8,128)(2,1)} %get-tuple-element.31), channel_id=1, source_target_pairs={{1,2},{2,1},{3,4},{4,3},{5,6},{6,5},{7,8},{8,7},{9,10},{10,9},{11,... | collective-permute-start | bytes 258056 | tf_op jit(solution)/shard_map/ppermute | solution.py:29
  7.3 6.2 %collective-permute-start.1 = (bf16[336,128]{1,0:T(8,128)(2,1)}, bf16[336,128]{1,0:T(8,128)(2,1)S(1)}, u32[]{:S(2)}, u32[]{:S(2)}) collective-permute-start(bf16[336,128]{1,0:T(8,128)(2,1)} %get-tuple-element.32), channel_id=1, source_target_pairs={{0,1},{1,0},{2,3},{3,2},{4,5},{5,4},{6,7},{7,6},{8,9},{9,8},{10,11... | collective-permute-start | bytes 258056 | tf_op jit(solution)/shard_map/ppermute | solution.py:30
  13.7 9.0 %collective-permute-start.2 = (bf16[80,128]{1,0:T(8,128)(2,1)S(1)}, bf16[80,128]{1,0:T(8,128)(2,1)S(1)}, u32[]{:S(2)}, u32[]{:S(2)}) collective-permute-start(bf16[80,128]{1,0:T(8,128)(2,1)S(1)} %get-tuple-element.36), channel_id=1, source_target_pairs={{16,32},{32,16},{48,64},{64,48},{80,96},{96,80},{112,128},{128,112... | collective-permute-start | bytes 61448 | tf_op jit(solution)/shard_map/ppermute | solution.py:29
  14.4 8.3 %collective-permute-start.3 = (bf16[80,128]{1,0:T(8,128)(2,1)S(1)}, bf16[80,128]{1,0:T(8,128)(2,1)S(1)}, u32[]{:S(2)}, u32[]{:S(2)}) collective-permute-start(bf16[80,128]{1,0:T(8,128)(2,1)S(1)} %get-tuple-element.37), channel_id=1, source_target_pairs={{0,16},{16,0},{32,48},{48,32},{64,80},{80,64},{96,112},{112,96},{1... | collective-permute-start | bytes 61448 | tf_op jit(solution)/shard_map/ppermute | solution.py:30
  75.4 17.3 %all-to-all-start.3 = ((bf16[32,24,256]{2,1,0:T(8,128)(2,1)}), bf16[32,24,256]{2,1,0:T(8,128)(2,1)S(1)}, u32[]{:S(2)}, u32[]{:S(2)}) async-start(bf16[32,24,256]{2,1,0:T(8,128)(2,1)} %shard_map.134), calls=%async_computation.3 | async-start | bytes 786432 | tf_op jit(solution)/shard_map/all_to_all | solution.py:385

commit v9 on v8

--- a/solution.py
+++ b/solution.py
@@ -283,13 +283,12 @@
     inside = (lane >= STEP) & (lane < STEP * (height + 1)) & ((slot == 1) | (slot == 2))
     grads = jnp.where(inside, grads, 0.0).astype(BF16)
     for row_off in range(3):
-        part = slice(row_off * STACK, (row_off + 1) * STACK)
-        terms[part] = (
-            inner_terms[part]
-            + lax.dot_general(
-                stacks[row_off], grads, (((1,), (1,)), ((), ())), preferred_element_type=F32
-            )
-        ).astype(BF16)
+        total = inner_terms[row_off * STACK : (row_off + 1) * STACK] + lax.dot_general(
+            stacks[row_off], grads, (((1,), (1,)), ((), ())), preferred_element_type=F32
+        )
+        for half in range(2):
+            start = (3 * half + row_off) * STACK
+            terms[start : start + STACK] = total[:, half * LANES : (half + 1) * LANES].astype(BF16)
 
 
 def backward_kernel(
@@ -354,31 +353,67 @@
     grad_hidden_prev[...] = rows[inputs * height :].astype(BF16)
 
 
-def finish_kernel(total, kernel_step, bias_step):
+def finish_kernel(total, kernel_step, bias_step, scaled, sems):
     block = kernel_step.shape[0] // 3
-    parts = [total[i * STACK : i * STACK + block].astype(F32) for i in range(3)]
-    bias_grad = total[block : block + 8].astype(F32)[:1]
+    halves = [total[half * 3 * STACK : (half + 1) * 3 * STACK].astype(F32) for half in range(2)]
+    whole = jnp.concatenate(halves, 1)
+    parts = [whole[i * STACK : i * STACK + block] for i in range(3)]
+    bias_grad = whole[block : block + 1]
     norm = jnp.sqrt(sum(jnp.sum(part * part) for part in parts) + jnp.sum(bias_grad * bias_grad))
     factor = jnp.minimum(1.0, CLIP_NORM / norm)
+    copies = []
     for i, part in enumerate(parts):
-        kernel_step[i * block : (i + 1) * block] = part * factor
+        rows = pl.ds(i * block, block)
+        scaled[rows] = part * factor
+        copies.append(pltpu.make_async_copy(scaled.at[rows], kernel_step.at[rows], sems.at[i]))
+        copies[-1].start()
     bias_step[...] = bias_grad * factor
-
-
-def sum_kernel(parts, *rest):
-    copies = rest[-1]
+    for copy in copies:
+        copy.wait()
+
+
+def sum_kernel(parts, copies):
     total = jnp.sum(parts[...].astype(F32), 0).astype(copies.dtype)
     copies[...] = jnp.broadcast_to(total[None], copies.shape)
 
 
-def summed(parts, copies, kind, *after):
+def summed(parts, copies, kind):
     return pl.pallas_call(
         sum_kernel,
         out_shape=jax.ShapeDtypeStruct((copies,) + parts.shape[1:], kind),
-        in_specs=vmem(1) + [pl.BlockSpec(memory_space=pl.ANY)] * len(after),
+        in_specs=vmem(1),
         out_specs=vmem(1)[0],
         compiler_params=pltpu.CompilerParams(vmem_limit_bytes=8 * 2**20),
-    )(parts, *after)
+    )(parts)
+
+
+def spread_kernel(parts, copies, few, sems):
+    total = jnp.sum(parts[...], 0).astype(few.dtype)
+    few[...] = jnp.broadcast_to(total[None], few.shape)
+    count = few.shape[0]
+    moves = [
+        pltpu.make_async_copy(few, copies.at[pl.ds(i * count, count)], sems.at[i])
+        for i in range(copies.shape[0] // count)
+    ]
+    for move in moves:
+        move.start()
+    for move in moves:
+        move.wait()
+
+
+def spread(parts, copies, kind):
+    few = max(copies // 8, 1)
+    return pl.pallas_call(
+        spread_kernel,
+        out_shape=jax.ShapeDtypeStruct((copies,) + parts.shape[1:], kind),
+        in_specs=vmem(1),
+        out_specs=pl.BlockSpec(memory_space=pl.ANY),
+        scratch_shapes=[
+            pltpu.VMEM((few,) + parts.shape[1:], kind),
+            pltpu.SemaphoreType.DMA((copies // few,)),
+        ],
+        compiler_params=pltpu.CompilerParams(vmem_limit_bytes=8 * 2**20),
+    )(parts)
 
 
 def exchanged(copies, axes):
@@ -470,7 +505,7 @@
     )(stacked, *rows, kernel.T, bias, *states)
     side_grads, side_cells, terms = called(
         functools.partial(sides_kernel, height=height),
-        [shape(gate_rows, LANES, BF16), shape(3 * units, LANES, F32), shape(3 * STACK, gate_rows, BF16)],
+        [shape(gate_rows, LANES, BF16), shape(3 * units, LANES, F32), shape(6 * STACK, LANES, BF16)],
         [],
         100_000_000,
         columns,
@@ -482,11 +517,11 @@
 
     plane = lax.axis_size(PLANE)
     low, high = lax.axis_size("z_lo"), lax.axis_size("z_hi")
-    mine = exchanged(terms.reshape(plane, -1, gate_rows), PLANE)
+    mine = exchanged(terms.reshape(plane, -1, LANES), PLANE)
     mine = exchanged(summed(mine, low, F32), "z_lo")
     mine = exchanged(summed(mine, high, F32), "z_hi")
-    mine = summed(mine, plane, BF16)
-    total = exchanged(mine, PLANE).reshape(3 * STACK, gate_rows)
+    mine = spread(mine, plane, BF16)
+    total = exchanged(mine, PLANE).reshape(6 * STACK, LANES)
     hidden, cell, grad_cell_prev, grad_frame, grad_hidden_prev = called(
         backward_kernel,
         [shape(*flat, BF16), field, field, shape(inputs * height, breadth, BF16), shape(*flat, BF16)],
@@ -501,9 +536,14 @@
         inner_back.reshape(flat),
         aliases={4: 0, 5: 1, 6: 2},
     )
-    kernel_step, bias_step = called(
-        finish_kernel, [shape(9 * channels, gate_rows, F32), shape(1, gate_rows, F32)], [], 1_000_000, total
-    )
+    kernel_step, bias_step = pl.pallas_call(
+        finish_kernel,
+        out_shape=(shape(9 * channels, gate_rows, F32), shape(1, gate_rows, F32)),
+        in_specs=vmem(1),
+        out_specs=(pl.BlockSpec(memory_space=pl.ANY), vmem(1)[0]),
+        scratch_shapes=[pltpu.VMEM((9 * channels, gate_rows), F32), pltpu.SemaphoreType.DMA((3,))],
+        compiler_params=pltpu.CompilerParams(vmem_limit_bytes=8 * 2**20),
+    )(total)
     whole = (units, height, breadth)
     return (
         hidden.reshape(whole),

time: 94.3 us -> 94.9 us (level)
    pallas_call x0 -> x2, Pallas kernels: none -> 2.54 us  [the longest x1 1.73 us: per_device(): pl.pallas_call(finish_kernel, out_shape=(shape(9 * channels, gate_rows, F...]
    pallas_call x5 -> x4, Pallas kernels: 7.59 us -> 6.4 us  [called(): pl.pallas_call(kernel, out_shape=tuple(outs), in_specs=vmem(len(args)), o...]
where the time goes in v9:
time: 94.9 us; the launch traced here: 94.5 us
  blocking collectives  50.9 us (54%)
  starting transfers between devices  22.3 us (23%)
  Pallas kernels  14.6 us (15%)
  waiting for transfers between devices  5.7 us (6%)
    all_to_all x3, blocking collectives, exchanged(): return lax.all_to_all(copies, axes, 0, 0, tiled=True)  50.9 us
    ppermute x2, starting transfers between devices, swapped(): return (other, lax.ppermute(to_pair, axes, pairs))  9.58 us
    all_to_all x1, starting transfers between devices, exchanged(): return lax.all_to_all(copies, axes, 0, 0, tiled=True)  7.38 us
    pallas_call x4, Pallas kernels, called(): pl.pallas_call(kernel, out_shape=tuple(outs), in_specs=vmem(len(args)), o...  6.4 us
    all_to_all x1, waiting for transfers between devices, exchanged(): return lax.all_to_all(copies, axes, 0, 0, tiled=True)  5.69 us
    ppermute x2, starting transfers between devices, swapped(): other = lax.ppermute(to_next, axes, across)  5.3 us
    pallas_call x1, Pallas kernels, per_device(): pl.pallas_call(forward_kernel, out_shape=(shape(*flat, BF16), cube, cube,...  3.66 us
    pallas_call x1, Pallas kernels, per_device(): pl.pallas_call(rows_kernel, out_shape=(strip, strip), in_specs=[pl.BlockS...  1.93 us
  transfers between devices with their start and end apart: 5, of which 1 were waited for; matrix products, arithmetic and copies ran while one was open for 0% of the time, Pallas kernels for 10%

profile of v9, /device:TPU:1, one launch (start us, length us, event | category | flops | bytes accessed | tf_op | source)
XLA Modules:
  0.0 94.5 jit_solution(4091895820902711838)
XLA Ops:
  0.6 0.0 copy-start
  0.6 0.0 copy-start.1
  0.7 0.0 copy-start.2
  0.7 0.0 copy-start.5
  0.7 0.0 copy-start.3
  0.7 0.0 copy-start.6
  0.7 1.9 %shard_map.127 = (bf16[336,128]{1,0:T(8,128)(2,1)}, bf16[336,128]{1,0:T(8,128)(2,1)}) custom-call(bf16[8,16,128]{2,1,0:T(8,128)(2,1)} %frame.1, bf16[64,16,128]{2,1,0:T(8,128)(2,1)} %hidden_prev.1, f32[64,16,128]{2,1,0:T(8,128)} %cell_prev.1, f32[64,16,128]{2,1,0:T(8,128)} %grad_hidden.1, f32[64,16,128]{2,1,0:T(8,128)} %grad_cell.1), custom_call_target="tpu_custom_call" | custom-call | flops 1000000 | bytes 1000000 | tf_op jit(solution)/shard_map/pallas_call | solution.py:452
  2.6 0.0 copy-start.4
  2.6 4.6 %collective-permute-start = (bf16[336,128]{1,0:T(8,128)(2,1)}, bf16[336,128]{1,0:T(8,128)(2,1)S(1)}, u32[]{:S(2)}, u32[]{:S(2)}) collective-permute-start(bf16[336,128]{1,0:T(8,128)(2,1)} %get-tuple-element.31), channel_id=1, source_target_pairs={{1,2},{2,1},{3,4},{4,3},{5,6},{6,5},{7,8},{8,7},{9,10},{10,9},{11,... | collective-permute-start | bytes 258056 | tf_op jit(solution)/shard_map/ppermute | solution.py:29
  7.3 4.9 %collective-permute-start.1 = (bf16[336,128]{1,0:T(8,128)(2,1)}, bf16[336,128]{1,0:T(8,128)(2,1)S(1)}, u32[]{:S(2)}, u32[]{:S(2)}) collective-permute-start(bf16[336,128]{1,0:T(8,128)(2,1)} %get-tuple-element.32), channel_id=1, source_target_pairs={{0,1},{1,0},{2,3},{3,2},{4,5},{5,4},{6,7},{7,6},{8,9},{9,8},{10,11... | collective-permute-start | bytes 258056 | tf_op jit(solution)/shard_map/ppermute | solution.py:30
  12.2 0.0 copy-done.6
  12.3 0.1 copy.17.bias
  12.4 0.0 copy-done
  12.4 0.0 copy-done.1
  12.4 0.0 copy-done.2
  12.4 0.0 copy-done.5
  12.4 0.0 copy-done.3
  12.4 1.0 %shard_map.126 = (f32[136,128]{1,0:T(8,128)S(1)}, bf16[256,2048]{1,0:T(8,128)(2,1)S(1)}) custom-call(bf16[128,128]{1,0:T(8,128)(2,1)S(1)} %bitcast.29, bf16[1024,128]{1,0:T(8,128)(2,1)S(1)} %bitcast.25, f32[1024,128]{1,0:T(8,128)S(1)} %bitcast.18, f32[1024,128]{1,0:T(8,128)S(1)} %bitcast.20, f32[1024,128]{1,0:T(8,128)S(1)} %bitcast.22), custom_call_target="tpu_custom_call" | custom-call | flops 1000000 | bytes 2000 | tf_op jit(solution)/shard_map/pallas_call | solution.py:428
  13.5 0.0 collective-permute-done.from_next
  13.5 0.0 collective-permute-done.1.from_pair
  13.5 0.2 shard_map.129
  13.7 0.7 collective-permute-start.2
  14.4 4.6 %collective-permute-start.3 = (bf16[80,128]{1,0:T(8,128)(2,1)S(1)}, bf16[80,128]{1,0:T(8,128)(2,1)S(1)}, u32[]{:S(2)}, u32[]{:S(2)}) collective-permute-start(bf16[80,128]{1,0:T(8,128)(2,1)S(1)} %get-tuple-element.37), channel_id=1, source_target_pairs={{0,16},{16,0},{32,48},{48,32},{64,80},{80,64},{96,112},{112,96},{1... | collective-permute-start | bytes 61448 | tf_op jit(solution)/shard_map/ppermute | solution.py:30
  19.1 0.0 copy-done.4
  19.1 3.7 %shard_map.128 = (bf16[1024,128]{1,0:T(8,128)(2,1)}, f32[64,16,128]{2,1,0:T(8,128)}, f32[64,16,128]{2,1,0:T(8,128)}, bf16[256,2304]{1,0:T(8,128)(2,1)S(1)}, f32[...) custom-call(bf16[256,2048]{1,0:T(8,128)(2,1)S(1)} %get-tuple-element.30.stacked, ...), custom_call_target="tpu_custom_call" | custom-call | flops 1400000000 | bytes 4000000 | tf_op jit(solution)/shard_map/pallas_call | solution.py:484
  22.7 0.0 collective-permute-done.2.from_next
  22.7 0.0 collective-permute-done.3.from_pair
  22.8 0.9 shard_map.130
  23.6 16.9 %all_to_all.20.parts = bf16[32,48,128]{2,1,0:T(8,128)(2,1)S(1)} all-to-all(bf16[32,48,128]{2,1,0:T(8,128)(2,1)S(1)} %bitcast.26), channel_id=1, replica_groups=mesh['z_hi'=4,'z_lo'=4,'x_hi'=2,'y'=4,'x_lo'=2,'core'=2] {'x_hi','y','x_..., dimensions={0} | all-to-all | bytes 786432 | tf_op jit(solution)/shard_map/all_to_all | solution.py:420
  40.5 0.1 shard_map.132
  40.6 11.4 %all_to_all.21.parts = f32[4,48,128]{2,1,0:T(8,128)S(1)} all-to-all(f32[4,48,128]{2,1,0:T(8,128)S(1)} %shard_map.132), channel_id=1, replica_groups=mesh['z_hi'=4,'z_lo'=4,'x_hi'=2,'y'=4,'x_lo'=2,'core'=2] {'z_lo'}, dimensions={0} | all-to-all | bytes 196608 | tf_op jit(solution)/shard_map/all_to_all | solution.py:420
  52.0 22.6 %all_to_all.22.parts = f32[4,48,128]{2,1,0:T(8,128)S(1)} all-to-all(f32[4,48,128]{2,1,0:T(8,128)S(1)} %shard_map.133), channel_id=1, replica_groups=mesh['z_hi'=4,'z_lo'=4,'x_hi'=2,'y'=4,'x_lo'=2,'core'=2] {'z_hi'}, dimensions={0} | all-to-all | bytes 196608 | tf_op jit(solution)/shard_map/all_to_all | solution.py:420
  74.6 0.8 shard_map.134
  75.4 7.4 %all-to-all-start.3 = ((bf16[32,48,128]{2,1,0:T(8,128)(2,1)}), bf16[32,48,128]{2,1,0:T(8,128)(2,1)S(1)}, u32[]{:S(2)}, u32[]{:S(2)}) async-start(bf16[32,48,128]{2,1,0:T(8,128)(2,1)} %shard_map.134), calls=%async_computation.3 | async-start | bytes 786432 | tf_op jit(solution)/shard_map/all_to_all | solution.py:420
  82.8 4.3 %shard_map.131 = (bf16[1024,128]{1,0:T(8,128)(2,1)}, f32[1024,128]{1,0:T(8,128)}, f32[1024,128]{1,0:T(8,128)}, bf16[128,128]{1,0:T(8,128)(2,1)}, bf16[1024,128]{1,0:T(8,128)(2,1)}) custom-call(bf16[648,256]{1,0:T(8,128)(2,1)S(1)} %bitcast.28, ...), custom_call_target="tpu_custom_call", output_to_operand_aliasing={{0}: (4, {}), {1}: (5, {}), {2}: (6, {})} | custom-call | flops 764000000 | bytes 1528000 | tf_op jit(solution)/shard_map/pallas_call | solution.py:428
  87.1 5.7 %all-to-all-done.3 = bf16[32,48,128]{2,1,0:T(8,128)(2,1)S(1)} async-done(((bf16[32,48,128]{2,1,0:T(8,128)(2,1)}), bf16[32,48,128]{2,1,0:T(8,128)(2,1)S(1)}, u32[]{:S(2)}, u32[]{:S(2)}) %all-to-all-start.3) | async-done | bytes 393248 | tf_op jit(solution)/shard_map/all_to_all | solution.py:420
  92.8 1.7 %shard_map.135 = (f32[648,256]{1,0:T(8,128)}, f32[1,256]{1,0:T(1,128)}) custom-call(bf16[1536,128]{1,0:T(8,128)(2,1)S(1)} %bitcast.24), custom_call_target="tpu_custom_call" | custom-call | tf_op jit(solution)/shard_map/pallas_call | solution.py:539
  (1 shorter events, 0.0 us)
Async XLA Ops:
  0.6 11.8 %copy-start = (f32[64,16,128]{2,1,0:T(8,128)S(1)}, f32[64,16,128]{2,1,0:T(8,128)}, u32[]{:S(2)}) copy-start(f32[64,16,128]{2,1,0:T(8,128)} %cell_prev.1) | copy-start | bytes 1572868
  0.6 11.8 %copy-start.1 = (f32[64,16,128]{2,1,0:T(8,128)S(1)}, f32[64,16,128]{2,1,0:T(8,128)}, u32[]{:S(2)}) copy-start(f32[64,16,128]{2,1,0:T(8,128)} %grad_hidden.1) | copy-start | bytes 1572868
  0.7 11.8 %copy-start.2 = (f32[64,16,128]{2,1,0:T(8,128)S(1)}, f32[64,16,128]{2,1,0:T(8,128)}, u32[]{:S(2)}) copy-start(f32[64,16,128]{2,1,0:T(8,128)} %grad_cell.1) | copy-start | bytes 1572868
  0.7 11.8 %copy-start.5 = (bf16[8,16,128]{2,1,0:T(8,128)(2,1)S(1)}, bf16[8,16,128]{2,1,0:T(8,128)(2,1)}, u32[]{:S(2)}) copy-start(bf16[8,16,128]{2,1,0:T(8,128)(2,1)} %frame.1) | copy-start | bytes 98308
  0.7 11.8 %copy-start.3 = (bf16[64,16,128]{2,1,0:T(8,128)(2,1)S(1)}, bf16[64,16,128]{2,1,0:T(8,128)(2,1)}, u32[]{:S(2)}) copy-start(bf16[64,16,128]{2,1,0:T(8,128)(2,1)} %hidden_prev.1) | copy-start | bytes 786436
  0.7 11.6 %copy-start.6 = (f32[256]{0:T(256)S(1)}, f32[256]{0:T(256)}, u32[]{:S(2)}) copy-start(f32[256]{0:T(256)} %param.11) | copy-start | bytes 3076
  2.6 16.4 %copy-start.4 = (bf16[256,648]{0,1:T(8,128)(2,1)S(1)}, bf16[256,648]{0,1:T(8,128)(2,1)}, u32[]{:S(2)}) copy-start(bf16[256,648]{0,1:T(8,128)(2,1)} %param.10) | copy-start | bytes 995332
  2.6 10.9 %collective-permute-start = (bf16[336,128]{1,0:T(8,128)(2,1)}, bf16[336,128]{1,0:T(8,128)(2,1)S(1)}, u32[]{:S(2)}, u32[]{:S(2)}) collective-permute-start(bf16[336,128]{1,0:T(8,128)(2,1)} %get-tuple-element.31), channel_id=1, source_target_pairs={{1,2},{2,1},{3,4},{4,3},{5,6},{6,5},{7,8},{8,7},{9,10},{10,9},{11,... | collective-permute-start | bytes 258056 | tf_op jit(solution)/shard_map/ppermute | solution.py:29
  7.3 6.2 %collective-permute-start.1 = (bf16[336,128]{1,0:T(8,128)(2,1)}, bf16[336,128]{1,0:T(8,128)(2,1)S(1)}, u32[]{:S(2)}, u32[]{:S(2)}) collective-permute-start(bf16[336,128]{1,0:T(8,128)(2,1)} %get-tuple-element.32), channel_id=1, source_target_pairs={{0,1},{1,0},{2,3},{3,2},{4,5},{5,4},{6,7},{7,6},{8,9},{9,8},{10,11... | collective-permute-start | bytes 258056 | tf_op jit(solution)/shard_map/ppermute | solution.py:30
  13.7 9.0 %collective-permute-start.2 = (bf16[80,128]{1,0:T(8,128)(2,1)S(1)}, bf16[80,128]{1,0:T(8,128)(2,1)S(1)}, u32[]{:S(2)}, u32[]{:S(2)}) collective-permute-start(bf16[80,128]{1,0:T(8,128)(2,1)S(1)} %get-tuple-element.36), channel_id=1, source_target_pairs={{16,32},{32,16},{48,64},{64,48},{80,96},{96,80},{112,128},{128,112... | collective-permute-start | bytes 61448 | tf_op jit(solution)/shard_map/ppermute | solution.py:29
  14.4 8.3 %collective-permute-start.3 = (bf16[80,128]{1,0:T(8,128)(2,1)S(1)}, bf16[80,128]{1,0:T(8,128)(2,1)S(1)}, u32[]{:S(2)}, u32[]{:S(2)}) collective-permute-start(bf16[80,128]{1,0:T(8,128)(2,1)S(1)} %get-tuple-element.37), channel_id=1, source_target_pairs={{0,16},{16,0},{32,48},{48,32},{64,80},{80,64},{96,112},{112,96},{1... | collective-permute-start | bytes 61448 | tf_op jit(solution)/shard_map/ppermute | solution.py:30
  75.4 17.4 %all-to-all-start.3 = ((bf16[32,48,128]{2,1,0:T(8,128)(2,1)}), bf16[32,48,128]{2,1,0:T(8,128)(2,1)S(1)}, u32[]{:S(2)}, u32[]{:S(2)}) async-start(bf16[32,48,128]{2,1,0:T(8,128)(2,1)} %shard_map.134), calls=%async_computation.3 | async-start | bytes 786432 | tf_op jit(solution)/shard_map/all_to_all | solution.py:420

commit v10 on v8

--- a/solution.py
+++ b/solution.py
@@ -283,13 +283,12 @@
     inside = (lane >= STEP) & (lane < STEP * (height + 1)) & ((slot == 1) | (slot == 2))
     grads = jnp.where(inside, grads, 0.0).astype(BF16)
     for row_off in range(3):
-        part = slice(row_off * STACK, (row_off + 1) * STACK)
-        terms[part] = (
-            inner_terms[part]
-            + lax.dot_general(
-                stacks[row_off], grads, (((1,), (1,)), ((), ())), preferred_element_type=F32
-            )
-        ).astype(BF16)
+        total = inner_terms[row_off * STACK : (row_off + 1) * STACK] + lax.dot_general(
+            stacks[row_off], grads, (((1,), (1,)), ((), ())), preferred_element_type=F32
+        )
+        for half in range(2):
+            start = (3 * half + row_off) * STACK
+            terms[start : start + STACK] = total[:, half * LANES : (half + 1) * LANES].astype(BF16)
 
 
 def backward_kernel(
@@ -356,8 +355,10 @@
 
 def finish_kernel(total, kernel_step, bias_step):
     block = kernel_step.shape[0] // 3
-    parts = [total[i * STACK : i * STACK + block].astype(F32) for i in range(3)]
-    bias_grad = total[block : block + 8].astype(F32)[:1]
+    halves = [total[half * 3 * STACK : (half + 1) * 3 * STACK].astype(F32) for half in range(2)]
+    whole = jnp.concatenate(halves, 1)
+    parts = [whole[i * STACK : i * STACK + block] for i in range(3)]
+    bias_grad = whole[block : block + 1]
     norm = jnp.sqrt(sum(jnp.sum(part * part) for part in parts) + jnp.sum(bias_grad * bias_grad))
     factor = jnp.minimum(1.0, CLIP_NORM / norm)
     for i, part in enumerate(parts):
@@ -365,20 +366,19 @@
     bias_step[...] = bias_grad * factor
 
 
-def sum_kernel(parts, *rest):
-    copies = rest[-1]
+def sum_kernel(parts, copies):
     total = jnp.sum(parts[...].astype(F32), 0).astype(copies.dtype)
     copies[...] = jnp.broadcast_to(total[None], copies.shape)
 
 
-def summed(parts, copies, kind, *after):
+def summed(parts, copies, kind):
     return pl.pallas_call(
         sum_kernel,
         out_shape=jax.ShapeDtypeStruct((copies,) + parts.shape[1:], kind),
-        in_specs=vmem(1) + [pl.BlockSpec(memory_space=pl.ANY)] * len(after),
+        in_specs=vmem(1),
         out_specs=vmem(1)[0],
         compiler_params=pltpu.CompilerParams(vmem_limit_bytes=8 * 2**20),
-    )(parts, *after)
+    )(parts)
 
 
 def exchanged(copies, axes):
@@ -470,7 +470,7 @@
     )(stacked, *rows, kernel.T, bias, *states)
     side_grads, side_cells, terms = called(
         functools.partial(sides_kernel, height=height),
-        [shape(gate_rows, LANES, BF16), shape(3 * units, LANES, F32), shape(3 * STACK, gate_rows, BF16)],
+        [shape(gate_rows, LANES, BF16), shape(3 * units, LANES, F32), shape(6 * STACK, LANES, BF16)],
         [],
         100_000_000,
         columns,
@@ -482,11 +482,11 @@
 
     plane = lax.axis_size(PLANE)
     low, high = lax.axis_size("z_lo"), lax.axis_size("z_hi")
-    mine = exchanged(terms.reshape(plane, -1, gate_rows), PLANE)
+    mine = exchanged(terms.reshape(plane, -1, LANES), PLANE)
     mine = exchanged(summed(mine, low, F32), "z_lo")
     mine = exchanged(summed(mine, high, F32), "z_hi")
     mine = summed(mine, plane, BF16)
-    total = exchanged(mine, PLANE).reshape(3 * STACK, gate_rows)
+    total = exchanged(mine, PLANE).reshape(6 * STACK, LANES)
     hidden, cell, grad_cell_prev, grad_frame, grad_hidden_prev = called(
         backward_kernel,
         [shape(*flat, BF16), field, field, shape(inputs * height, breadth, BF16), shape(*flat, BF16)],

time: 94.3 us -> 94.3 us (level)
  no operation moved by 1% of the time
where the time goes in v10:
time: 94.3 us; the launch traced here: 93.9 us
  blocking collectives  50.9 us (54%)
  starting transfers between devices  22.2 us (24%)
  Pallas kernels  14 us (15%)
  waiting for transfers between devices  5.69 us (6%)
    all_to_all x3, blocking collectives, exchanged(): return lax.all_to_all(copies, axes, 0, 0, tiled=True)  50.9 us
    ppermute x2, starting transfers between devices, swapped(): return (other, lax.ppermute(to_pair, axes, pairs))  9.58 us
    pallas_call x5, Pallas kernels, called(): pl.pallas_call(kernel, out_shape=tuple(outs), in_specs=vmem(len(args)), o...  7.59 us
    all_to_all x1, starting transfers between devices, exchanged(): return lax.all_to_all(copies, axes, 0, 0, tiled=True)  7.36 us
    all_to_all x1, waiting for transfers between devices, exchanged(): return lax.all_to_all(copies, axes, 0, 0, tiled=True)  5.68 us
    ppermute x2, starting transfers between devices, swapped(): other = lax.ppermute(to_next, axes, across)  5.3 us
    pallas_call x1, Pallas kernels, per_device(): pl.pallas_call(forward_kernel, out_shape=(shape(*flat, BF16), cube, cube,...  3.66 us
    pallas_call x1, Pallas kernels, per_device(): pl.pallas_call(rows_kernel, out_shape=(strip, strip), in_specs=[pl.BlockS...  1.93 us
  transfers between devices with their start and end apart: 5, of which 1 were waited for; matrix products, arithmetic and copies ran while one was open for 0% of the time, Pallas kernels for 10%

profile of v10, /device:TPU:1, one launch (start us, length us, event | category | flops | bytes accessed | tf_op | source)
XLA Modules:
  0.0 93.9 jit_solution(3091901702108090078)
XLA Ops:
  0.6 0.0 copy-start
  0.6 0.0 copy-start.1
  0.7 0.0 copy-start.2
  0.7 0.0 copy-start.5
  0.7 0.0 copy-start.3
  0.7 0.0 copy-start.6
  0.7 1.9 %shard_map.127 = (bf16[336,128]{1,0:T(8,128)(2,1)}, bf16[336,128]{1,0:T(8,128)(2,1)}) custom-call(bf16[8,16,128]{2,1,0:T(8,128)(2,1)} %frame.1, bf16[64,16,128]{2,1,0:T(8,128)(2,1)} %hidden_prev.1, f32[64,16,128]{2,1,0:T(8,128)} %cell_prev.1, f32[64,16,128]{2,1,0:T(8,128)} %grad_hidden.1, f32[64,16,128]{2,1,0:T(8,128)} %grad_cell.1), custom_call_target="tpu_custom_call" | custom-call | flops 1000000 | bytes 1000000 | tf_op jit(solution)/shard_map/pallas_call | solution.py:417
  2.6 0.0 copy-start.4
  2.6 4.6 %collective-permute-start = (bf16[336,128]{1,0:T(8,128)(2,1)}, bf16[336,128]{1,0:T(8,128)(2,1)S(1)}, u32[]{:S(2)}, u32[]{:S(2)}) collective-permute-start(bf16[336,128]{1,0:T(8,128)(2,1)} %get-tuple-element.31), channel_id=1, source_target_pairs={{1,2},{2,1},{3,4},{4,3},{5,6},{6,5},{7,8},{8,7},{9,10},{10,9},{11,... | collective-permute-start | bytes 258056 | tf_op jit(solution)/shard_map/ppermute | solution.py:29
  7.3 4.9 %collective-permute-start.1 = (bf16[336,128]{1,0:T(8,128)(2,1)}, bf16[336,128]{1,0:T(8,128)(2,1)S(1)}, u32[]{:S(2)}, u32[]{:S(2)}) collective-permute-start(bf16[336,128]{1,0:T(8,128)(2,1)} %get-tuple-element.32), channel_id=1, source_target_pairs={{0,1},{1,0},{2,3},{3,2},{4,5},{5,4},{6,7},{7,6},{8,9},{9,8},{10,11... | collective-permute-start | bytes 258056 | tf_op jit(solution)/shard_map/ppermute | solution.py:30
  12.2 0.0 copy-done.6
  12.3 0.1 copy.17.bias
  12.4 0.0 copy-done
  12.4 0.0 copy-done.1
  12.4 0.0 copy-done.2
  12.4 0.0 copy-done.5
  12.4 0.0 copy-done.3
  12.4 1.0 %shard_map.126 = (f32[136,128]{1,0:T(8,128)S(1)}, bf16[256,2048]{1,0:T(8,128)(2,1)S(1)}) custom-call(bf16[128,128]{1,0:T(8,128)(2,1)S(1)} %bitcast.29, bf16[1024,128]{1,0:T(8,128)(2,1)S(1)} %bitcast.25, f32[1024,128]{1,0:T(8,128)S(1)} %bitcast.18, f32[1024,128]{1,0:T(8,128)S(1)} %bitcast.20, f32[1024,128]{1,0:T(8,128)S(1)} %bitcast.22), custom_call_target="tpu_custom_call" | custom-call | flops 1000000 | bytes 2000 | tf_op jit(solution)/shard_map/pallas_call | solution.py:393
  13.5 0.0 collective-permute-done.from_next
  13.5 0.0 collective-permute-done.1.from_pair
  13.5 0.2 shard_map.129
  13.7 0.7 collective-permute-start.2
  14.4 4.6 %collective-permute-start.3 = (bf16[80,128]{1,0:T(8,128)(2,1)S(1)}, bf16[80,128]{1,0:T(8,128)(2,1)S(1)}, u32[]{:S(2)}, u32[]{:S(2)}) collective-permute-start(bf16[80,128]{1,0:T(8,128)(2,1)S(1)} %get-tuple-element.37), channel_id=1, source_target_pairs={{0,16},{16,0},{32,48},{48,32},{64,80},{80,64},{96,112},{112,96},{1... | collective-permute-start | bytes 61448 | tf_op jit(solution)/shard_map/ppermute | solution.py:30
  19.1 0.0 copy-done.4
  19.1 3.7 %shard_map.128 = (bf16[1024,128]{1,0:T(8,128)(2,1)}, f32[64,16,128]{2,1,0:T(8,128)}, f32[64,16,128]{2,1,0:T(8,128)}, bf16[256,2304]{1,0:T(8,128)(2,1)S(1)}, f32[...) custom-call(bf16[256,2048]{1,0:T(8,128)(2,1)S(1)} %get-tuple-element.30.stacked, ...), custom_call_target="tpu_custom_call" | custom-call | flops 1400000000 | bytes 4000000 | tf_op jit(solution)/shard_map/pallas_call | solution.py:449
  22.7 0.0 collective-permute-done.2.from_next
  22.7 0.0 collective-permute-done.3.from_pair
  22.8 0.9 shard_map.130
  23.6 16.9 %all_to_all.20.parts = bf16[32,48,128]{2,1,0:T(8,128)(2,1)S(1)} all-to-all(bf16[32,48,128]{2,1,0:T(8,128)(2,1)S(1)} %bitcast.26), channel_id=1, replica_groups=mesh['z_hi'=4,'z_lo'=4,'x_hi'=2,'y'=4,'x_lo'=2,'core'=2] {'x_hi','y','x_..., dimensions={0} | all-to-all | bytes 786432 | tf_op jit(solution)/shard_map/all_to_all | solution.py:385
  40.5 0.1 shard_map.132
  40.6 11.4 %all_to_all.21.parts = f32[4,48,128]{2,1,0:T(8,128)S(1)} all-to-all(f32[4,48,128]{2,1,0:T(8,128)S(1)} %shard_map.132), channel_id=1, replica_groups=mesh['z_hi'=4,'z_lo'=4,'x_hi'=2,'y'=4,'x_lo'=2,'core'=2] {'z_lo'}, dimensions={0} | all-to-all | bytes 196608 | tf_op jit(solution)/shard_map/all_to_all | solution.py:385
  52.0 22.6 %all_to_all.22.parts = f32[4,48,128]{2,1,0:T(8,128)S(1)} all-to-all(f32[4,48,128]{2,1,0:T(8,128)S(1)} %shard_map.133), channel_id=1, replica_groups=mesh['z_hi'=4,'z_lo'=4,'x_hi'=2,'y'=4,'x_lo'=2,'core'=2] {'z_hi'}, dimensions={0} | all-to-all | bytes 196608 | tf_op jit(solution)/shard_map/all_to_all | solution.py:385
  74.6 0.8 shard_map.134
  75.4 7.4 %all-to-all-start.3 = ((bf16[32,48,128]{2,1,0:T(8,128)(2,1)}), bf16[32,48,128]{2,1,0:T(8,128)(2,1)S(1)}, u32[]{:S(2)}, u32[]{:S(2)}) async-start(bf16[32,48,128]{2,1,0:T(8,128)(2,1)} %shard_map.134), calls=%async_computation.3 | async-start | bytes 786432 | tf_op jit(solution)/shard_map/all_to_all | solution.py:385
  82.8 4.3 %shard_map.131 = (bf16[1024,128]{1,0:T(8,128)(2,1)}, f32[1024,128]{1,0:T(8,128)}, f32[1024,128]{1,0:T(8,128)}, bf16[128,128]{1,0:T(8,128)(2,1)}, bf16[1024,128]{1,0:T(8,128)(2,1)}) custom-call(bf16[648,256]{1,0:T(8,128)(2,1)S(1)} %bitcast.28, ...), custom_call_target="tpu_custom_call", output_to_operand_aliasing={{0}: (4, {}), {1}: (5, {}), {2}: (6, {})} | custom-call | flops 764000000 | bytes 1528000 | tf_op jit(solution)/shard_map/pallas_call | solution.py:393
  87.1 5.7 %all-to-all-done.3 = bf16[32,48,128]{2,1,0:T(8,128)(2,1)S(1)} async-done(((bf16[32,48,128]{2,1,0:T(8,128)(2,1)}), bf16[32,48,128]{2,1,0:T(8,128)(2,1)S(1)}, u32[]{:S(2)}, u32[]{:S(2)}) %all-to-all-start.3) | async-done | bytes 393248 | tf_op jit(solution)/shard_map/all_to_all | solution.py:385
  92.7 1.2 %shard_map.135 = (f32[648,256]{1,0:T(8,128)}, f32[1,256]{1,0:T(1,128)}) custom-call(bf16[1536,128]{1,0:T(8,128)(2,1)S(1)} %bitcast.24), custom_call_target="tpu_custom_call" | custom-call | flops 1000000 | bytes 2000 | tf_op jit(solution)/shard_map/pallas_call | solution.py:393
  (1 shorter events, 0.0 us)
Async XLA Ops:
  0.6 11.8 %copy-start = (f32[64,16,128]{2,1,0:T(8,128)S(1)}, f32[64,16,128]{2,1,0:T(8,128)}, u32[]{:S(2)}) copy-start(f32[64,16,128]{2,1,0:T(8,128)} %cell_prev.1) | copy-start | bytes 1572868
  0.6 11.8 %copy-start.1 = (f32[64,16,128]{2,1,0:T(8,128)S(1)}, f32[64,16,128]{2,1,0:T(8,128)}, u32[]{:S(2)}) copy-start(f32[64,16,128]{2,1,0:T(8,128)} %grad_hidden.1) | copy-start | bytes 1572868
  0.7 11.8 %copy-start.2 = (f32[64,16,128]{2,1,0:T(8,128)S(1)}, f32[64,16,128]{2,1,0:T(8,128)}, u32[]{:S(2)}) copy-start(f32[64,16,128]{2,1,0:T(8,128)} %grad_cell.1) | copy-start | bytes 1572868
  0.7 11.8 %copy-start.5 = (bf16[8,16,128]{2,1,0:T(8,128)(2,1)S(1)}, bf16[8,16,128]{2,1,0:T(8,128)(2,1)}, u32[]{:S(2)}) copy-start(bf16[8,16,128]{2,1,0:T(8,128)(2,1)} %frame.1) | copy-start | bytes 98308
  0.7 11.8 %copy-start.3 = (bf16[64,16,128]{2,1,0:T(8,128)(2,1)S(1)}, bf16[64,16,128]{2,1,0:T(8,128)(2,1)}, u32[]{:S(2)}) copy-start(bf16[64,16,128]{2,1,0:T(8,128)(2,1)} %hidden_prev.1) | copy-start | bytes 786436
  0.7 11.6 %copy-start.6 = (f32[256]{0:T(256)S(1)}, f32[256]{0:T(256)}, u32[]{:S(2)}) copy-start(f32[256]{0:T(256)} %param.11) | copy-start | bytes 3076
  2.6 16.4 %copy-start.4 = (bf16[256,648]{0,1:T(8,128)(2,1)S(1)}, bf16[256,648]{0,1:T(8,128)(2,1)}, u32[]{:S(2)}) copy-start(bf16[256,648]{0,1:T(8,128)(2,1)} %param.10) | copy-start | bytes 995332
  2.6 10.9 %collective-permute-start = (bf16[336,128]{1,0:T(8,128)(2,1)}, bf16[336,128]{1,0:T(8,128)(2,1)S(1)}, u32[]{:S(2)}, u32[]{:S(2)}) collective-permute-start(bf16[336,128]{1,0:T(8,128)(2,1)} %get-tuple-element.31), channel_id=1, source_target_pairs={{1,2},{2,1},{3,4},{4,3},{5,6},{6,5},{7,8},{8,7},{9,10},{10,9},{11,... | collective-permute-start | bytes 258056 | tf_op jit(solution)/shard_map/ppermute | solution.py:29
  7.3 6.2 %collective-permute-start.1 = (bf16[336,128]{1,0:T(8,128)(2,1)}, bf16[336,128]{1,0:T(8,128)(2,1)S(1)}, u32[]{:S(2)}, u32[]{:S(2)}) collective-permute-start(bf16[336,128]{1,0:T(8,128)(2,1)} %get-tuple-element.32), channel_id=1, source_target_pairs={{0,1},{1,0},{2,3},{3,2},{4,5},{5,4},{6,7},{7,6},{8,9},{9,8},{10,11... | collective-permute-start | bytes 258056 | tf_op jit(solution)/shard_map/ppermute | solution.py:30
  13.7 9.0 %collective-permute-start.2 = (bf16[80,128]{1,0:T(8,128)(2,1)S(1)}, bf16[80,128]{1,0:T(8,128)(2,1)S(1)}, u32[]{:S(2)}, u32[]{:S(2)}) collective-permute-start(bf16[80,128]{1,0:T(8,128)(2,1)S(1)} %get-tuple-element.36), channel_id=1, source_target_pairs={{16,32},{32,16},{48,64},{64,48},{80,96},{96,80},{112,128},{128,112... | collective-permute-start | bytes 61448 | tf_op jit(solution)/shard_map/ppermute | solution.py:29
  14.4 8.3 %collective-permute-start.3 = (bf16[80,128]{1,0:T(8,128)(2,1)S(1)}, bf16[80,128]{1,0:T(8,128)(2,1)S(1)}, u32[]{:S(2)}, u32[]{:S(2)}) collective-permute-start(bf16[80,128]{1,0:T(8,128)(2,1)S(1)} %get-tuple-element.37), channel_id=1, source_target_pairs={{0,16},{16,0},{32,48},{48,32},{64,80},{80,64},{96,112},{112,96},{1... | collective-permute-start | bytes 61448 | tf_op jit(solution)/shard_map/ppermute | solution.py:30
  75.4 17.3 %all-to-all-start.3 = ((bf16[32,48,128]{2,1,0:T(8,128)(2,1)}), bf16[32,48,128]{2,1,0:T(8,128)(2,1)S(1)}, u32[]{:S(2)}, u32[]{:S(2)}) async-start(bf16[32,48,128]{2,1,0:T(8,128)(2,1)} %shard_map.134), calls=%async_computation.3 | async-start | bytes 786432 | tf_op jit(solution)/shard_map/all_to_all | solution.py:385
